TPU v7x, 32 devices: a whole 2x2x4 slice. The times are simulated.
32 devices in a mesh: dp: 8 (over z, y), head: 4 (over x, core).
Axes of the slice: x: 2, y: 2, z: 4, core: 2. Of those that a mesh axis runs over, the one named last changes fastest.
Arguments:
- tokens: bfloat16 [9408, 512], P('dp'), may hold values from -6 to 6
- cotangent: bfloat16 [9408, 512], P('dp'), may hold values from -16 to 16
- crop_image: int32 [32, 6], P('dp'), may hold values from 0 to 2, never falling along the last dimension, each value on 1 to 3 neighbouring positions
- crop_class: int32 [32, 6], P('dp'), may hold values 0 or 1
- weights: float32 [12, 512, 512], P(None, 'dp', 'head'), may hold values from -4 to 4
- row_state: float32 [12, 512], P(None, 'dp'), as said below
- col_state: float32 [12, 512], P(None, 'head'), as said below
- weights_ema: float32 [12, 512, 512], P(None, 'dp', 'head'), may hold values from -4 to 4
- small_params: float32 [71, 512], replicated, may hold values from -4 to 8
- small_state: float32 [71, 512], replicated, as said below
- small_ema: float32 [71, 512], replicated, may hold values from -4 to 8
Outputs:
- block_out: bfloat16 [9408, 512], P('dp')
- input_grad: bfloat16 [9408, 512], P('dp')
- weight_grads: float32 [12, 512, 512], P(None, 'dp', 'head')
- new_row_state: float32 [12, 512], P(None, 'dp')
- new_col_state: float32 [12, 512], P(None, 'head')
- new_weights: float32 [12, 512, 512], P(None, 'dp', 'head')
- weights_copy: bfloat16 [12, 512, 512], P(None, 'dp', 'head')
- new_weights_ema: float32 [12, 512, 512], P(None, 'dp', 'head')
- small_grads: float32 [71, 512], replicated
- new_small_state: float32 [71, 512], replicated
- new_small_params: float32 [71, 512], replicated
- new_small_ema: float32 [71, 512], replicated
- clip_rms: float32 [83], replicated
Inputs may be any that keep to these rules, and one draw needn't show every extreme that they name: `crop_image`: along each row the values never fall; each of the 3 images has 1 to 3 crops, and in every group one image has exactly 3 crops. `crop_class`: 1 marks a crop of 3 x 3 cells in the top left corner of its grid, 0 a full crop. `row_state`: entries are positive. `col_state`: entries are positive. `small_state`: entries are positive.
All inputs are finite; a program needn't handle non-finite values. No bound on the sum of `crop_class` on one device may be relied on, other than what follows from the above.
Results may differ from a plain program's by a relative error of at most 0.014.
Values may be sent and summed in bfloat16 or wider, within the bound.
A program may use at most 128 MiB of HBM per device.

v0:
```python
import math

import jax
import jax.numpy as jnp
from jax import lax
from jax.sharding import PartitionSpec as P

D = 512
HEAD_DIM = 64
GRID = 7
SMALL_GRID = 3
WINDOW = 7
IMG_GROUP = 3


FULL_PRECISION = lax.Precision.HIGHEST
NORM_EPS = 1e-06
SQUARE_FLOOR = 1e-30
SECOND_DECAY = 0.999
STEP_RATE = 0.02
SMALL_RATE = 0.05
AVERAGE_KEEP = 0.9
NEG_LARGE = -1e30
ROOT_HALF = 0.7071067811865476
INV_ROOT_TAU = 0.3989422804014327


def in_blocks(x, dim, size):
    shape = x.shape
    tiles = x.reshape(*shape[:dim], size, shape[dim] // size, *shape[dim + 1 :])
    return jnp.moveaxis(tiles, dim, 0)


def sent_and_summed(x, axis, dim):
    tiles = in_blocks(x, dim, lax.axis_size(axis))
    arrived = lax.all_to_all(tiles, axis, split_axis=0, concat_axis=0, tiled=True)
    return arrived.astype(jnp.float32).sum(axis=0)


def crop_live(class_row):
    grid_rows = lax.broadcasted_iota(jnp.int32, (GRID, GRID), 0)
    grid_cols = lax.broadcasted_iota(jnp.int32, (GRID, GRID), 1)
    inside = (grid_rows < SMALL_GRID) & (grid_cols < SMALL_GRID)
    return jnp.where((class_row[:, None, None] == 0) | inside[None, :, :], 1.0, 0.0).astype(
        jnp.float32
    )


def image_table(image_rows):
    group_count, per_group = image_rows.shape
    labels = (
        lax.broadcasted_iota(jnp.int32, image_rows.shape, 0) * IMG_GROUP + image_rows
    ).reshape(-1)
    images = lax.broadcasted_iota(jnp.int32, (group_count * IMG_GROUP, group_count * per_group), 0)
    return jnp.where(images == labels[None, :], 1.0, 0.0).astype(jnp.float32)


def window_mask(first_channel, channels):
    shape_taps = (WINDOW * WINDOW, channels)
    head_ids = (first_channel + lax.broadcasted_iota(jnp.int32, shape_taps, 1)) // HEAD_DIM
    reach_cells = jnp.where(head_ids < 2, 1, jnp.where(head_ids < 5, 2, 3))
    tap_ids = lax.broadcasted_iota(jnp.int32, shape_taps, 0)
    centre = WINDOW // 2
    row_off = jnp.abs(tap_ids // WINDOW - centre)
    col_off = jnp.abs(tap_ids % WINDOW - centre)
    return jnp.where((row_off <= reach_cells) & (col_off <= reach_cells), 1.0, 0.0).astype(
        jnp.float32
    )


def conv_grid(source, tap_table, window):
    reach_cells = window // 2
    padded = jnp.pad(
        source, ((0, 0), (reach_cells, reach_cells), (reach_cells, reach_cells), (0, 0))
    )
    summed = jnp.zeros_like(source)
    for row_tap in range(window):
        for col_tap in range(window):
            summed = (
                summed
                + tap_table[row_tap * window + col_tap]
                * padded[:, row_tap : row_tap + GRID, col_tap : col_tap + GRID, :]
            )
    return summed


def conv_grid_back(upstream, source, tap_table, window):
    reach_cells = window // 2
    pad_widths = ((0, 0), (reach_cells, reach_cells), (reach_cells, reach_cells), (0, 0))
    padded_up = jnp.pad(upstream, pad_widths)
    padded_src = jnp.pad(source, pad_widths)
    back_field = jnp.zeros_like(source)
    tap_grads = []
    for row_tap in range(window):
        for col_tap in range(window):
            row_from = 2 * reach_cells - row_tap
            col_from = 2 * reach_cells - col_tap
            back_field = (
                back_field
                + tap_table[row_tap * window + col_tap]
                * padded_up[:, row_from : row_from + GRID, col_from : col_from + GRID, :]
            )
            tap_grads.append(
                jnp.sum(
                    upstream * padded_src[:, row_tap : row_tap + GRID, col_tap : col_tap + GRID, :],
                    axis=(0, 1, 2),
                )
            )
    return (back_field, jnp.stack(tap_grads))


def norm_rows(row_block, norm_gain, norm_shift):
    centre = jnp.mean(row_block, axis=1, keepdims=True)
    offset = row_block - centre
    inverse = lax.rsqrt(jnp.mean(offset * offset, axis=1, keepdims=True) + NORM_EPS)
    unit_rows = offset * inverse
    return (unit_rows * norm_gain + norm_shift, unit_rows, inverse)


def norm_back(upstream, unit_rows, inverse, norm_gain):
    scaled = upstream * norm_gain
    return inverse * (
        scaled
        - jnp.mean(scaled, axis=1, keepdims=True)
        - unit_rows * jnp.mean(scaled * unit_rows, axis=1, keepdims=True)
    )


def gelu_exact(values):
    return values * 0.5 * (1.0 + lax.erf(values * ROOT_HALF))


def gelu_slope(values):
    return (
        0.5 * (1.0 + lax.erf(values * ROOT_HALF))
        + values * jnp.exp(-0.5 * values * values) * INV_ROOT_TAU
    )


def share_rows(rows):
    return lax.all_gather(rows, "head", axis=0, tiled=True)


def owner_rows(part):
    return lax.psum_scatter(part, "head", scatter_dimension=0, tiled=True)


def attend(query_low, key_low, value_low, live_cube, image_onehot, tap_table):
    slot_count, cell_count, channels = query_low.shape
    split_shape = (slot_count, cell_count, channels // HEAD_DIM, HEAD_DIM)
    masked_keys = jnp.where(live_cube > 0, key_low.astype(jnp.float32), NEG_LARGE)
    slot_top = jnp.max(masked_keys, axis=1)
    image_top = jnp.max(
        jnp.where(image_onehot[:, :, None] > 0, slot_top[None, :, :], NEG_LARGE), axis=1
    )
    slot_shift = jnp.dot(image_onehot.T, image_top, precision=FULL_PRECISION)
    raised = jnp.where(live_cube > 0, jnp.exp(masked_keys - slot_shift[:, None, :]), 0.0)
    image_total = jnp.dot(image_onehot, jnp.sum(raised, axis=1), precision=FULL_PRECISION)
    spread_total = jnp.dot(image_onehot.T, image_total, precision=FULL_PRECISION)
    soft_keys = raised / spread_total[:, None, :]
    soft_low = soft_keys.astype(jnp.bfloat16)
    slot_context = jnp.einsum(
        "snhd,snhe->shde",
        soft_low.reshape(split_shape),
        value_low.reshape(split_shape),
        preferred_element_type=jnp.float32,
    )
    image_context = jnp.einsum(
        "is,shde->ihde", image_onehot, slot_context, precision=FULL_PRECISION
    ).astype(jnp.bfloat16)
    spread_context = jnp.einsum(
        "is,ihde->shde",
        image_onehot.astype(jnp.bfloat16),
        image_context,
        preferred_element_type=jnp.float32,
    ).astype(jnp.bfloat16)
    factor = jnp.einsum(
        "snhd,shde->snhe",
        query_low.reshape(split_shape),
        spread_context,
        preferred_element_type=jnp.float32,
    ).reshape(query_low.shape)
    rel_source = (value_low.astype(jnp.float32) * live_cube).reshape(
        slot_count, GRID, GRID, channels
    )
    relative = conv_grid(rel_source, tap_table, WINDOW).reshape(query_low.shape)
    mixed_out = (
        factor * (1.0 / math.sqrt(HEAD_DIM)) + query_low.astype(jnp.float32) * relative
    ) * live_cube
    return (mixed_out, (soft_keys, soft_low, spread_context, relative, rel_source))


def attend_back(grad_mixed, query_low, value_low, live_cube, image_onehot, tap_table, kept):
    soft_keys, soft_low, spread_context, relative, rel_source = kept
    slot_count, cell_count, channels = query_low.shape
    split_shape = (slot_count, cell_count, channels // HEAD_DIM, HEAD_DIM)
    query_vals = query_low.astype(jnp.float32)
    value_vals = value_low.astype(jnp.float32)
    grad_live = grad_mixed * live_cube
    grad_factor = (grad_live * (1.0 / math.sqrt(HEAD_DIM))).reshape(split_shape)
    grad_query = grad_live * relative + jnp.einsum(
        "snhe,shde->snhd", grad_factor, spread_context.astype(jnp.float32), precision=FULL_PRECISION
    ).reshape(query_low.shape)
    grad_relative = (grad_live * query_vals).reshape(slot_count, GRID, GRID, channels)
    back_field, grad_taps = conv_grid_back(grad_relative, rel_source, tap_table, WINDOW)
    grad_slot_context = jnp.einsum(
        "snhd,snhe->shde", query_vals.reshape(split_shape), grad_factor, precision=FULL_PRECISION
    )
    grad_image_context = jnp.einsum(
        "is,shde->ihde", image_onehot, grad_slot_context, precision=FULL_PRECISION
    )
    grad_spread = jnp.einsum(
        "is,ihde->shde", image_onehot, grad_image_context, precision=FULL_PRECISION
    )
    grad_soft = jnp.einsum(
        "shde,snhe->snhd", grad_spread, value_vals.reshape(split_shape), precision=FULL_PRECISION
    ).reshape(query_low.shape)
    grad_value = back_field.reshape(query_low.shape) * live_cube + jnp.einsum(
        "snhd,shde->snhe",
        soft_low.astype(jnp.float32).reshape(split_shape),
        grad_spread,
        precision=FULL_PRECISION,
    ).reshape(query_low.shape)
    image_inner = jnp.dot(
        image_onehot, jnp.sum(soft_keys * grad_soft, axis=1), precision=FULL_PRECISION
    )
    spread_inner = jnp.dot(image_onehot.T, image_inner, precision=FULL_PRECISION)
    grad_key = soft_keys * (grad_soft - spread_inner[:, None, :])
    return (grad_query, grad_key, grad_value, grad_taps)


def local(
    tokens,
    cotangent,
    crop_image,
    crop_class,
    weights,
    row_state,
    col_state,
    weights_ema,
    small_params,
    small_state,
    small_ema,
):
    head_index = lax.axis_index("head")
    gathered = lax.all_gather(weights.astype(jnp.bfloat16), "dp", axis=1, tiled=True)
    group_rows = tokens.shape[0] // lax.axis_size("head")
    own_tokens = lax.dynamic_slice_in_dim(tokens, head_index * group_rows, group_rows, 0)
    own_cot = lax.dynamic_slice_in_dim(cotangent, head_index * group_rows, group_rows, 0)
    own_class = lax.dynamic_slice_in_dim(crop_class, head_index, 1, 0)
    first_channel = head_index * gathered.shape[2]
    channels = gathered.shape[2]
    cell_count = GRID * GRID
    own_grid = crop_live(own_class.reshape(-1))
    own_slots = own_grid.shape[0]
    own_live = own_grid.reshape(own_slots * cell_count, 1)
    wide_grid = crop_live(crop_class.reshape(-1))
    slot_count = wide_grid.shape[0]
    live_rows = wide_grid.reshape(slot_count * cell_count, 1)
    live_cube = wide_grid.reshape(slot_count, cell_count, 1)
    image_onehot = image_table(crop_image)
    cube_shape = (slot_count, cell_count, channels)
    query_bias = lax.dynamic_slice_in_dim(small_params[2], first_channel, channels, 0)
    value_bias = lax.dynamic_slice_in_dim(small_params[3], first_channel, channels, 0)
    hidden_bias = lax.dynamic_slice_in_dim(small_params[9:13], first_channel, channels, 1)
    pos_taps = small_params[13:22]
    rel_mask = window_mask(first_channel, channels)
    rel_taps = lax.dynamic_slice_in_dim(small_params[22:], first_channel, channels, 1) * rel_mask
    inputs = own_tokens.astype(jnp.float32)
    pos_source = (inputs * own_live).reshape(own_slots, GRID, GRID, D)
    first_sum = inputs + conv_grid(pos_source, pos_taps, 3).reshape(-1, D) + small_params[8]
    normed_one, unit_one, inverse_one = norm_rows(first_sum, small_params[0], small_params[1])
    normed_one = normed_one.astype(jnp.bfloat16)
    wide_one = share_rows(normed_one)
    projected = jnp.einsum(
        "rd,kdc->krc", wide_one, gathered[0:3], preferred_element_type=jnp.float32
    )
    query_low = (projected[0] + query_bias).astype(jnp.bfloat16).reshape(cube_shape)
    key_low = projected[1].astype(jnp.bfloat16).reshape(cube_shape)
    value_low = (projected[2] + value_bias).astype(jnp.bfloat16).reshape(cube_shape)
    mixed_out, kept = attend(query_low, key_low, value_low, live_cube, image_onehot, rel_taps)
    mixed_low = mixed_out.reshape(-1, channels).astype(jnp.bfloat16)
    proj_part = lax.dot_general(
        mixed_low, gathered[3], (((1,), (1,)), ((), ())), preferred_element_type=jnp.float32
    )
    proj_full = owner_rows(proj_part)
    second_sum = first_sum + proj_full + small_params[4]
    normed_two, unit_two, inverse_two = norm_rows(second_sum, small_params[5], small_params[6])
    normed_two = normed_two.astype(jnp.bfloat16)
    wide_two = share_rows(normed_two)
    hidden = (
        jnp.einsum("rd,kdc->rkc", wide_two, gathered[4:8], preferred_element_type=jnp.float32)
        + hidden_bias[None, :, :]
    )
    active_low = gelu_exact(hidden).astype(jnp.bfloat16)
    down_part = jnp.einsum(
        "rkc,kdc->rd", active_low, gathered[8:12], preferred_element_type=jnp.float32
    )
    down_full = owner_rows(down_part)
    block_rows = (second_sum + down_full + small_params[7]).astype(jnp.bfloat16)
    grad_out = own_cot.astype(jnp.float32) * own_live
    wide_grad_low = (cotangent.astype(jnp.float32) * live_rows).astype(jnp.bfloat16)
    grad_down = jnp.einsum(
        "rd,rkc->kdc", wide_grad_low, active_low, preferred_element_type=jnp.float32
    )
    grad_hidden = jnp.einsum(
        "rd,kdc->rkc", wide_grad_low, gathered[8:12], preferred_element_type=jnp.float32
    ) * gelu_slope(hidden)
    grad_hidden_low = grad_hidden.astype(jnp.bfloat16)
    grad_up = jnp.einsum(
        "rd,rkc->kdc", wide_two, grad_hidden_low, preferred_element_type=jnp.float32
    )
    back_part = jnp.einsum(
        "rkc,kdc->rd", grad_hidden_low, gathered[4:8], preferred_element_type=jnp.float32
    )
    back_two = owner_rows(back_part)
    grad_second = grad_out + norm_back(back_two, unit_two, inverse_two, small_params[5])
    grad_second_low = grad_second.astype(jnp.bfloat16)
    wide_second = share_rows(grad_second_low)
    grad_proj = lax.dot_general(
        wide_second, mixed_low, (((0,), (0,)), ((), ())), preferred_element_type=jnp.float32
    )
    grad_mixed = jnp.dot(wide_second, gathered[3], preferred_element_type=jnp.float32)
    grad_query, grad_key, grad_value, grad_rel = attend_back(
        grad_mixed.reshape(cube_shape),
        query_low,
        value_low,
        live_cube,
        image_onehot,
        rel_taps,
        kept,
    )
    grad_qkv_low = (
        jnp.stack([grad_query, grad_key, grad_value]).reshape(3, -1, channels).astype(jnp.bfloat16)
    )
    grad_in = jnp.einsum("rd,krc->kdc", wide_one, grad_qkv_low, preferred_element_type=jnp.float32)
    front_part = jnp.einsum(
        "krc,kdc->rd", grad_qkv_low, gathered[0:3], preferred_element_type=jnp.float32
    )
    back_one = owner_rows(front_part)
    grad_first = grad_second + norm_back(back_one, unit_one, inverse_one, small_params[0])
    back_pos, grad_pos_taps = conv_grid_back(
        grad_first.reshape(own_slots, GRID, GRID, D), pos_source, pos_taps, 3
    )
    grad_tokens = (grad_first + back_pos.reshape(-1, D) * own_live).astype(jnp.bfloat16)
    block_rows, grad_tokens = (
        lax.all_gather(block_rows, "head", axis=0, tiled=True),
        lax.all_gather(grad_tokens, "head", axis=0, tiled=True),
    )
    zero_row = jnp.zeros((D,), jnp.float32)
    full_rows = jnp.stack(
        [
            jnp.sum(back_one * unit_one, axis=0),
            jnp.sum(back_one, axis=0),
            zero_row,
            zero_row,
            jnp.sum(grad_second, axis=0),
            jnp.sum(back_two * unit_two, axis=0),
            jnp.sum(back_two, axis=0),
            jnp.sum(grad_out, axis=0),
            jnp.sum(grad_first, axis=0),
        ]
    )
    full_part = jnp.concatenate(
        [
            full_rows,
            jnp.zeros((4, D), jnp.float32),
            grad_pos_taps,
            jnp.zeros((WINDOW * WINDOW, D), jnp.float32),
        ],
        axis=0,
    )
    local_part = jnp.concatenate(
        [
            jnp.zeros((2, channels), jnp.float32),
            jnp.sum(grad_query, axis=(0, 1))[None, :],
            jnp.sum(grad_value, axis=(0, 1))[None, :],
            jnp.zeros((5, channels), jnp.float32),
            jnp.sum(grad_hidden, axis=0),
            jnp.zeros((9, channels), jnp.float32),
            grad_rel * rel_mask,
        ],
        axis=0,
    )
    placed = lax.dynamic_update_slice(
        jnp.zeros((full_part.shape[0], D), jnp.float32), local_part, (0, first_channel)
    )
    local_grads = jnp.concatenate([grad_in, grad_proj[None, :, :], grad_up, grad_down], axis=0)
    weight_grad = sent_and_summed(local_grads.astype(jnp.bfloat16), "dp", 1)
    small_total = lax.psum(full_part + placed, ("dp", "head"))
    squares = weight_grad * weight_grad + SQUARE_FLOOR
    row_total = lax.psum(jnp.sum(squares, axis=2), "head")
    new_rows = SECOND_DECAY * row_state + (1.0 - SECOND_DECAY) * (row_total / D)
    col_total, row_mass = lax.psum((jnp.sum(squares, axis=1), jnp.sum(new_rows, axis=1)), "dp")
    new_cols = SECOND_DECAY * col_state + (1.0 - SECOND_DECAY) * (col_total / D)
    estimate = new_rows[:, :, None] * new_cols[:, None, :] / (row_mass / D)[:, None, None]
    update = weight_grad * lax.rsqrt(estimate)
    update_sq = lax.psum(jnp.sum(update * update, axis=(1, 2)), ("dp", "head"))
    update_rms = jnp.sqrt(update_sq / (D * D))
    new_weights = weights - STEP_RATE * update / jnp.maximum(1.0, update_rms)[:, None, None]
    new_ema = AVERAGE_KEEP * weights_ema + (1.0 - AVERAGE_KEEP) * new_weights
    new_small_state = SECOND_DECAY * small_state + (1.0 - SECOND_DECAY) * (
        small_total * small_total + SQUARE_FLOOR
    )
    small_update = small_total * lax.rsqrt(new_small_state)
    small_rms = jnp.sqrt(jnp.mean(small_update * small_update, axis=1))
    new_small = small_params - SMALL_RATE * small_update / jnp.maximum(1.0, small_rms)[:, None]
    new_small_ema = AVERAGE_KEEP * small_ema + (1.0 - AVERAGE_KEEP) * new_small
    return (
        block_rows,
        grad_tokens,
        weight_grad,
        new_rows,
        new_cols,
        new_weights,
        new_weights.astype(jnp.bfloat16),
        new_ema,
        small_total,
        new_small_state,
        new_small,
        new_small_ema,
        jnp.concatenate([update_rms, small_rms]),
    )


def solution(mesh):
    in_specs = (
        P("dp", None),
        P("dp", None),
        P("dp", None),
        P("dp", None),
        P(None, "dp", "head"),
        P(None, "dp"),
        P(None, "head"),
        P(None, "dp", "head"),
        P(),
        P(),
        P(),
    )
    out_specs = (
        P("dp", None),
        P("dp", None),
        P(None, "dp", "head"),
        P(None, "dp"),
        P(None, "head"),
        P(None, "dp", "head"),
        P(None, "dp", "head"),
        P(None, "dp", "head"),
        P(),
        P(),
        P(),
        P(),
        P(),
    )
    return jax.shard_map(local, mesh=mesh, in_specs=in_specs, out_specs=out_specs, check_vma=False)
```

profile of v0, /device:TPU:10, one launch (start us, length us, event | category | flops | bytes accessed | tf_op | source)
XLA Modules:
  0.0 617.3 jit_solution(1170685293395563308)
XLA Ops:
  20.7 11.9 %all-gather.14.cloned.1.call-done = bf16[4,294,512]{2,1,0:T(8,128)(2,1)} async-done(((bf16[1,294,512]{2,1,0:T(8,128)(2,1)}), bf16[4,294,512]{2,1,0:T(8,128)(2,1)}) %all-gather.14.cloned.1.call-update) | async-done | bytes 1204240 | tf_op jit(solution)/shard_map/all_gather | solution.py:141
  35.2 45.7 %all-gather.12.cloned.1.call-done = bf16[12,512,128]{2,1,0:T(8,128)(2,1)} async-done(((bf16[12,64,128]{2,1,0:T(8,128)(2,1)}), bf16[12,512,128]{2,1,0:T(8,128)(2,1)}) %all-gather.12.cloned.1.call-update) | async-done | bytes 1572880 | tf_op jit(solution)/shard_map/all_gather | solution.py:246
  95.6 4.6 multiply_add_fusion
  111.2 25.6 %fusion = f32[296,512]{1,0:T(8,128)S(1)} fusion(f32[1176,512]{1,0:T(8,128)} %fusion.190), kind=kCustom, calls=%all-reduce-scatter | all-reduce-scatter fusion | flops 606209 | bytes 3015168
  147.5 15.0 %all-gather.16.cloned.1.call-done = bf16[4,294,512]{2,1,0:T(8,128)(2,1)} async-done(((bf16[1,294,512]{2,1,0:T(8,128)(2,1)}), bf16[4,294,512]{2,1,0:T(8,128)(2,1)}) %all-gather.16.cloned.1.call-update) | async-done | bytes 1204240 | tf_op jit(solution)/shard_map/all_gather | solution.py:141
  165.1 3.6 multiply_convert_fusion.1
  174.8 27.1 %fusion.2 = f32[296,512]{1,0:T(8,128)} fusion(f32[1176,512]{1,0:T(8,128)} %convolution_bitcast_fusion.1), kind=kCustom, calls=%all-reduce-scatter.2 | all-reduce-scatter fusion | flops 606209 | bytes 3015168
  207.7 3.4 concatenate.38
  233.7 3.5 fusion.41
  239.2 3.3 convolution_bitcast_fusion.2
  248.4 3.6 fusion.25
  266.1 4.4 fusion.153
  284.0 3.6 multiply_reduce_fusion
  291.4 4.6 fusion.29
  312.0 44.4 %fusion.264 = (f32[296,512]{1,0:T(8,128)S(1)}, f32[296,512]{1,0:T(8,128)}) fusion(f32[1176,512]{1,0:T(8,128)} %convolution_bitcast_fusion.2, f32[1176,512]{1,0:T(8,128)} %convolution_bitcast_fusion), kind=kCustom, calls=%all-reduce-scatter.4 | all-reduce-scatter fusion | flops 1212417 | bytes 6029824
  362.4 6.2 %all-to-all-start = ((bf16[8,12,64,128]{3,2,1,0:T(8,128)(2,1)}), bf16[8,12,64,128]{3,2,1,0:T(8,128)(2,1)S(1)}, u32[]{:S(2)}, u32[]{:S(2)}) async-start(bf16[8,12,64,128]{3,2,1,0:T(8,128)(2,1)} %copy.219), calls=%async_computation | async-start | bytes 3145728 | tf_op jit(solution)/shard_map/all_to_all | solution.py:36
  374.6 3.4 multiply_reduce_fusion.58
  380.1 5.8 multiply_reduce_fusion.50
  389.2 3.6 concatenate.37
  396.1 118.7 %all-reduce.16.cloned.1.call-done = f32[71,512]{1,0:T(8,128)} async-done(((f32[71,512]{1,0:T(8,128)}), f32[71,512]{1,0:T(8,128)}) %all-reduce.16.cloned.1.call-update) | async-done | bytes 145424 | tf_op jit(solution)/shard_map/psum | solution.py:390
  517.7 14.9 %all-gather.18.cloned.1.call-done = bf16[4,294,512]{2,1,0:T(8,128)(2,1)} async-done(((bf16[1,294,512]{2,1,0:T(8,128)(2,1)}), bf16[4,294,512]{2,1,0:T(8,128)(2,1)}) %all-gather.18.cloned.1.call-update) | async-done | bytes 1204240 | tf_op jit(solution)/shard_map/all_gather | solution.py:347
  535.7 7.2 %psum.35 = f32[12,64]{1,0:T(8,128)S(1)} all-reduce(f32[12,64]{1,0:T(8,128)S(1)} %get-tuple-element.80), channel_id=1, replica_groups=mesh['dp'=8,'head'=4] {'head'}, use_global_device_ids=true, to_apply=%region_18.19 | all-reduce | flops 768 | bytes 6144 | tf_op jit(solution)/shard_map/psum | solution.py:392
  543.1 19.1 %all-reduce.12 = (f32[12,128]{1,0:T(8,128)S(1)}, f32[12]{0:T(128)S(1)}) all-reduce(f32[12,128]{1,0:T(8,128)S(1)} %get-tuple-element.79, f32[12]{0:T(128)S(1)} %get-tuple-element.99), channel_id=1, replica_groups=mesh['dp'=8,'head'=4] {'dp'}, use_global_device_ids=true, to_apply=%region_20.21 | all-reduce | flops 1548 | bytes 12384 | tf_op jit(solution)/shard_map/psum | solution.py:394
  565.2 41.7 %psum.38 = f32[12]{0:T(128)S(1)} all-reduce(f32[12]{0:T(128)S(1)} %multiply_reduce_fusion.67), channel_id=1, replica_groups=mesh['dp'=8,'head'=4] {'dp','head'}, use_global_device_ids=true, to_apply=%region_24.25 | all-reduce | flops 12 | bytes 96 | tf_op jit(solution)/shard_map/psum | solution.py:398
  (640 shorter events, 173.8 us)
Async XLA Ops:
  7.2 25.4 %all-gather.14.cloned.1.call-start = ((), (), s32[]{:S(2)}) async-start(), calls=%async_computation.3 | async-start | bytes 1515520 | tf_op jit(solution)/shard_map/all_gather | solution.py:141
  14.5 66.3 %all-gather.12.cloned.1.call-start = ((), (), s32[]{:S(2)}) async-start(), calls=%async_computation.1 | async-start | bytes 1769472 | tf_op jit(solution)/shard_map/all_gather | solution.py:246
  15.3 147.2 %all-gather.16.cloned.1.call-start = ((), (), s32[]{:S(2)}) async-start(), calls=%async_computation.4 | async-start | bytes 1515520 | tf_op jit(solution)/shard_map/all_gather | solution.py:141
  15.5 67.5 %copy-start.73 = (pred[24]{0:T(512)(128)(4,1)}, pred[24]{0:T(512)(128)(4,1)S(1)}, u32[]{:S(2)}) copy-start(pred[24]{0:T(512)(128)(4,1)S(1)} %eq.44) | copy-start | bytes 76
  16.5 78.4 %copy-start.161 = (f32[128]{0:T(128)}, f32[128]{0:T(128)S(1)}, u32[]{:S(2)}) copy-start(f32[128]{0:T(128)S(1)} %get-tuple-element.183) | copy-start | bytes 1540
  19.2 76.0 %copy-start.77 = (f32[128]{0:T(128)}, f32[128]{0:T(128)S(1)}, u32[]{:S(2)}) copy-start(f32[128]{0:T(128)S(1)} %get-tuple-element.169) | copy-start | bytes 1540
  19.2 76.0 %copy-start.79 = (f32[128]{0:T(128)}, f32[128]{0:T(128)S(1)}, u32[]{:S(2)}) copy-start(f32[128]{0:T(128)S(1)} %get-tuple-element.170) | copy-start | bytes 1540
  19.2 76.0 %copy-start.81 = (f32[128]{0:T(128)}, f32[128]{0:T(128)S(1)}, u32[]{:S(2)}) copy-start(f32[128]{0:T(128)S(1)} %get-tuple-element.171) | copy-start | bytes 1540
  19.2 76.0 %copy-start.83 = (f32[128]{0:T(128)}, f32[128]{0:T(128)S(1)}, u32[]{:S(2)}) copy-start(f32[128]{0:T(128)S(1)} %get-tuple-element.172) | copy-start | bytes 1540
  136.9 5.1 collective-permute-start
  147.2 95.4 %all-gather.20.cloned.1.call-start = ((), (), s32[]{:S(2)}) async-start(), calls=%async_computation.6 | async-start | bytes 1515520 | tf_op jit(solution)/shard_map/all_gather | solution.py:141
  202.6 5.0 collective-permute-start.2
  357.3 14.3 %collective-permute-start.3 = (f32[6,512]{1,0:T(8,128)S(1)}, f32[6,512]{1,0:T(8,128)S(1)}, u32[]{:S(2)}, u32[]{:S(2)}) collective-permute-start(f32[6,512]{1,0:T(8,128)S(1)} %slice.947), channel_id=1, source_target_pairs={{0,1},{1,2},{2,3},{4,5},{5,6},{6,7},{8,9},{9,10},{10,11},{12,13},{... | collective-permute-start | bytes 36872
  362.4 172.9 %all-to-all-start = ((bf16[8,12,64,128]{3,2,1,0:T(8,128)(2,1)}), bf16[8,12,64,128]{3,2,1,0:T(8,128)(2,1)S(1)}, u32[]{:S(2)}, u32[]{:S(2)}) async-start(bf16[8,12,64,128]{3,2,1,0:T(8,128)(2,1)} %copy.219), calls=%async_computation | async-start | bytes 3145728 | tf_op jit(solution)/shard_map/all_to_all | solution.py:36
  368.6 146.3 %all-reduce.16.cloned.1.call-start = ((), (), s32[]{:S(2)}) async-start(), calls=%async_computation.2 | async-start | bytes 294912 | tf_op jit(solution)/shard_map/psum | solution.py:390
  369.2 20.0 %collective-permute-start.1 = (f32[6,512]{1,0:T(8,128)}, f32[6,512]{1,0:T(8,128)}, u32[]{:S(2)}, u32[]{:S(2)}) collective-permute-start(f32[6,512]{1,0:T(8,128)} %slice.945), channel_id=1, source_target_pairs={{0,1},{1,2},{2,3},{4,5},{5,6},{6,7},{8,9},{9,10},{10,11},{12,13},{... | collective-permute-start | bytes 36872
  389.1 143.5 %all-gather.18.cloned.1.call-start = ((), (), s32[]{:S(2)}) async-start(), calls=%async_computation.5 | async-start | bytes 1515520 | tf_op jit(solution)/shard_map/all_gather | solution.py:347
  394.8 167.8 %all-gather.22.cloned.1.call-start = ((), (), s32[]{:S(2)}) async-start(), calls=%async_computation.7 | async-start | bytes 1515520 | tf_op jit(solution)/shard_map/all_gather | solution.py:348
  395.2 119.6 %copy-start.47 = (f32[71,512]{1,0:T(8,128)S(1)}, f32[71,512]{1,0:T(8,128)}, u32[]{:S(2)}) copy-start(f32[71,512]{1,0:T(8,128)} %param.20) | copy-start | bytes 436228
  395.2 120.7 %copy-start.42 = (f32[71,512]{1,0:T(8,128)S(1)}, f32[71,512]{1,0:T(8,128)}, u32[]{:S(2)}) copy-start(f32[71,512]{1,0:T(8,128)} %param.19) | copy-start | bytes 436228
  395.2 120.7 %copy-start.48 = (f32[71,512]{1,0:T(8,128)S(1)}, f32[71,512]{1,0:T(8,128)}, u32[]{:S(2)}) copy-start(f32[71,512]{1,0:T(8,128)} %param.21) | copy-start | bytes 436228
  535.5 71.4 %copy-start.4 = (f32[12,64,128]{2,1,0:T(8,128)}, f32[12,64,128]{2,1,0:T(8,128)S(1)}, u32[]{:S(2)}) copy-start(f32[12,64,128]{2,1,0:T(8,128)S(1)} %convert_reduce_fusion) | copy-start | bytes 1179652
  535.5 71.4 %copy-start.32 = (f32[12,64,128]{2,1,0:T(8,128)S(1)}, f32[12,64,128]{2,1,0:T(8,128)}, u32[]{:S(2)}) copy-start(f32[12,64,128]{2,1,0:T(8,128)} %param.15) | copy-start | bytes 1179652
  535.5 71.4 %copy-start.44 = (f32[12,64,128]{2,1,0:T(8,128)S(1)}, f32[12,64,128]{2,1,0:T(8,128)}, u32[]{:S(2)}) copy-start(f32[12,64,128]{2,1,0:T(8,128)} %param.18) | copy-start | bytes 1179652
  (206 other events, 1472.2 us)
Sparse Core Ops, SparseCore 0:
  14.7 17.8 all-gather.13
  35.3 45.4 all-gather.11
  147.3 15.1 all-gather.15
  216.8 17.6 all-gather.19
  389.2 125.5 all-reduce.15
  516.8 15.7 all-gather.17
  534.7 17.6 all-gather.21
where the time goes:
time: 630 us; the launch traced here: 617 us
  waiting for transfers between devices  211 us (33%)
  blocking collectives  165 us (26%)
  local copies, waits for them, and re-layouts  93.3 us (15%)
  other arithmetic  58.2 us (9%)
  matrix products  56.5 us (9%)
  between operations  18.6 us (3%)
  starting transfers between devices  14.4 us (2%)
    psum x1, waiting for transfers between devices, local(): small_total = lax.psum(full_part + placed, ('dp', 'head'))  119 us
    unnamed x3, blocking collectives  97.1 us
    all_gather x1, waiting for transfers between devices, local(): lax.all_gather(weights.astype(jnp.bfloat16), 'dp', axis=1, tiled=True)  45.7 us
    psum x1, blocking collectives, local(): update_sq = lax.psum(jnp.sum(update * update, axis=(1, 2)), ('dp', 'head'))  41.7 us
    unnamed x451, local copies, waits for them, and re-layouts  31.8 us
    all_gather x3, waiting for transfers between devices, share_rows(): return lax.all_gather(rows, 'head', axis=0, tiled=True)  26.9 us
    psum x1, blocking collectives, local(): lax.psum((jnp.sum(squares, axis=1), jnp.sum(new_rows, axis=1)), 'dp')  19.1 us
    reduce_sum x5, other arithmetic, conv_grid_back(): jnp.sum(upstream * padded_src[:, row_tap:row_tap + GRID, col_tap:col_tap...  16 us
  transfers between devices with their start and end apart: 12, of which 7 were waited for; matrix products, arithmetic and copies ran while one was open for 11% of the time, Pallas kernels for 0%

commit v1 on v0

v1 whole, which is shorter than its diff:
```python
import math

import jax
import jax.numpy as jnp
from jax import lax
from jax.experimental import pallas as pl
from jax.experimental.pallas import tpu as pltpu
from jax.sharding import PartitionSpec as P

D = 512
HEAD_DIM = 64
GRID = 7
SMALL_GRID = 3
WINDOW = 7
IMG_GROUP = 3
CELLS = GRID * GRID
SLOTS = 8
CELL_PAD = CELLS + 1
ROWS = CELL_PAD * SLOTS
LANES = 128
WIDE = 256
REACHES = (1, 2, 3, 3)
HALO = WINDOW // 2

NORM_EPS = 1e-06
SQUARE_FLOOR = 1e-30
SECOND_DECAY = 0.999
STEP_RATE = 0.02
SMALL_RATE = 0.05
AVERAGE_KEEP = 0.9
NEG_LARGE = -1e30
ROOT_HALF = 0.7071067811865476
INV_ROOT_TAU = 0.3989422804014327
INV_SCALE = 1.0 / math.sqrt(HEAD_DIM)

F32 = jnp.float32
BF16 = jnp.bfloat16
NN = (((1,), (0,)), ((), ()))
NT = (((1,), (1,)), ((), ()))
TN = (((0,), (0,)), ((), ()))


def dot(a, b, dims=NN):
    return lax.dot_general(a, b, dims, preferred_element_type=F32)


def lane_block(b):
    return slice(b * WIDE, (b + 1) * WIDE)


def wide(col):
    return jnp.concatenate([col] * (D // LANES), axis=1)


def rows_loop(count, size, body, init=None, unroll=1):
    def step(j, carry):
        return body(pl.multiple_of(j * size, size), carry)

    return lax.fori_loop(0, count // size, step, init, unroll=unroll)


def conv(src, halo, tap, reach, lanes, put):
    def line(y, _):
        sums = [jnp.zeros((SLOTS, LANES), F32) for _ in range(GRID)]
        for a in range(-reach, reach + 1):
            base = (y + (a + halo)) * GRID
            cells = [src[base + x, :, lanes] for x in range(GRID)]
            for b in range(-reach, reach + 1):
                t = tap(a, b)
                for x in range(GRID):
                    if 0 <= x + b < GRID:
                        sums[x] = sums[x] + t * cells[x + b]
        for x in range(GRID):
            put(y * GRID + x, sums[x])
        return 0

    lax.fori_loop(0, GRID, line, 0)


def tap_sums(up, src, halo, reach, lanes, put):
    for a in range(-reach, reach + 1):

        def line(y, sums):
            sums = list(sums)
            ups = [up(y * GRID + x) for x in range(GRID)]
            base = (y + (a + halo)) * GRID
            cells = [src[base + x, :, lanes] for x in range(GRID)]
            for i, b in enumerate(range(-reach, reach + 1)):
                for x in range(GRID):
                    if 0 <= x + b < GRID:
                        sums[i] = sums[i] + ups[x] * cells[x + b]
            return tuple(sums)

        start = tuple(jnp.zeros((SLOTS, LANES), F32) for _ in range(2 * reach + 1))
        sums = lax.fori_loop(0, GRID, line, start)
        for i, b in enumerate(range(-reach, reach + 1)):
            put(a, b, jnp.sum(sums[i], axis=0, keepdims=True))


def fold(x):
    return jnp.sum(x.reshape(x.shape[0] // SLOTS, SLOTS, x.shape[1]), axis=0)


def erf_parts(h):
    e = lax.erf(h * ROOT_HALF)
    half = 0.5 * (1.0 + e)
    return h * half, half + h * jnp.exp(-0.5 * h * h) * INV_ROOT_TAU


def norm_rows(v, gain, shift):
    centre = jnp.sum(v, axis=1, keepdims=True) * (1.0 / D)
    offset = v - centre
    spread = jnp.sum(offset * offset, axis=1, keepdims=True) * (1.0 / D)
    inverse = lax.rsqrt(spread + NORM_EPS)
    unit = offset * inverse
    return unit * gain + shift, unit, inverse


def norm_back(up, unit, inverse, gain):
    z = up * gain
    mean_z = jnp.sum(z, axis=1, keepdims=True) * (1.0 / D)
    mean_zu = jnp.sum(z * unit, axis=1, keepdims=True) * (1.0 / D)
    return inverse * (z - mean_z - unit * mean_zu)


class Block:
    def __init__(self, refs):
        self.__dict__.update(refs)

    def matrix(self, k, lo, hi):
        parts = []
        for h in range(lo, hi):
            part = self.w[h, :, k]
            if part.shape[1] % 16:
                part = part.astype(F32).reshape(D, LANES).astype(BF16)
            else:
                part = part.reshape(D, LANES)
            parts.append(part)
        return jnp.concatenate(parts, axis=1)

    def times(self, lhs, k, b):
        return dot(lhs, self.matrix(k, 2 * b, 2 * b + 2))

    def times_t(self, lhs, k, b):
        return dot(lhs, self.matrix(k, 0, 4)[lane_block(b), :], NT)

    def put_grad(self, k, lhs_t, rhs):
        for b in range(2):
            g = dot(lhs_t, rhs[:, lane_block(b)])
            for i in range(2):
                piece = g[:, i * LANES : (i + 1) * LANES]
                rows = self.g.shape[3]
                piece = piece.reshape(D // rows, rows, LANES)
                self.g[2 * b + i, :, k] = piece.astype(BF16)

    def row(self, j):
        return self.small[j : j + 1, :]

    def setup(self):
        head = lax.axis_index("head")
        slots = self.cls.shape[1]
        self.sums[...] = jnp.zeros(self.sums.shape, F32)
        sub = lax.broadcasted_iota(jnp.int32, (SLOTS, LANES), 0)
        valid = jnp.where(sub < slots, 1.0, 0.0)
        full = jnp.zeros((SLOTS, LANES), F32)
        images = [jnp.zeros((SLOTS, LANES), F32) for _ in range(IMG_GROUP)]
        for s in range(slots):
            full = jnp.where(sub == s, jnp.where(self.cls[head, s] == 0, 1.0, 0.0), full)
            for i in range(IMG_GROUP):
                images[i] = jnp.where(
                    sub == s, jnp.where(self.img[head, s] == i, 1.0, 0.0), images[i]
                )
        for cell in range(CELLS):
            small = cell // GRID < SMALL_GRID and cell % GRID < SMALL_GRID
            self.live[cell * SLOTS : (cell + 1) * SLOTS, :] = valid if small else full
        self.live[CELLS * SLOTS :, :] = jnp.zeros((SLOTS, LANES), F32)
        for i in range(IMG_GROUP):
            self.im8[i] = images[i]
            self.im16[i] = jnp.concatenate([images[i], images[i]], axis=0).astype(BF16)
        self.pos_src[0:GRID] = jnp.zeros((GRID, SLOTS, D), F32)
        self.pos_src[GRID + CELLS :] = jnp.zeros((GRID, SLOTS, D), F32)
        for pad in (self.rel_src, self.dq_src):
            pad[0 : HALO * GRID] = jnp.zeros((HALO * GRID, SLOTS, D), F32)
            pad[HALO * GRID + CELLS :] = jnp.zeros((HALO * GRID, SLOTS, D), F32)
        tap = lax.broadcasted_iota(jnp.int32, (WINDOW * WINDOW, 1), 0)
        row_off = jnp.abs(tap // WINDOW - HALO)
        col_off = jnp.abs(tap % WINDOW - HALO)
        off = jnp.maximum(row_off, col_off)
        heads = lax.broadcasted_iota(jnp.int32, (1, D), 1) // HEAD_DIM
        reach = jnp.where(heads < 2, 1, jnp.where(heads < 5, 2, 3))
        mask = jnp.where(off <= reach, 1.0, 0.0)
        self.window[...] = mask
        self.rel_taps[...] = self.small[22 : 22 + WINDOW * WINDOW, :] * mask

    def place(self, rows_ref, first, r0, size):
        count = rows_ref.shape[0]
        r = r0 + lax.broadcasted_iota(jnp.int32, (size, 1), 0)
        cell, slot = r >> 3, r & 7
        want = first + slot * CELLS + cell
        want = jnp.where((slot < self.cls.shape[1]) & (cell < CELLS), want, -1)
        col = lax.broadcasted_iota(jnp.int32, (size, count), 1)
        pick = jnp.where(col == want, 1.0, 0.0).astype(BF16)
        return dot(pick, rows_ref[...])

    def unplace(self, src_ref, out_ref):
        count = out_ref.shape[0]
        r = lax.broadcasted_iota(jnp.int32, (1, ROWS), 1)
        cell, slot = r >> 3, r & 7
        target = jnp.where((slot < self.cls.shape[1]) & (cell < CELLS), slot * CELLS + cell, -1)
        t = lax.broadcasted_iota(jnp.int32, (count, ROWS), 0)
        pick = jnp.where(t == target, 1.0, 0.0).astype(BF16)
        out_ref[...] = dot(pick, src_ref[...]).astype(BF16)

    def read(self):
        first = lax.axis_index("head") * (self.cls.shape[1] * CELLS)
        size = 80

        def body(r0, _):
            live = wide(self.live[pl.ds(r0, size), :])
            x = self.place(self.tokens, first, r0, size)
            self.first[pl.ds(r0, size), :] = x
            c0 = r0 // SLOTS
            self.pos_src[pl.ds(GRID + c0, size // SLOTS)] = (x * live).reshape(-1, SLOTS, D)
            c = self.place(self.cot, first, r0, size)
            self.go[pl.ds(r0, size), :] = (c * live).astype(BF16)
            return 0

        rows_loop(ROWS, size, body, 0)

    def norm_one(self):
        for c in range(D // LANES):
            lanes = slice(c * LANES, (c + 1) * LANES)

            def put(cell, value):
                rows = pl.ds(pl.multiple_of(cell * SLOTS, SLOTS), SLOTS)
                self.first[rows, lanes] = self.first[rows, lanes] + value + self.small[8:9, lanes]

            def tap(a, b):
                t = 13 + (a + 1) * 3 + b + 1
                return self.small[t : t + 1, lanes]

            conv(self.pos_src, 1, tap, 1, lanes, put)

        def body(r0, _):
            rows = pl.ds(r0, 16)
            n, u, inv = norm_rows(self.first[rows, :], self.row(0), self.row(1))
            self.n1[rows, :] = n.astype(BF16)
            self.u1[rows, :] = u
            self.inv1[rows, :] = jnp.broadcast_to(inv, (16, LANES))
            return 0

        rows_loop(ROWS, 16, body, 0, unroll=5)

    def project(self):
        for b in range(2):
            cols = lane_block(b)
            self.q[:, cols] = (self.times(self.n1[...], 0, b) + self.small[2:3, cols]).astype(BF16)
            self.k[:, cols] = self.times(self.n1[...], 1, b).astype(BF16)
            self.v[:, cols] = (self.times(self.n1[...], 2, b) + self.small[3:4, cols]).astype(BF16)

    def image_sum(self, x):
        total = jnp.zeros((SLOTS, D), F32)
        for i in range(IMG_GROUP):
            im = wide(self.im8[i])
            total = total + im * jnp.sum(im * x, axis=0, keepdims=True)
        return total

    def softmax(self):
        def top(r0, best):
            live = wide(self.live[pl.ds(r0, 16), :])
            keys = jnp.where(live > 0, self.k[pl.ds(r0, 16), :].astype(F32), NEG_LARGE)
            return jnp.maximum(best, jnp.max(keys.reshape(2, SLOTS, D), axis=0))

        best = rows_loop(ROWS, 16, top, jnp.full((SLOTS, D), NEG_LARGE, F32), unroll=5)
        shift = jnp.zeros((SLOTS, D), F32)
        for i in range(IMG_GROUP):
            im = wide(self.im8[i])
            most = jnp.max(jnp.where(im > 0, best, NEG_LARGE), axis=0, keepdims=True)
            shift = jnp.where(im > 0, most, shift)
        shift2 = jnp.concatenate([shift, shift], axis=0)

        def raise_(r0, total):
            rows = pl.ds(r0, 16)
            live = wide(self.live[rows, :])
            keys = self.k[rows, :].astype(F32)
            e = jnp.where(live > 0, jnp.exp(jnp.where(live > 0, keys - shift2, 0.0)), 0.0)
            self.soft[rows, :] = e
            return total + fold(e)

        total = self.image_sum(
            rows_loop(ROWS, 16, raise_, jnp.zeros((SLOTS, D), F32), unroll=5)
        )
        scale = 1.0 / jnp.where(total > 0, total, 1.0)
        scale2 = jnp.concatenate([scale, scale], axis=0)

        def divide(r0, _):
            rows = pl.ds(r0, 16)
            soft = self.soft[rows, :] * scale2
            self.soft[rows, :] = soft
            self.soft_low[rows, :] = soft.astype(BF16)
            return 0

        rows_loop(ROWS, 16, divide, 0, unroll=5)

    def by_image(self, x):
        tiles = x.reshape(ROWS // 16, 16, WIDE)
        parts = []
        for i in range(IMG_GROUP):
            im = jnp.concatenate([self.im16[i]] * (WIDE // LANES), axis=1)
            parts.append((tiles * im[None]).reshape(ROWS, WIDE))
        return jnp.concatenate(parts, axis=1)

    def head_blocks(self, x):
        r = lax.broadcasted_iota(jnp.int32, x.shape, 0) // HEAD_DIM
        c = (lax.broadcasted_iota(jnp.int32, x.shape, 1) % WIDE) // HEAD_DIM
        return jnp.where(r == c, x, 0.0).astype(BF16)

    def stacked(self, x):
        return jnp.concatenate([x[:, lane_block(i)] for i in range(IMG_GROUP)], axis=0)

    def attend(self):
        for b in range(2):
            cols = lane_block(b)
            ctx = dot(self.soft_low[:, cols], self.by_image(self.v[:, cols]), TN)
            ctx = self.head_blocks(ctx)
            self.ctx[b] = ctx
            self.factor[:, cols] = dot(self.by_image(self.q[:, cols]), self.stacked(ctx))

        def fill(r0, _):
            rows = pl.ds(r0, 16)
            v = self.v[rows, :].astype(F32) * wide(self.live[rows, :])
            c0 = r0 // SLOTS
            self.rel_src[pl.ds(HALO * GRID + c0, 2)] = v.reshape(2, SLOTS, D)
            return 0

        rows_loop(ROWS, 16, fill, 0, unroll=5)
        for c in range(D // LANES):
            lanes = slice(c * LANES, (c + 1) * LANES)

            def put(cell, value):
                rows = pl.ds(pl.multiple_of(cell * SLOTS, SLOTS), SLOTS)
                self.rel[rows, lanes] = value

            def tap(a, b):
                t = (a + HALO) * WINDOW + b + HALO
                return self.rel_taps[t : t + 1, lanes]

            conv(self.rel_src, HALO, tap, REACHES[c], lanes, put)
        self.rel[CELLS * SLOTS :, :] = jnp.zeros((SLOTS, D), F32)

        def mix(r0, _):
            rows = pl.ds(r0, 16)
            m = self.factor[rows, :] * INV_SCALE + self.q[rows, :].astype(F32) * self.rel[rows, :]
            self.mixed[rows, :] = (m * wide(self.live[rows, :])).astype(BF16)
            return 0

        rows_loop(ROWS, 16, mix, 0, unroll=5)

    def norm_two(self):
        for b in range(2):
            cols = lane_block(b)
            p = self.times_t(self.mixed[...], 3, b)
            self.second[:, cols] = self.first[:, cols] + p + self.small[4:5, cols]

        def body(r0, _):
            rows = pl.ds(r0, 16)
            n, u, inv = norm_rows(self.second[rows, :], self.row(5), self.row(6))
            self.n2[rows, :] = n.astype(BF16)
            self.u2[rows, :] = u
            self.inv2[rows, :] = jnp.broadcast_to(inv, (16, LANES))
            return 0

        rows_loop(ROWS, 16, body, 0, unroll=5)

    def up(self, r):
        for b in range(2):
            cols = lane_block(b)
            h = self.times(self.n2[...], 4 + r, b) + self.small[pl.ds(9 + r, 1), cols]
            self.slope[r, :, cols] = h

        def body(r0, _):
            rows = pl.ds(r0, 16)
            act, slope = erf_parts(self.slope[r, rows, :])
            self.active[r, rows, :] = act.astype(BF16)
            self.slope[r, rows, :] = slope
            return 0

        rows_loop(ROWS, 16, body, 0, unroll=5)

    def down(self, r):
        for b in range(2):
            cols = lane_block(b)
            self.second[:, cols] += self.times_t(self.active[r], 8 + r, b)

    def finish_out(self):
        def body(r0, _):
            rows = pl.ds(r0, 16)
            self.low[rows, :] = (self.second[rows, :] + self.row(7)).astype(BF16)
            return 0

        rows_loop(ROWS, 16, body, 0, unroll=5)
        self.unplace(self.low, self.out)

    def grad_hidden(self, r):
        go = self.go[...]
        for b in range(2):
            cols = lane_block(b)
            self.factor[:, cols] = self.times(go, 8 + r, b)

        def body(r0, total):
            rows = pl.ds(r0, 16)
            g = self.factor[rows, :] * self.slope[r, rows, :]
            self.low[rows, :] = g.astype(BF16)
            return total + fold(g)

        total = rows_loop(ROWS, 16, body, jnp.zeros((SLOTS, D), F32), unroll=5)
        self.sums[pl.ds(9 + r, 1), :] = jnp.sum(total, axis=0, keepdims=True)

    def back_mlp(self, r):
        self.grad_hidden(r)
        self.put_grad(8 + r, self.go_t[...], self.active[r])
        self.put_grad(4 + r, self.n2_t[...], self.low[...])
        for b in range(2):
            cols = lane_block(b)
            self.back[:, cols] += self.times_t(self.low[...], 4 + r, b)

    def back_two(self):
        zero = jnp.zeros((SLOTS, D), F32)

        def body(r0, sums):
            rows = pl.ds(r0, 16)
            back, u = self.back[rows, :], self.u2[rows, :]
            go = self.go[rows, :].astype(F32)
            gs = go + norm_back(back, u, wide(self.inv2[rows, :]), self.row(5))
            self.second[rows, :] = gs
            self.low[rows, :] = gs.astype(BF16)
            new = (gs, back * u, back, go)
            return tuple(s + fold(n) for s, n in zip(sums, new, strict=True))

        sums = rows_loop(ROWS, 16, body, (zero,) * 4, unroll=5)
        for j, s in zip((4, 5, 6, 7), sums, strict=True):
            self.sums[j : j + 1, :] = jnp.sum(s, axis=0, keepdims=True)

    def back_attend(self):
        self.put_grad(3, self.low[...].T, self.mixed[...])
        for b in range(2):
            cols = lane_block(b)
            self.factor[:, cols] = self.times(self.low[...], 3, b)

        def fill(r0, _):
            rows = pl.ds(r0, 16)
            d = self.factor[rows, :] * wide(self.live[rows, :])
            self.factor[rows, :] = d
            self.f[rows, :] = (d * INV_SCALE).astype(BF16)
            c0 = r0 // SLOTS
            dq = d * self.q[rows, :].astype(F32)
            self.dq_src[pl.ds(HALO * GRID + c0, 2)] = dq.reshape(2, SLOTS, D)
            return 0

        rows_loop(ROWS, 16, fill, 0, unroll=5)
        for b in range(2):
            cols = lane_block(b)
            f3 = self.by_image(self.f[:, cols])
            g = self.head_blocks(dot(self.q[:, cols], f3, TN))
            self.gq[:, cols] = dot(f3, self.ctx[b], NT)
            self.gk[:, cols] = dot(self.by_image(self.v[:, cols]), g, NT)
            self.gv[:, cols] = dot(self.by_image(self.soft_low[:, cols]), self.stacked(g))

        for c in range(D // LANES):
            lanes = slice(c * LANES, (c + 1) * LANES)

            def put(cell, value):
                rows = pl.ds(pl.multiple_of(cell * SLOTS, SLOTS), SLOTS)
                self.gv[rows, lanes] = self.gv[rows, lanes] + value * self.live[rows, :]

            def tap(a, b):
                t = (HALO - a) * WINDOW + HALO - b
                return self.rel_taps[t : t + 1, lanes]

            conv(self.dq_src, HALO, tap, REACHES[c], lanes, put)

            def up(cell):
                return self.dq_src[HALO * GRID + cell, :, lanes]

            def put_tap(a, b, value):
                t = (a + HALO) * WINDOW + b + HALO
                keep = self.window[t : t + 1, lanes]
                self.sums[22 + t : 23 + t, lanes] = value * keep

            tap_sums(up, self.rel_src, HALO, REACHES[c], lanes, put_tap)

        zero = jnp.zeros((SLOTS, D), F32)

        def inner(r0, total):
            rows = pl.ds(r0, 16)
            return total + fold(self.soft[rows, :] * self.gk[rows, :])

        shared = self.image_sum(rows_loop(ROWS, 16, inner, zero, unroll=5))
        shared2 = jnp.concatenate([shared, shared], axis=0)

        def low(r0, sums):
            rows = pl.ds(r0, 16)
            gq = self.gq[rows, :] + self.factor[rows, :] * self.rel[rows, :]
            gk = self.soft[rows, :] * (self.gk[rows, :] - shared2)
            gv = self.gv[rows, :]
            self.gl[0, rows, :] = gq.astype(BF16)
            self.gl[1, rows, :] = gk.astype(BF16)
            self.gl[2, rows, :] = gv.astype(BF16)
            return sums[0] + fold(gq), sums[1] + fold(gv)

        sums = rows_loop(ROWS, 16, low, (zero, zero), unroll=5)
        for j, s in zip((2, 3), sums, strict=True):
            self.sums[j : j + 1, :] = jnp.sum(s, axis=0, keepdims=True)

    def back_project(self):
        n1_t = self.n1[...].T
        for k in range(3):
            self.put_grad(k, n1_t, self.gl[k])
        for b in range(2):
            cols = lane_block(b)
            back = self.times_t(self.gl[0], 0, b)
            back = back + self.times_t(self.gl[1], 1, b)
            self.back[:, cols] = back + self.times_t(self.gl[2], 2, b)

    def back_one(self):
        zero = jnp.zeros((SLOTS, D), F32)
        self.pos_up[0:GRID] = jnp.zeros((GRID, SLOTS, D), F32)
        self.pos_up[GRID + CELLS :] = jnp.zeros((GRID, SLOTS, D), F32)

        def body(r0, sums):
            rows = pl.ds(r0, 16)
            back, u = self.back[rows, :], self.u1[rows, :]
            gf = self.second[rows, :] + norm_back(back, u, wide(self.inv1[rows, :]), self.row(0))
            c0 = r0 // SLOTS
            self.pos_up[pl.ds(GRID + c0, 2)] = gf.reshape(2, SLOTS, D)
            new = (back * u, back, gf)
            return tuple(s + fold(n) for s, n in zip(sums, new, strict=True))

        sums = rows_loop(ROWS, 16, body, (zero,) * 3, unroll=5)
        for j, s in zip((0, 1, 8), sums, strict=True):
            self.sums[j : j + 1, :] = jnp.sum(s, axis=0, keepdims=True)
        for c in range(D // LANES):
            lanes = slice(c * LANES, (c + 1) * LANES)

            def put(cell, value):
                rows = pl.ds(pl.multiple_of(cell * SLOTS, SLOTS), SLOTS)
                gf = self.pos_up[GRID + cell, :, lanes]
                self.first[rows, lanes] = gf + value * self.live[rows, :]

            def tap(a, b):
                t = 13 + (1 - a) * 3 + 1 - b
                return self.small[t : t + 1, lanes]

            conv(self.pos_up, 1, tap, 1, lanes, put)

            def up(cell):
                return self.pos_up[GRID + cell, :, lanes]

            def put_tap(a, b, value):
                t = 13 + (a + 1) * 3 + b + 1
                self.sums[t : t + 1, lanes] = value

            tap_sums(up, self.pos_src, 1, 1, lanes, put_tap)

        def down(r0, _):
            rows = pl.ds(r0, 16)
            self.low[rows, :] = self.first[rows, :].astype(BF16)
            return 0

        rows_loop(ROWS, 16, down, 0, unroll=5)
        self.unplace(self.low, self.grad_in)


def scratch_of():
    f, h = (ROWS, D), (ROWS, LANES)
    halo3 = ((GRID + 2 * HALO) * GRID, SLOTS, D)
    halo1 = ((GRID + 2) * GRID, SLOTS, D)
    return {
        "live": (h, F32),
        "im8": ((IMG_GROUP, SLOTS, LANES), F32),
        "im16": ((IMG_GROUP, 16, LANES), BF16),
        "window": ((WINDOW * WINDOW, D), F32),
        "rel_taps": ((WINDOW * WINDOW, D), F32),
        "pos_src": (halo1, F32),
        "pos_up": (halo1, F32),
        "rel_src": (halo3, F32),
        "dq_src": (halo3, F32),
        "first": (f, F32),
        "u1": (f, F32),
        "inv1": (h, F32),
        "second": (f, F32),
        "u2": (f, F32),
        "inv2": (h, F32),
        "n1": (f, BF16),
        "n2": (f, BF16),
        "n2_t": ((D, ROWS), BF16),
        "go": (f, BF16),
        "go_t": ((D, ROWS), BF16),
        "q": (f, BF16),
        "k": (f, BF16),
        "v": (f, BF16),
        "soft": (f, F32),
        "soft_low": (f, BF16),
        "ctx": ((2, WIDE, IMG_GROUP * WIDE), BF16),
        "factor": (f, F32),
        "rel": (f, F32),
        "mixed": (f, BF16),
        "slope": ((4, ROWS, D), F32),
        "active": ((4, ROWS, D), BF16),
        "low": (f, BF16),
        "back": (f, F32),
        "f": (f, BF16),
        "gq": (f, F32),
        "gk": (f, F32),
        "gv": (f, F32),
        "gl": ((3, ROWS, D), BF16),
    }


def run_block(blk):
    blk.setup()
    blk.read()
    blk.norm_one()
    blk.project()
    blk.softmax()
    blk.attend()
    blk.norm_two()

    def forward(r, _):
        blk.up(r)
        blk.down(r)
        return 0

    lax.fori_loop(0, 4, forward, 0)
    blk.finish_out()
    blk.n2_t[...] = blk.n2[...].T
    blk.go_t[...] = blk.go[...].T
    blk.back[...] = jnp.zeros((ROWS, D), F32)

    def backward(r, _):
        blk.back_mlp(r)
        return 0

    lax.fori_loop(0, 4, backward, 0)
    blk.back_two()
    blk.back_attend()
    blk.back_project()
    blk.back_one()


def block_kernel(cls, img, tokens, cot, w, small, out, grad_in, g, sums, *scratch):
    refs = {"cls": cls, "img": img, "tokens": tokens, "cot": cot, "w": w, "small": small}
    refs.update({"out": out, "grad_in": grad_in, "g": g, "sums": sums})
    refs.update(zip(scratch_of(), scratch, strict=True))
    run_block(Block(refs))


def block_call(cls, img, tokens, cot, w, small):
    own = cls.shape[1] * CELLS
    smem = pl.BlockSpec(memory_space=pltpu.SMEM)
    vmem = pl.BlockSpec(memory_space=pltpu.VMEM)
    return pl.pallas_call(
        block_kernel,
        out_shape=(
            jax.ShapeDtypeStruct((own, D), BF16),
            jax.ShapeDtypeStruct((own, D), BF16),
            jax.ShapeDtypeStruct(w.shape, BF16),
            jax.ShapeDtypeStruct(small.shape, F32),
        ),
        in_specs=[smem, smem, vmem, vmem, vmem, vmem],
        out_specs=(vmem,) * 4,
        scratch_shapes=[pltpu.VMEM(*v) for v in scratch_of().values()],
        compiler_params=pltpu.CompilerParams(vmem_limit_bytes=63 << 20),
        name="block",
    )(cls, img, tokens, cot, w, small)


def local(
    tokens,
    cotangent,
    crop_image,
    crop_class,
    weights,
    row_state,
    col_state,
    weights_ema,
    small_params,
    small_state,
    small_ema,
):
    heads, parts = lax.axis_size("head"), lax.axis_size("dp")
    both = ("head", "dp")
    w = lax.all_gather(weights.astype(BF16), both, axis=0, tiled=False)
    w = w.reshape(heads, parts, *weights.shape)
    out, grad_in, g, sums = block_call(crop_class, crop_image, tokens, cotangent, w, small_params)
    out = lax.all_gather(out, "head", axis=0, tiled=True)
    grad_in = lax.all_gather(grad_in, "head", axis=0, tiled=True)
    g = g.reshape(heads * parts, *weights.shape)
    weight_grad = lax.all_to_all(g, both, split_axis=0, concat_axis=0, tiled=True)
    weight_grad = weight_grad.astype(F32).sum(axis=0)
    small_total = lax.psum(sums, ("dp", "head"))
    squares = weight_grad * weight_grad + SQUARE_FLOOR
    row_total = lax.psum(jnp.sum(squares, axis=2), "head")
    new_rows = SECOND_DECAY * row_state + (1.0 - SECOND_DECAY) * (row_total / D)
    col_total, row_mass = lax.psum((jnp.sum(squares, axis=1), jnp.sum(new_rows, axis=1)), "dp")
    new_cols = SECOND_DECAY * col_state + (1.0 - SECOND_DECAY) * (col_total / D)
    estimate = new_rows[:, :, None] * new_cols[:, None, :] / (row_mass / D)[:, None, None]
    update = weight_grad * lax.rsqrt(estimate)
    update_sq = lax.psum(jnp.sum(update * update, axis=(1, 2)), ("dp", "head"))
    update_rms = jnp.sqrt(update_sq / (D * D))
    new_weights = weights - STEP_RATE * update / jnp.maximum(1.0, update_rms)[:, None, None]
    new_ema = AVERAGE_KEEP * weights_ema + (1.0 - AVERAGE_KEEP) * new_weights
    new_small_state = SECOND_DECAY * small_state + (1.0 - SECOND_DECAY) * (
        small_total * small_total + SQUARE_FLOOR
    )
    small_update = small_total * lax.rsqrt(new_small_state)
    small_rms = jnp.sqrt(jnp.mean(small_update * small_update, axis=1))
    new_small = small_params - SMALL_RATE * small_update / jnp.maximum(1.0, small_rms)[:, None]
    new_small_ema = AVERAGE_KEEP * small_ema + (1.0 - AVERAGE_KEEP) * new_small
    return (
        out,
        grad_in,
        weight_grad,
        new_rows,
        new_cols,
        new_weights,
        new_weights.astype(BF16),
        new_ema,
        small_total,
        new_small_state,
        new_small,
        new_small_ema,
        jnp.concatenate([update_rms, small_rms]),
    )


def solution(mesh):
    in_specs = (
        P("dp", None),
        P("dp", None),
        P("dp", None),
        P("dp", None),
        P(None, "dp", "head"),
        P(None, "dp"),
        P(None, "head"),
        P(None, "dp", "head"),
        P(),
        P(),
        P(),
    )
    out_specs = (
        P("dp", None),
        P("dp", None),
        P(None, "dp", "head"),
        P(None, "dp"),
        P(None, "head"),
        P(None, "dp", "head"),
        P(None, "dp", "head"),
        P(None, "dp", "head"),
        P(),
        P(),
        P(),
        P(),
        P(),
    )
    return jax.shard_map(local, mesh=mesh, in_specs=in_specs, out_specs=out_specs, check_vma=False)
```

time: 630 us -> 424 us (0.67)
  the two profiles are of different devices: /device:TPU:10 before, /device:TPU:0 now
where the time goes in v1:
time: 424 us; the launch traced here: 423 us
  waiting for transfers between devices  281 us (66%)
  blocking collectives  64.9 us (15%)
  Pallas kernels  41.3 us (10%)
  between operations  14 us (3%)
  other arithmetic  11.8 us (3%)
  local copies, waits for them, and re-layouts  6.03 us (1%)
    psum x1, waiting for transfers between devices, local(): small_total = lax.psum(sums, ('dp', 'head'))  185 us
    all_gather x1, waiting for transfers between devices, local(): w = lax.all_gather(weights.astype(BF16), both, axis=0, tiled=False)  74.8 us
    pallas_call x1, Pallas kernels, block_call(): pl.pallas_call(block_kernel, out_shape=(jax.ShapeDtypeStruct((own, D), BF...  41.3 us
    psum x1, blocking collectives, local(): update_sq = lax.psum(jnp.sum(update * update, axis=(1, 2)), ('dp', 'head'))  36.9 us
    psum x1, blocking collectives, local(): lax.psum((jnp.sum(squares, axis=1), jnp.sum(new_rows, axis=1)), 'dp')  21.4 us
    all_gather x1, waiting for transfers between devices, local(): out = lax.all_gather(out, 'head', axis=0, tiled=True)  18.9 us
  transfers between devices with their start and end apart: 5, of which 3 were waited for; matrix products, arithmetic and copies ran while one was open for 2% of the time, Pallas kernels for 0%

profile of v1, /device:TPU:0, one launch (start us, length us, event | category | flops | bytes accessed | tf_op | source)
XLA Modules:
  0.0 422.7 jit_solution(5120513378912290966)
XLA Ops:
  7.2 1.7 convert_element_type.9
  9.0 74.8 %all-gather.7.cloned.1.call-done = bf16[384,64,128]{2,1,0:T(8,128)(2,1)} async-done(((bf16[12,64,128]{2,1,0:T(8,128)(2,1)}), bf16[384,64,128]{2,1,0:T(8,128)(2,1)}) %all-gather.7.cloned.1.call-update) | async-done | bytes 6291472 | tf_op jit(solution)/shard_map/all_gather | solution.py:693
  83.7 41.3 %block.1 = (bf16[294,512]{1,0:T(8,128)(2,1)}, bf16[294,512]{1,0:T(8,128)(2,1)}, bf16[4,8,12,64,128]{4,3,2,1,0:T(8,128)(2,1)}, f32[71,512]{1,0:T(8,128)}) custom-call(s32[4,6]{1,0:T(4,128)} %cls.1, s32[4,6]{1,0:T(4,128)} %img.1, bf16[1176,512]{1,0:T(8,128)(2,1)} %tokens.1, bf16[1176,512]{1,0:T(8,128)(2,1)} %cot.1, bf16[4,8,12,64,128]{4,3,2,1,0:T(8,128)(2,1)} %bitcast.5, ...), custom_call_target="tpu_custom_call" | custom-call | tf_op jit(solution)/shard_map/block/pallas_call | solution.py:662
  125.0 3.8 all-to-all-start
  128.8 0.7 all-reduce.3.cloned.1.call-update
  129.6 0.7 all-gather.9.cloned.1.call-update
  130.3 0.2 all-gather.11.cloned.1.call-start
  130.5 0.3 all-gather.11.cloned.1.call-update
  130.8 185.1 %all-reduce.3.cloned.1.call-done = f32[71,512]{1,0:T(8,128)} async-done(((f32[71,512]{1,0:T(8,128)}), f32[71,512]{1,0:T(8,128)}) %all-reduce.3.cloned.1.call-update) | async-done | bytes 145424 | tf_op jit(solution)/shard_map/psum | solution.py:701
  316.0 1.1 multiply_reduce_fusion.1
  317.1 1.8 multiply_add_fusion.2
  318.8 18.9 %all-gather.9.cloned.1.call-done = bf16[4,294,512]{2,1,0:T(8,128)(2,1)} async-done(((bf16[1,294,512]{2,1,0:T(8,128)(2,1)}), bf16[4,294,512]{2,1,0:T(8,128)(2,1)}) %all-gather.9.cloned.1.call-update) | async-done | bytes 1204240 | tf_op jit(solution)/shard_map/all_gather | solution.py:696
  337.7 2.6 reshape.46
  340.4 4.3 %convert_reduce_fusion = f32[12,64,128]{2,1,0:T(8,128)S(1)} fusion(bf16[32,12,64,128]{3,2,1,0:T(8,128)(2,1)} %all-to-all-done), kind=kLoop, calls=%fused_computation | loop fusion | flops 6193152 | bytes 6684672 | tf_op jit(solution)/shard_map/reduce_sum | solution.py:700
  344.7 0.2 fusion
  344.9 6.6 %psum.35 = f32[12,64]{1,0:T(8,128)S(1)} all-reduce(f32[12,64]{1,0:T(8,128)S(1)} %get-tuple-element.22), channel_id=1, replica_groups=mesh['dp'=8,'head'=4] {'head'}, use_global_device_ids=true, to_apply=%region_2.0 | all-reduce | flops 768 | bytes 6144 | tf_op jit(solution)/shard_map/psum | solution.py:703
  351.6 21.4 %all-reduce = (f32[12,128]{1,0:T(8,128)S(1)}, f32[12]{0:T(128)S(1)}) all-reduce(f32[12,128]{1,0:T(8,128)S(1)} %get-tuple-element.21, f32[12]{0:T(128)S(1)} %get-tuple-element.31), channel_id=1, replica_groups=mesh['dp'=8,'head'=4] {'dp'}, use_global_device_ids=true, to_apply=%region_4.0 | all-reduce | flops 1548 | bytes 12384 | tf_op jit(solution)/shard_map/psum | solution.py:705
  373.1 0.3 multiply_reduce_fusion
  373.4 2.7 reshape.48
  376.1 36.9 %psum.38 = f32[12]{0:T(128)S(1)} all-reduce(f32[12]{0:T(128)S(1)} %multiply_reduce_fusion), channel_id=1, replica_groups=mesh['dp'=8,'head'=4] {'dp','head'}, use_global_device_ids=true, to_apply=%region_8.0 | all-reduce | flops 12 | bytes 96 | tf_op jit(solution)/shard_map/psum | solution.py:709
  413.1 1.0 multiply_add_fusion
  414.1 0.8 convert_element_type.11
  414.9 0.6 pad_maximum_fusion
  415.5 0.7 copy.25
  (37 shorter events, 0.4 us)
Async XLA Ops:
  7.2 76.6 %all-gather.7.cloned.1.call-start = ((), (), s32[]{:S(2)}) async-start(), calls=%async_computation.2 | async-start | bytes 6488064 | tf_op jit(solution)/shard_map/all_gather | solution.py:693
  125.0 191.0 %copy-start.7 = (f32[71,512]{1,0:T(8,128)S(1)}, f32[71,512]{1,0:T(8,128)}, u32[]{:S(2)}) copy-start(f32[71,512]{1,0:T(8,128)} %param.20) | copy-start | bytes 436228
  125.0 215.4 %all-to-all-start = ((bf16[32,12,64,128]{3,2,1,0:T(8,128)(2,1)}), bf16[32,12,64,128]{3,2,1,0:T(8,128)(2,1)}, u32[]{:S(2)}, u32[]{:S(2)}) async-start(bf16[32,12,64,128]{3,2,1,0:T(8,128)(2,1)} %bitcast.4), calls=%async_computation | async-start | bytes 12582912 | tf_op jit(solution)/shard_map/all_to_all | solution.py:699
  128.8 188.3 %copy-start.5 = (f32[71,512]{1,0:T(8,128)S(1)}, f32[71,512]{1,0:T(8,128)}, u32[]{:S(2)}) copy-start(f32[71,512]{1,0:T(8,128)} %small.1) | copy-start | bytes 436228
  128.8 188.3 %copy-start.8 = (f32[71,512]{1,0:T(8,128)S(1)}, f32[71,512]{1,0:T(8,128)}, u32[]{:S(2)}) copy-start(f32[71,512]{1,0:T(8,128)} %param.21) | copy-start | bytes 436228
  128.8 187.2 %all-reduce.3.cloned.1.call-start = ((), (), s32[]{:S(2)}) async-start(), calls=%async_computation.1 | async-start | bytes 294912 | tf_op jit(solution)/shard_map/psum | solution.py:701
  129.5 208.2 %all-gather.9.cloned.1.call-start = ((), (), s32[]{:S(2)}) async-start(), calls=%async_computation.3 | async-start | bytes 1515520 | tf_op jit(solution)/shard_map/all_gather | solution.py:696
  130.3 243.2 %all-gather.11.cloned.1.call-start = ((), (), s32[]{:S(2)}) async-start(), calls=%async_computation.4 | async-start | bytes 1515520 | tf_op jit(solution)/shard_map/all_gather | solution.py:697
  317.0 23.3 %copy-start.4 = (f32[71,512]{1,0:T(8,128)}, f32[71,512]{1,0:T(8,128)S(1)}, u32[]{:S(2)}) copy-start(f32[71,512]{1,0:T(8,128)S(1)} %get-tuple-element.46) | copy-start | bytes 436228
  340.4 11.1 %copy-start.11 = (f32[12,64]{1,0:T(8,128)S(1)}, f32[12,64]{1,0:T(8,128)}, u32[]{:S(2)}) copy-start(f32[12,64]{1,0:T(8,128)} %param.16) | copy-start | bytes 9220
  340.4 32.7 %copy-start.12 = (f32[12,128]{1,0:T(8,128)S(1)}, f32[12,128]{1,0:T(8,128)}, u32[]{:S(2)}) copy-start(f32[12,128]{1,0:T(8,128)} %param.17) | copy-start | bytes 18436
  344.7 68.4 %copy-start = (f32[12,64,128]{2,1,0:T(8,128)}, f32[12,64,128]{2,1,0:T(8,128)S(1)}, u32[]{:S(2)}) copy-start(f32[12,64,128]{2,1,0:T(8,128)S(1)} %convert_reduce_fusion) | copy-start | bytes 1179652
  351.6 61.5 %copy-start.9 = (f32[12,64]{1,0:T(8,128)}, f32[12,64]{1,0:T(8,128)S(1)}, u32[]{:S(2)}) copy-start(f32[12,64]{1,0:T(8,128)S(1)} %get-tuple-element.40) | copy-start | bytes 9220
  373.1 40.0 %copy-start.10 = (f32[12,128]{1,0:T(8,128)}, f32[12,128]{1,0:T(8,128)S(1)}, u32[]{:S(2)}) copy-start(f32[12,128]{1,0:T(8,128)S(1)} %multiply_add_fusion.4) | copy-start | bytes 18436
  373.4 39.7 %copy-start.1 = (f32[12,64,128]{2,1,0:T(8,128)S(1)}, f32[12,64,128]{2,1,0:T(8,128)}, u32[]{:S(2)}) copy-start(f32[12,64,128]{2,1,0:T(8,128)} %param.15) | copy-start | bytes 1179652
  373.4 39.7 %copy-start.6 = (f32[12,64,128]{2,1,0:T(8,128)S(1)}, f32[12,64,128]{2,1,0:T(8,128)}, u32[]{:S(2)}) copy-start(f32[12,64,128]{2,1,0:T(8,128)} %param.18) | copy-start | bytes 1179652
  413.1 2.4 copy-start.3
  414.1 2.0 copy-start.2
Sparse Core Ops, SparseCore 0:
  11.5 72.2 all-gather.6
  135.7 180.1 all-reduce.2
  318.1 19.5 all-gather.8
  339.7 17.8 all-gather.10

commit v2 on v1

--- a/solution.py
+++ b/solution.py
@@ -130,8 +130,8 @@
     def matrix(self, k, lo, hi):
         parts = []
         for h in range(lo, hi):
-            part = self.w[h, :, k]
-            if part.shape[1] % 16:
+            part = self.w[h // 2, h % 2, :, :, k]
+            if part.shape[-2] % 16:
                 part = part.astype(F32).reshape(D, LANES).astype(BF16)
             else:
                 part = part.reshape(D, LANES)
@@ -149,9 +149,9 @@
             g = dot(lhs_t, rhs[:, lane_block(b)])
             for i in range(2):
                 piece = g[:, i * LANES : (i + 1) * LANES]
-                rows = self.g.shape[3]
-                piece = piece.reshape(D // rows, rows, LANES)
-                self.g[2 * b + i, :, k] = piece.astype(BF16)
+                parts, two, _, rows, _ = self.g.shape[2:]
+                piece = piece.reshape(parts, two, rows, LANES)
+                self.g[b, i, :, :, k] = piece.astype(BF16)
 
     def row(self, j):
         return self.small[j : j + 1, :]
@@ -251,12 +251,14 @@
 
         rows_loop(ROWS, 16, body, 0, unroll=5)
 
-    def project(self):
+    def project(self, k):
+        low = (self.q, self.k, self.v)[k]
         for b in range(2):
             cols = lane_block(b)
-            self.q[:, cols] = (self.times(self.n1[...], 0, b) + self.small[2:3, cols]).astype(BF16)
-            self.k[:, cols] = self.times(self.n1[...], 1, b).astype(BF16)
-            self.v[:, cols] = (self.times(self.n1[...], 2, b) + self.small[3:4, cols]).astype(BF16)
+            p = self.times(self.n1[...], k, b)
+            if k != 1:
+                p = p + self.small[2 + k // 2 : 3 + k // 2, cols]
+            low[:, cols] = p.astype(BF16)
 
     def image_sum(self, x):
         total = jnp.zeros((SLOTS, D), F32)
@@ -372,25 +374,30 @@
 
         rows_loop(ROWS, 16, body, 0, unroll=5)
 
-    def up(self, r):
+    def mlp(self, r):
+        up, down = 4 + 2 * r, 5 + 2 * r
         for b in range(2):
             cols = lane_block(b)
-            h = self.times(self.n2[...], 4 + r, b) + self.small[pl.ds(9 + r, 1), cols]
-            self.slope[r, :, cols] = h
-
-        def body(r0, _):
-            rows = pl.ds(r0, 16)
-            act, slope = erf_parts(self.slope[r, rows, :])
-            self.active[r, rows, :] = act.astype(BF16)
-            self.slope[r, rows, :] = slope
-            return 0
-
-        rows_loop(ROWS, 16, body, 0, unroll=5)
-
-    def down(self, r):
+            h = self.times(self.n2[...], up, b) + self.small[pl.ds(9 + r, 1), cols]
+            self.hidden[:, cols] = h
+            self.factor[:, cols] = self.times(self.go[...], down, b)
+
+        def body(r0, total):
+            rows = pl.ds(r0, 16)
+            act, slope = erf_parts(self.hidden[rows, :])
+            g = self.factor[rows, :] * slope
+            self.active[rows, :] = act.astype(BF16)
+            self.low[rows, :] = g.astype(BF16)
+            return total + fold(g)
+
+        total = rows_loop(ROWS, 16, body, jnp.zeros((SLOTS, D), F32), unroll=5)
+        self.sums[pl.ds(9 + r, 1), :] = jnp.sum(total, axis=0, keepdims=True)
+        self.put_grad(down, self.go_t[...], self.active)
+        self.put_grad(up, self.n2_t[...], self.low)
         for b in range(2):
             cols = lane_block(b)
-            self.second[:, cols] += self.times_t(self.active[r], 8 + r, b)
+            self.second[:, cols] += self.times_t(self.active[...], down, b)
+            self.back[:, cols] += self.times_t(self.low[...], up, b)
 
     def finish_out(self):
         def body(r0, _):
@@ -400,29 +407,6 @@
 
         rows_loop(ROWS, 16, body, 0, unroll=5)
         self.unplace(self.low, self.out)
-
-    def grad_hidden(self, r):
-        go = self.go[...]
-        for b in range(2):
-            cols = lane_block(b)
-            self.factor[:, cols] = self.times(go, 8 + r, b)
-
-        def body(r0, total):
-            rows = pl.ds(r0, 16)
-            g = self.factor[rows, :] * self.slope[r, rows, :]
-            self.low[rows, :] = g.astype(BF16)
-            return total + fold(g)
-
-        total = rows_loop(ROWS, 16, body, jnp.zeros((SLOTS, D), F32), unroll=5)
-        self.sums[pl.ds(9 + r, 1), :] = jnp.sum(total, axis=0, keepdims=True)
-
-    def back_mlp(self, r):
-        self.grad_hidden(r)
-        self.put_grad(8 + r, self.go_t[...], self.active[r])
-        self.put_grad(4 + r, self.n2_t[...], self.low[...])
-        for b in range(2):
-            cols = lane_block(b)
-            self.back[:, cols] += self.times_t(self.low[...], 4 + r, b)
 
     def back_two(self):
         zero = jnp.zeros((SLOTS, D), F32)
@@ -442,7 +426,7 @@
             self.sums[j : j + 1, :] = jnp.sum(s, axis=0, keepdims=True)
 
     def back_attend(self):
-        self.put_grad(3, self.low[...].T, self.mixed[...])
+        self.put_grad(3, self.low[...].T, self.mixed)
         for b in range(2):
             cols = lane_block(b)
             self.factor[:, cols] = self.times(self.low[...], 3, b)
@@ -515,7 +499,7 @@
     def back_project(self):
         n1_t = self.n1[...].T
         for k in range(3):
-            self.put_grad(k, n1_t, self.gl[k])
+            self.put_grad(k, n1_t, self.gl.at[k])
         for b in range(2):
             cols = lane_block(b)
             back = self.times_t(self.gl[0], 0, b)
@@ -569,6 +553,16 @@
 
         rows_loop(ROWS, 16, down, 0, unroll=5)
         self.unplace(self.low, self.grad_in)
+
+
+SLOT_OF = (0, 1, 2, 3, 4, 6, 8, 10, 5, 7, 9, 11)
+EARLY = 4
+
+
+def route(slot):
+    if slot < EARLY:
+        return ("xzy", "yzx")[slot % 2] + "c"
+    return ("zxy", "zyx")[slot % 2] + "c"
 
 
 def scratch_of():
@@ -605,8 +599,8 @@
         "factor": (f, F32),
         "rel": (f, F32),
         "mixed": (f, BF16),
-        "slope": ((4, ROWS, D), F32),
-        "active": ((4, ROWS, D), BF16),
+        "hidden": (f, F32),
+        "active": (f, BF16),
         "low": (f, BF16),
         "back": (f, F32),
         "f": (f, BF16),
@@ -617,62 +611,184 @@
     }
 
 
-def run_block(blk):
+class Links:
+    def __init__(self):
+        dp, head = lax.axis_index("dp"), lax.axis_index("head")
+        self.depth = lax.axis_size("dp") // 2
+        self.at = {"x": head // 2, "c": head % 2, "z": dp // 2, "y": dp % 2}
+
+    def count(self, axis):
+        return self.depth if axis == "z" else 2
+
+    def peer(self, axis, step):
+        return lax.rem(self.at[axis] + step, self.count(axis))
+
+    def device(self, axis, step):
+        at = dict(self.at)
+        at[axis] = self.peer(axis, step)
+        return (at["z"] * 2 + at["y"], at["x"] * 2 + at["c"])
+
+    def steps(self, axis, do):
+        last = self.count(axis)
+        if last <= 4:
+            for step in range(1, last):
+                do(step)
+        else:
+
+            def body(step, _):
+                do(step)
+                return 0
+
+            lax.fori_loop(1, last, body, 0)
+
+    def greet(self):
+        barrier = pltpu.get_barrier_semaphore()
+        for axis in "zyxc":
+
+            def signal(step, axis=axis):
+                pl.semaphore_signal(
+                    barrier,
+                    inc=1,
+                    device_id=self.device(axis, step),
+                    device_id_type=pl.DeviceIdType.MESH,
+                )
+
+            self.steps(axis, signal)
+        pl.semaphore_wait(barrier, self.depth + 2)
+
+    def copy(self, src, dst, send, recv, device):
+        return pltpu.make_async_remote_copy(
+            src_ref=src,
+            dst_ref=dst,
+            send_sem=send,
+            recv_sem=recv,
+            device_id=device,
+            device_id_type=pl.DeviceIdType.MESH,
+        )
+
+
+class Gather:
+    def __init__(self, links, w, send, recv):
+        self.links, self.w, self.send, self.recv = links, w, send, recv
+
+    def region(self, slot, whole, **at):
+        at = {**self.links.at, **at}
+        place = [slice(None) if axis in whole else at[axis] for axis in "xczy"]
+        return self.w.at[(*place, slot)]
+
+    def some(self, slot, axis, whole):
+        at = {}
+        if axis == "z":
+            at["z"] = pl.ds(0, self.links.depth - 1)
+        return self.region(slot, whole, **at)
+
+    def start(self, slot, phase):
+        path = route(slot)
+        axis = path[phase]
+        part = self.region(slot, path[:phase])
+
+        def go(step):
+            self.links.copy(
+                part,
+                part,
+                self.send.at[slot, phase],
+                self.recv.at[slot, phase],
+                self.links.device(axis, step),
+            ).start()
+
+        self.links.steps(axis, go)
+
+    def descriptor(self, slot, phase):
+        path = route(slot)
+        part = self.some(slot, path[phase], path[:phase])
+        sems = (self.send.at[slot, phase], self.recv.at[slot, phase])
+        return self.links.copy(part, part, *sems, self.links.device(path[phase], 1))
+
+    def arrive(self, slot, phase):
+        self.descriptor(slot, phase).wait_recv()
+
+    def sent(self, slot, phase):
+        self.descriptor(slot, phase).wait_send()
+
+    def wave(self, w):
+        for pair in range(6):
+            phase = w - pair
+            for slot in (2 * pair, 2 * pair + 1):
+                if 1 <= phase <= 4:
+                    self.arrive(slot, phase - 1)
+                if 1 <= phase <= 3:
+                    self.start(slot, phase)
+
+
+def block_kernel(
+    cls, img, tokens, cot, weights, small, out, grad_in, g, sums, w, ag_send, ag_recv, *scratch
+):
+    refs = {"cls": cls, "img": img, "tokens": tokens, "cot": cot, "w": w, "small": small}
+    refs.update({"out": out, "grad_in": grad_in, "g": g, "sums": sums})
+    refs.update(zip(scratch_of(), scratch, strict=True))
+    blk = Block(refs)
+    links = Links()
+    at = links.at
+    for k in range(12):
+        w[at["x"], at["c"], at["z"], at["y"], SLOT_OF[k]] = weights[k].astype(BF16)
+    links.greet()
+    gather = Gather(links, w, ag_send, ag_recv)
+    for slot in range(12):
+        gather.start(slot, 0)
     blk.setup()
     blk.read()
     blk.norm_one()
-    blk.project()
+    blk.go_t[...] = blk.go[...].T
+    blk.back[...] = jnp.zeros((ROWS, D), F32)
+    for i in range(1, 5):
+        gather.wave(i)
+    blk.project(0)
+    blk.project(1)
     blk.softmax()
+    gather.wave(5)
+    blk.project(2)
     blk.attend()
     blk.norm_two()
-
-    def forward(r, _):
-        blk.up(r)
-        blk.down(r)
-        return 0
-
-    lax.fori_loop(0, 4, forward, 0)
+    blk.n2_t[...] = blk.n2[...].T
+    for r in range(4):
+        gather.wave(6 + r)
+        blk.mlp(r)
     blk.finish_out()
-    blk.n2_t[...] = blk.n2[...].T
-    blk.go_t[...] = blk.go[...].T
-    blk.back[...] = jnp.zeros((ROWS, D), F32)
-
-    def backward(r, _):
-        blk.back_mlp(r)
-        return 0
-
-    lax.fori_loop(0, 4, backward, 0)
     blk.back_two()
     blk.back_attend()
     blk.back_project()
     blk.back_one()
-
-
-def block_kernel(cls, img, tokens, cot, w, small, out, grad_in, g, sums, *scratch):
-    refs = {"cls": cls, "img": img, "tokens": tokens, "cot": cot, "w": w, "small": small}
-    refs.update({"out": out, "grad_in": grad_in, "g": g, "sums": sums})
-    refs.update(zip(scratch_of(), scratch, strict=True))
-    run_block(Block(refs))
-
-
-def block_call(cls, img, tokens, cot, w, small):
+    for slot in range(12):
+        for phase in range(4):
+            gather.sent(slot, phase)
+
+
+def block_call(cls, img, tokens, cot, weights, small):
     own = cls.shape[1] * CELLS
     smem = pl.BlockSpec(memory_space=pltpu.SMEM)
     vmem = pl.BlockSpec(memory_space=pltpu.VMEM)
+    spread = (2, 2, lax.axis_size("dp") // 2, 2, *weights.shape)
     return pl.pallas_call(
         block_kernel,
         out_shape=(
             jax.ShapeDtypeStruct((own, D), BF16),
             jax.ShapeDtypeStruct((own, D), BF16),
-            jax.ShapeDtypeStruct(w.shape, BF16),
+            jax.ShapeDtypeStruct(spread, BF16),
             jax.ShapeDtypeStruct(small.shape, F32),
         ),
         in_specs=[smem, smem, vmem, vmem, vmem, vmem],
         out_specs=(vmem,) * 4,
-        scratch_shapes=[pltpu.VMEM(*v) for v in scratch_of().values()],
-        compiler_params=pltpu.CompilerParams(vmem_limit_bytes=63 << 20),
+        scratch_shapes=[
+            pltpu.VMEM(spread, BF16),
+            pltpu.SemaphoreType.DMA((12, 4)),
+            pltpu.SemaphoreType.DMA((12, 4)),
+            *[pltpu.VMEM(*v) for v in scratch_of().values()],
+        ],
+        compiler_params=pltpu.CompilerParams(
+            collective_id=0, has_side_effects=True, vmem_limit_bytes=63 << 20
+        ),
         name="block",
-    )(cls, img, tokens, cot, w, small)
+    )(cls, img, tokens, cot, weights, small)
 
 
 def local(
@@ -690,14 +806,14 @@
 ):
     heads, parts = lax.axis_size("head"), lax.axis_size("dp")
     both = ("head", "dp")
-    w = lax.all_gather(weights.astype(BF16), both, axis=0, tiled=False)
-    w = w.reshape(heads, parts, *weights.shape)
-    out, grad_in, g, sums = block_call(crop_class, crop_image, tokens, cotangent, w, small_params)
+    out, grad_in, g, sums = block_call(
+        crop_class, crop_image, tokens, cotangent, weights, small_params
+    )
     out = lax.all_gather(out, "head", axis=0, tiled=True)
     grad_in = lax.all_gather(grad_in, "head", axis=0, tiled=True)
     g = g.reshape(heads * parts, *weights.shape)
     weight_grad = lax.all_to_all(g, both, split_axis=0, concat_axis=0, tiled=True)
-    weight_grad = weight_grad.astype(F32).sum(axis=0)
+    weight_grad = weight_grad.astype(F32).sum(axis=0)[jnp.array(SLOT_OF)]
     small_total = lax.psum(sums, ("dp", "head"))
     squares = weight_grad * weight_grad + SQUARE_FLOOR
     row_total = lax.psum(jnp.sum(squares, axis=2), "head")

time: 424 us -> 386 us (0.910)
  waiting for transfers between devices: 281 us -> 199 us
  Pallas kernels: 41.3 us -> 82.2 us
    all_gather x1 -> x0, waiting for transfers between devices: 74.8 us -> none  [local(): w = lax.all_gather(weights.astype(BF16), both, axis=0, tiled=False)]
    pallas_call x1, Pallas kernels: 41.3 us -> 82.2 us  [block_call(): pl.pallas_call(block_kernel, out_shape=(jax.ShapeDtypeStruct((own, D), BF...]
    all_gather x1, waiting for transfers between devices: 18.9 us -> 0.01 us  [local(): out = lax.all_gather(out, 'head', axis=0, tiled=True)]
    psum x1, waiting for transfers between devices: 185 us -> 197 us  [local(): small_total = lax.psum(sums, ('dp', 'head'))]
  transfers between devices with their start and end apart: 5 -> 4, of which waited for: 3 -> 1; matrix products, arithmetic and copies ran while one was open for 2% -> 3% of each run, Pallas kernels for 0% -> 0%
where the time goes in v2:
time: 386 us; the launch traced here: 385 us
  waiting for transfers between devices  199 us (52%)
  Pallas kernels  82.2 us (21%)
  blocking collectives  66.8 us (17%)
  between operations  15.7 us (4%)
  other arithmetic  10.1 us (3%)
  local copies, waits for them, and re-layouts  6.62 us (2%)
  starting transfers between devices  3.9 us (1%)
    psum x1, waiting for transfers between devices, local(): small_total = lax.psum(sums, ('dp', 'head'))  197 us
    pallas_call x1, Pallas kernels, block_call(): pl.pallas_call(block_kernel, out_shape=(jax.ShapeDtypeStruct((own, D), BF...  82.2 us
    psum x1, blocking collectives, local(): update_sq = lax.psum(jnp.sum(update * update, axis=(1, 2)), ('dp', 'head'))  36.8 us
    psum x1, blocking collectives, local(): lax.psum((jnp.sum(squares, axis=1), jnp.sum(new_rows, axis=1)), 'dp')  21.9 us
    psum x1, blocking collectives, local(): row_total = lax.psum(jnp.sum(squares, axis=2), 'head')  8.03 us
  transfers between devices with their start and end apart: 4, of which 1 were waited for; matrix products, arithmetic and copies ran while one was open for 3% of the time, Pallas kernels for 0%

profile of v2, /device:TPU:0, one launch (start us, length us, event | category | flops | bytes accessed | tf_op | source)
XLA Modules:
  0.0 384.6 jit_solution(387682969432161329)
XLA Ops:
  8.0 82.2 %block.1 = (bf16[294,512]{1,0:T(8,128)(2,1)}, bf16[294,512]{1,0:T(8,128)(2,1)}, bf16[2,2,4,2,12,64,128]{6,5,4,3,2,1,0:T(8,128)(2,1)}, f32[71,512]{1,0:T(8,128)}) custom-call(s32[4,6]{1,0:T(4,128)} %cls.1, s32[4,6]{1,0:T(4,128)} %img.1, bf16[1176,512]{1,0:T(8,128)(2,1)} %tokens.1, bf16[1176,512]{1,0:T(8,128)(2,1)} %cot.1, f32[12,64,128]{2,1,0:T(8,128)} %weights.1, ...), custom_call_target="tpu_custom_call" | custom-call | tf_op jit(solution)/shard_map/block/pallas_call | solution.py:771
  90.2 3.8 all-to-all-start
  94.1 0.7 all-reduce.3.cloned.1.call-update
  94.8 0.0 all-gather.5.cloned.1.call-start
  94.8 0.5 all-gather.5.cloned.1.call-update
  95.4 0.0 all-gather.7.cloned.1.call-start
  95.4 0.5 all-gather.7.cloned.1.call-update
  96.0 197.5 %all-reduce.3.cloned.1.call-done = f32[71,512]{1,0:T(8,128)} async-done(((f32[71,512]{1,0:T(8,128)}), f32[71,512]{1,0:T(8,128)}) %all-reduce.3.cloned.1.call-update) | async-done | bytes 145424 | tf_op jit(solution)/shard_map/psum | solution.py:817
  293.5 1.1 multiply_reduce_fusion.1
  294.6 1.8 multiply_add_fusion.2
  296.3 2.6 reshape.48
  299.0 4.3 %convert_reduce_fusion = f32[12,64,128]{2,1,0:T(8,128)S(1)} fusion(bf16[32,12,64,128]{3,2,1,0:T(8,128)(2,1)} %all-to-all-done), kind=kLoop, calls=%fused_computation.1 | loop fusion | flops 6193152 | bytes 6684672 | tf_op jit(solution)/shard_map/reduce_sum | solution.py:816
  303.3 0.6 gather_fusion
  303.9 0.2 fusion
  304.1 8.0 %psum.35 = f32[12,64]{1,0:T(8,128)S(1)} all-reduce(f32[12,64]{1,0:T(8,128)S(1)} %get-tuple-element.22), channel_id=1, replica_groups=mesh['dp'=8,'head'=4] {'head'}, use_global_device_ids=true, to_apply=%region_2.0 | all-reduce | flops 768 | bytes 6144 | tf_op jit(solution)/shard_map/psum | solution.py:819
  312.1 0.1 fusion.2
  312.3 21.9 %all-reduce = (f32[12,128]{1,0:T(8,128)S(1)}, f32[12]{0:T(128)S(1)}) all-reduce(f32[12,128]{1,0:T(8,128)S(1)} %get-tuple-element.21, f32[12]{0:T(128)S(1)} %get-tuple-element.31), channel_id=1, replica_groups=mesh['dp'=8,'head'=4] {'dp'}, use_global_device_ids=true, to_apply=%region_4.0 | all-reduce | flops 1548 | bytes 12384 | tf_op jit(solution)/shard_map/psum | solution.py:821
  334.2 0.3 multiply_reduce_fusion
  334.6 2.7 reshape.50
  337.3 36.8 %psum.38 = f32[12]{0:T(128)S(1)} all-reduce(f32[12]{0:T(128)S(1)} %multiply_reduce_fusion), channel_id=1, replica_groups=mesh['dp'=8,'head'=4] {'dp','head'}, use_global_device_ids=true, to_apply=%region_8.0 | all-reduce | flops 12 | bytes 96 | tf_op jit(solution)/shard_map/psum | solution.py:825
  374.2 1.0 multiply_add_fusion
  375.2 0.8 convert_element_type.7
  375.9 0.6 pad_maximum_fusion
  376.5 0.7 copy.27
  (37 shorter events, 0.2 us)
Async XLA Ops:
  90.2 5.7 %copy-start.13 = (s32[12]{0:T(128)S(1)}, s32[12]{0:T(128)}, u32[]{:S(2)}) copy-start(s32[12]{0:T(128)} %constant.54) | copy-start | bytes 148
  90.2 203.3 %copy-start.7 = (f32[71,512]{1,0:T(8,128)S(1)}, f32[71,512]{1,0:T(8,128)}, u32[]{:S(2)}) copy-start(f32[71,512]{1,0:T(8,128)} %param.21) | copy-start | bytes 436228
  90.2 208.7 %all-to-all-start = ((bf16[32,12,64,128]{3,2,1,0:T(8,128)(2,1)}), bf16[32,12,64,128]{3,2,1,0:T(8,128)(2,1)}, u32[]{:S(2)}, u32[]{:S(2)}) async-start(bf16[32,12,64,128]{3,2,1,0:T(8,128)(2,1)} %bitcast.3), calls=%async_computation | async-start | bytes 12582912 | tf_op jit(solution)/shard_map/all_to_all | solution.py:815
  94.0 200.5 %copy-start.4 = (f32[71,512]{1,0:T(8,128)S(1)}, f32[71,512]{1,0:T(8,128)}, u32[]{:S(2)}) copy-start(f32[71,512]{1,0:T(8,128)} %small.1) | copy-start | bytes 436228
  94.0 200.5 %copy-start.8 = (f32[71,512]{1,0:T(8,128)S(1)}, f32[71,512]{1,0:T(8,128)}, u32[]{:S(2)}) copy-start(f32[71,512]{1,0:T(8,128)} %param.22) | copy-start | bytes 436228
  94.0 199.4 %all-reduce.3.cloned.1.call-start = ((), (), s32[]{:S(2)}) async-start(), calls=%async_computation.1 | async-start | bytes 294912 | tf_op jit(solution)/shard_map/psum | solution.py:817
  94.8 201.6 %all-gather.5.cloned.1.call-start = ((), (), s32[]{:S(2)}) async-start(), calls=%async_computation.2 | async-start | bytes 1515520 | tf_op jit(solution)/shard_map/all_gather | solution.py:812
  95.4 239.2 %all-gather.7.cloned.1.call-start = ((), (), s32[]{:S(2)}) async-start(), calls=%async_computation.3 | async-start | bytes 1515520 | tf_op jit(solution)/shard_map/all_gather | solution.py:813
  294.5 4.4 %copy-start.5 = (f32[71,512]{1,0:T(8,128)}, f32[71,512]{1,0:T(8,128)S(1)}, u32[]{:S(2)}) copy-start(f32[71,512]{1,0:T(8,128)S(1)} %get-tuple-element.59) | copy-start | bytes 436228
  303.3 8.8 %copy-start.11 = (f32[12,64]{1,0:T(8,128)S(1)}, f32[12,64]{1,0:T(8,128)}, u32[]{:S(2)}) copy-start(f32[12,64]{1,0:T(8,128)} %param.17) | copy-start | bytes 9220
  303.3 30.9 %copy-start.12 = (f32[12,128]{1,0:T(8,128)S(1)}, f32[12,128]{1,0:T(8,128)}, u32[]{:S(2)}) copy-start(f32[12,128]{1,0:T(8,128)} %param.18) | copy-start | bytes 18436
  303.9 70.2 %copy-start = (f32[12,64,128]{2,1,0:T(8,128)}, f32[12,64,128]{2,1,0:T(8,128)S(1)}, u32[]{:S(2)}) copy-start(f32[12,64,128]{2,1,0:T(8,128)S(1)} %gather_fusion) | copy-start | bytes 1179652
  312.2 61.9 %copy-start.9 = (f32[12,64]{1,0:T(8,128)}, f32[12,64]{1,0:T(8,128)S(1)}, u32[]{:S(2)}) copy-start(f32[12,64]{1,0:T(8,128)S(1)} %get-tuple-element.53) | copy-start | bytes 9220
  334.2 39.9 %copy-start.10 = (f32[12,128]{1,0:T(8,128)}, f32[12,128]{1,0:T(8,128)S(1)}, u32[]{:S(2)}) copy-start(f32[12,128]{1,0:T(8,128)S(1)} %multiply_add_fusion.4) | copy-start | bytes 18436
  334.5 39.6 %copy-start.2 = (f32[12,64,128]{2,1,0:T(8,128)S(1)}, f32[12,64,128]{2,1,0:T(8,128)}, u32[]{:S(2)}) copy-start(f32[12,64,128]{2,1,0:T(8,128)} %weights.1) | copy-start | bytes 1179652
  334.5 39.6 %copy-start.6 = (f32[12,64,128]{2,1,0:T(8,128)S(1)}, f32[12,64,128]{2,1,0:T(8,128)}, u32[]{:S(2)}) copy-start(f32[12,64,128]{2,1,0:T(8,128)} %param.19) | copy-start | bytes 1179652
  374.1 2.4 copy-start.3
  375.2 2.0 copy-start.1
Sparse Core Ops, SparseCore 0:
  100.4 192.9 all-reduce.2
Sparse Core Ops, SparseCore 1:
  96.8 36.3 all-gather.4
  134.6 38.6 all-gather.6

commit v3 on v2

--- a/solution.py
+++ b/solution.py
@@ -1,4 +1,7 @@
+import functools
 import math
+import types
+from typing import Any, NamedTuple
 
 import jax
 import jax.numpy as jnp
@@ -7,6 +10,7 @@
 from jax.experimental.pallas import tpu as pltpu
 from jax.sharding import PartitionSpec as P
 
+DP, HEAD = "dp", "head"
 D = 512
 HEAD_DIM = 64
 GRID = 7
@@ -157,7 +161,7 @@
         return self.small[j : j + 1, :]
 
     def setup(self):
-        head = lax.axis_index("head")
+        head = lax.axis_index(HEAD)
         slots = self.cls.shape[1]
         self.sums[...] = jnp.zeros(self.sums.shape, F32)
         sub = lax.broadcasted_iota(jnp.int32, (SLOTS, LANES), 0)
@@ -204,15 +208,18 @@
 
     def unplace(self, src_ref, out_ref):
         count = out_ref.shape[0]
+        own = self.cls.shape[1] * CELLS
+        lead = lax.rem(lax.axis_index(HEAD) * own, 16)
         r = lax.broadcasted_iota(jnp.int32, (1, ROWS), 1)
         cell, slot = r >> 3, r & 7
-        target = jnp.where((slot < self.cls.shape[1]) & (cell < CELLS), slot * CELLS + cell, -1)
+        target = lead + slot * CELLS + cell
+        target = jnp.where((slot < self.cls.shape[1]) & (cell < CELLS), target, -1)
         t = lax.broadcasted_iota(jnp.int32, (count, ROWS), 0)
         pick = jnp.where(t == target, 1.0, 0.0).astype(BF16)
         out_ref[...] = dot(pick, src_ref[...]).astype(BF16)
 
     def read(self):
-        first = lax.axis_index("head") * (self.cls.shape[1] * CELLS)
+        first = lax.axis_index(HEAD) * (self.cls.shape[1] * CELLS)
         size = 80
 
         def body(r0, _):
@@ -406,7 +413,7 @@
             return 0
 
         rows_loop(ROWS, 16, body, 0, unroll=5)
-        self.unplace(self.low, self.out)
+        self.unplace(self.low, self.out_own)
 
     def back_two(self):
         zero = jnp.zeros((SLOTS, D), F32)
@@ -425,8 +432,10 @@
         for j, s in zip((4, 5, 6, 7), sums, strict=True):
             self.sums[j : j + 1, :] = jnp.sum(s, axis=0, keepdims=True)
 
-    def back_attend(self):
+    def grad_proj(self):
         self.put_grad(3, self.low[...].T, self.mixed)
+
+    def back_heads(self):
         for b in range(2):
             cols = lane_block(b)
             self.factor[:, cols] = self.times(self.low[...], 3, b)
@@ -450,7 +459,8 @@
             self.gk[:, cols] = dot(self.by_image(self.v[:, cols]), g, NT)
             self.gv[:, cols] = dot(self.by_image(self.soft_low[:, cols]), self.stacked(g))
 
-        for c in range(D // LANES):
+    def back_window(self, tiles):
+        for c in tiles:
             lanes = slice(c * LANES, (c + 1) * LANES)
 
             def put(cell, value):
@@ -473,6 +483,7 @@
 
             tap_sums(up, self.rel_src, HALO, REACHES[c], lanes, put_tap)
 
+    def back_qkv(self):
         zero = jnp.zeros((SLOTS, D), F32)
 
         def inner(r0, total):
@@ -496,10 +507,12 @@
         for j, s in zip((2, 3), sums, strict=True):
             self.sums[j : j + 1, :] = jnp.sum(s, axis=0, keepdims=True)
 
-    def back_project(self):
+    def grad_qkv(self):
         n1_t = self.n1[...].T
         for k in range(3):
             self.put_grad(k, n1_t, self.gl.at[k])
+
+    def back_project(self):
         for b in range(2):
             cols = lane_block(b)
             back = self.times_t(self.gl[0], 0, b)
@@ -523,6 +536,8 @@
         sums = rows_loop(ROWS, 16, body, (zero,) * 3, unroll=5)
         for j, s in zip((0, 1, 8), sums, strict=True):
             self.sums[j : j + 1, :] = jnp.sum(s, axis=0, keepdims=True)
+
+    def back_first(self):
         for c in range(D // LANES):
             lanes = slice(c * LANES, (c + 1) * LANES)
 
@@ -552,7 +567,7 @@
             return 0
 
         rows_loop(ROWS, 16, down, 0, unroll=5)
-        self.unplace(self.low, self.grad_in)
+        self.unplace(self.low, self.in_own)
 
 
 SLOT_OF = (0, 1, 2, 3, 4, 6, 8, 10, 5, 7, 9, 11)
@@ -569,52 +584,52 @@
     f, h = (ROWS, D), (ROWS, LANES)
     halo3 = ((GRID + 2 * HALO) * GRID, SLOTS, D)
     halo1 = ((GRID + 2) * GRID, SLOTS, D)
-    return {
-        "live": (h, F32),
-        "im8": ((IMG_GROUP, SLOTS, LANES), F32),
-        "im16": ((IMG_GROUP, 16, LANES), BF16),
-        "window": ((WINDOW * WINDOW, D), F32),
-        "rel_taps": ((WINDOW * WINDOW, D), F32),
-        "pos_src": (halo1, F32),
-        "pos_up": (halo1, F32),
-        "rel_src": (halo3, F32),
-        "dq_src": (halo3, F32),
-        "first": (f, F32),
-        "u1": (f, F32),
-        "inv1": (h, F32),
-        "second": (f, F32),
-        "u2": (f, F32),
-        "inv2": (h, F32),
-        "n1": (f, BF16),
-        "n2": (f, BF16),
-        "n2_t": ((D, ROWS), BF16),
-        "go": (f, BF16),
-        "go_t": ((D, ROWS), BF16),
-        "q": (f, BF16),
-        "k": (f, BF16),
-        "v": (f, BF16),
-        "soft": (f, F32),
-        "soft_low": (f, BF16),
-        "ctx": ((2, WIDE, IMG_GROUP * WIDE), BF16),
-        "factor": (f, F32),
-        "rel": (f, F32),
-        "mixed": (f, BF16),
-        "hidden": (f, F32),
-        "active": (f, BF16),
-        "low": (f, BF16),
-        "back": (f, F32),
-        "f": (f, BF16),
-        "gq": (f, F32),
-        "gk": (f, F32),
-        "gv": (f, F32),
-        "gl": ((3, ROWS, D), BF16),
-    }
+    return dict(
+        live=(h, F32),
+        im8=((IMG_GROUP, SLOTS, LANES), F32),
+        im16=((IMG_GROUP, 16, LANES), BF16),
+        window=((WINDOW * WINDOW, D), F32),
+        rel_taps=((WINDOW * WINDOW, D), F32),
+        pos_src=(halo1, F32),
+        pos_up=(halo1, F32),
+        rel_src=(halo3, F32),
+        dq_src=(halo3, F32),
+        first=(f, F32),
+        u1=(f, F32),
+        inv1=(h, F32),
+        second=(f, F32),
+        u2=(f, F32),
+        inv2=(h, F32),
+        n1=(f, BF16),
+        n2=(f, BF16),
+        n2_t=((D, ROWS), BF16),
+        go=(f, BF16),
+        go_t=((D, ROWS), BF16),
+        q=(f, BF16),
+        k=(f, BF16),
+        v=(f, BF16),
+        soft=(f, F32),
+        soft_low=(f, BF16),
+        ctx=((2, WIDE, IMG_GROUP * WIDE), BF16),
+        factor=(f, F32),
+        rel=(f, F32),
+        mixed=(f, BF16),
+        hidden=(f, F32),
+        active=(f, BF16),
+        low=(f, BF16),
+        back=(f, F32),
+        f=(f, BF16),
+        gq=(f, F32),
+        gk=(f, F32),
+        gv=(f, F32),
+        gl=((3, ROWS, D), BF16),
+    )
 
 
 class Links:
     def __init__(self):
-        dp, head = lax.axis_index("dp"), lax.axis_index("head")
-        self.depth = lax.axis_size("dp") // 2
+        dp, head = lax.axis_index(DP), lax.axis_index(HEAD)
+        self.depth = lax.axis_size(DP) // 2
         self.at = {"x": head // 2, "c": head % 2, "z": dp // 2, "y": dp % 2}
 
     def count(self, axis):
@@ -641,20 +656,38 @@
 
             lax.fori_loop(1, last, body, 0)
 
+    def others(self, name, do):
+        size = lax.axis_size(name)
+        index = {DP: lax.axis_index(DP), HEAD: lax.axis_index(HEAD)}
+        own = index[name]
+
+        def one(step):
+            peer = lax.rem(own + step, size)
+            at = {**index, name: peer}
+            do(step, (at[DP], at[HEAD]))
+
+        if size <= 8:
+            for step in range(1, size):
+                one(step)
+        else:
+
+            def body(step, _):
+                one(step)
+                return 0
+
+            lax.fori_loop(1, size, body, 0)
+
     def greet(self):
         barrier = pltpu.get_barrier_semaphore()
-        for axis in "zyxc":
-
-            def signal(step, axis=axis):
-                pl.semaphore_signal(
-                    barrier,
-                    inc=1,
-                    device_id=self.device(axis, step),
-                    device_id_type=pl.DeviceIdType.MESH,
-                )
-
-            self.steps(axis, signal)
-        pl.semaphore_wait(barrier, self.depth + 2)
+
+        def signal(step, device):
+            pl.semaphore_signal(
+                barrier, inc=1, device_id=device, device_id_type=pl.DeviceIdType.MESH
+            )
+
+        self.others(HEAD, signal)
+        self.others(DP, signal)
+        pl.semaphore_wait(barrier, lax.axis_size(HEAD) + lax.axis_size(DP) - 2)
 
     def copy(self, src, dst, send, recv, device):
         return pltpu.make_async_remote_copy(
@@ -720,22 +753,420 @@
                     self.start(slot, phase)
 
 
-def block_kernel(
-    cls, img, tokens, cot, weights, small, out, grad_in, g, sums, w, ag_send, ag_recv, *scratch
-):
-    refs = {"cls": cls, "img": img, "tokens": tokens, "cot": cot, "w": w, "small": small}
-    refs.update({"out": out, "grad_in": grad_in, "g": g, "sums": sums})
-    refs.update(zip(scratch_of(), scratch, strict=True))
-    blk = Block(refs)
+class Scatter:
+    def __init__(self, links, refs, send, recv):
+        self.links, self.g, self.refs, self.total = links, refs.g, refs, refs.wg
+        self.send, self.recv = send, recv
+
+    def path(self, slot):
+        return route(slot)[::-1]
+
+    def region(self, slot, whole, **at):
+        at = {**self.links.at, **at}
+        place = [slice(None) if axis in whole else at[axis] for axis in "xczy"]
+        return self.g.at[(*place, slot)]
+
+    def box(self, slot, phase):
+        r = self.refs
+        if phase == 0:
+            return r.box_c.at[slot]
+        if phase == 1:
+            return (r.box_y, r.box_x)[slot % 2].at[slot // 2]
+        if slot < EARLY:
+            return (r.box_early2, r.box_early3)[phase - 2].at[slot]
+        return (r.box_late2, r.box_late3)[phase - 2].at[slot - EARLY]
+
+    def start(self, slot, phase):
+        path = self.path(slot)
+        axis, rest = path[phase], path[phase + 1 :]
+
+        def go(step):
+            box = self.box(slot, phase)
+            if axis == "z":
+                box = box.at[step - 1]
+            self.links.copy(
+                self.region(slot, rest, **{axis: self.links.peer(axis, step)}),
+                box,
+                self.send.at[slot, phase],
+                self.recv.at[slot, phase],
+                self.links.device(axis, step),
+            ).start()
+
+        self.links.steps(axis, go)
+
+    def descriptor(self, slot, phase):
+        box = self.box(slot, phase)
+        sems = (self.send.at[slot, phase], self.recv.at[slot, phase])
+        return self.links.copy(box, box, *sems, self.links.device(self.path(slot)[phase], 1))
+
+    def sent(self, slot, phase):
+        self.descriptor(slot, phase).wait_send()
+
+    def tick(self, slot, phase):
+        path = self.path(slot)
+        self.descriptor(slot, phase - 1).wait_recv()
+        axis, rest = path[phase - 1], path[phase:]
+        own = self.region(slot, rest)
+        box = self.box(slot, phase - 1)
+        if phase == 4:
+            value = own[...].astype(F32)
+            parts = [box.at[j] for j in range(box.shape[0])] if axis == "z" else [box]
+            for part in parts:
+                value = value + part[...].astype(F32)
+            self.total[SLOT_OF.index(slot)] = value
+            return
+        if axis == "z":
+            value = own[...].astype(F32)
+            for j in range(box.shape[0]):
+                value = value + box[j].astype(F32)
+            own[...] = value.astype(BF16)
+        else:
+            own[...] = own[...] + box[...]
+        self.start(slot, phase)
+
+
+class Small:
+    def __init__(self, links, parts, in_c, in_x, in_y, in_z, full, send, recv):
+        self.links, self.parts, self.full = links, parts, full
+        self.in_c, self.in_x, self.in_y, self.in_z = in_c, in_x, in_y, in_z
+        self.send, self.recv = send, recv
+
+    def go(self, stage, src, dst, axis):
+        sems = (self.send.at[stage], self.recv.at[stage])
+        self.links.steps(
+            axis, lambda step: self.links.copy(src, dst, *sems, self.links.device(axis, step)).start()
+        )
+
+    def wait(self, stage, ref, axis):
+        sems = (self.send.at[stage], self.recv.at[stage])
+        return self.links.copy(ref, ref, *sems, self.links.device(axis, 1))
+
+    def tick(self, stage):
+        at = self.links.at
+        x, c, z = at["x"], at["c"], at["z"]
+        mine = self.parts.at[c, x]
+        if stage == 0:
+            self.go(0, self.parts.at[1 - c], self.in_c, "c")
+        if stage == 1:
+            self.wait(0, self.in_c, "c").wait_recv()
+            self.parts[c] = self.parts[c] + self.in_c[...]
+            self.go(1, self.parts.at[c, 1 - x], self.in_x, "x")
+        if stage == 2:
+            self.wait(1, self.in_x, "x").wait_recv()
+            mine[...] = mine[...] + self.in_x[...]
+            self.go(2, mine, self.in_y, "y")
+        if stage == 3:
+            self.wait(2, self.in_y, "y").wait_recv()
+            self.in_z[z] = mine[...] + self.in_y[...]
+            self.go(3, self.in_z.at[z], self.in_z.at[z], "z")
+        if stage == 4:
+            self.wait(3, self.in_z.at[pl.ds(0, self.links.depth - 1)], "z").wait_recv()
+            self.full[c, x] = jnp.sum(self.in_z[...], axis=0)
+            self.go(4, self.full.at[c, x], self.full.at[c, x], "x")
+        if stage == 5:
+            self.wait(4, self.full.at[c, x], "x").wait_recv()
+            self.go(5, self.full.at[c], self.full.at[c], "c")
+        if stage == 6:
+            self.wait(5, self.full.at[c], "c").wait_recv()
+
+    def sent(self):
+        at = self.links.at
+        refs = (self.in_c, self.in_x, self.in_y, None, self.full.at[at["c"], at["x"]])
+        for stage, axis in enumerate("cxyzxc"):
+            if axis == "z":
+                ref = self.in_z.at[pl.ds(0, self.links.depth - 1)]
+            else:
+                ref = self.full.at[at["c"]] if stage == 5 else refs[stage]
+            self.wait(stage, ref, axis).wait_send()
+
+
+class Rows:
+    def __init__(self, links, blocks, send, recv):
+        self.links, self.blocks, self.send, self.recv = links, blocks, send, recv
+
+    def block(self, x, c):
+        return self.blocks.at[2 * x + c]
+
+    def hop(self, i):
+        x, c = self.links.at["x"], self.links.at["c"]
+        ref, axis = (((x, c), "x"), ((x, c), "c"), ((1 - x, c), "c"))[i]
+        block = self.block(*ref)
+        return self.links.copy(
+            block, block, self.send.at[i], self.recv.at[i], self.links.device(axis, 1)
+        )
+
+    def spread(self):
+        self.hop(0).start()
+        self.hop(1).start()
+
+    def forward(self):
+        self.hop(0).wait_recv()
+        self.hop(2).start()
+
+    def arrive(self):
+        self.hop(1).wait_recv()
+        self.hop(2).wait_recv()
+
+    def sent(self):
+        for i in range(3):
+            self.hop(i).wait_send()
+
+    def join(self, own, out):
+        heads, end = self.blocks.shape[0], out.shape[0]
+        for h in range(heads):
+            lo, hi = h * own, (h + 1) * own
+            base = lo // 16 * 16
+            first = base + 16 if lo % 16 else base
+            last = hi // 16 * 16 if h + 1 < heads else end
+            out[first:last, :] = self.blocks[h, first - base : last - base, :]
+            if lo % 16:
+                before = (lo - own) // 16 * 16
+                tail = self.blocks[h - 1, base - before : base - before + 16, :]
+                out[base : base + 16, :] = tail + self.blocks[h, 0:16, :]
+
+
+class Exchange:
+    def __init__(self, links, name, buffer, send, recv):
+        self.links, self.name, self.buffer, self.send, self.recv = links, name, buffer, send, recv
+
+    def start(self, value):
+        own = lax.axis_index(self.name)
+        self.buffer[own] = value
+        mine = self.buffer.at[own]
+        self.links.others(
+            self.name,
+            lambda step, device: self.links.copy(mine, mine, self.send, self.recv, device).start(),
+        )
+
+    def descriptor(self):
+        ref = self.buffer.at[pl.ds(0, self.buffer.shape[0] - 1)]
+        index = {DP: lax.axis_index(DP), HEAD: lax.axis_index(HEAD)}
+        return self.links.copy(ref, ref, self.send, self.recv, (index[DP], index[HEAD]))
+
+    def total(self):
+        self.descriptor().wait_recv()
+        return jnp.sum(self.buffer[...], axis=0)
+
+    def sent(self):
+        self.descriptor().wait_send()
+
+
+def exact(a, b, dims):
+    return lax.dot_general(
+        a, b, dims, precision=lax.Precision.HIGHEST, preferred_element_type=F32
+    )
+
+
+class Adafactor:
+    def __init__(self, refs):
+        self.__dict__.update(refs)
+
+    def eye(self, count):
+        r = lax.broadcasted_iota(jnp.int32, (count, LANES), 0)
+        c = lax.broadcasted_iota(jnp.int32, (count, LANES), 1)
+        return jnp.where(r == c, 1.0, 0.0)
+
+    def lane(self, shape, k, value, rest):
+        lanes = lax.broadcasted_iota(jnp.int32, shape, 1)
+        return jnp.where(lanes == k, value, rest)
+
+    def squares(self):
+        count, rows, _ = self.wg.shape
+        by_row = jnp.zeros((rows, LANES), F32)
+        by_col = []
+        for k in range(count):
+            g = self.wg[k]
+            s = g * g + SQUARE_FLOOR
+            by_row = self.lane(by_row.shape, k, jnp.sum(s, axis=1, keepdims=True), by_row)
+            by_col.append(jnp.sum(s, axis=0, keepdims=True))
+        self.col_part[0:count, :] = jnp.concatenate(by_col, axis=0)
+        self.row_share.start(by_row)
+
+    def rows(self):
+        count = self.wg.shape[0]
+        state = exact(self.row_state[...], self.eye(count), TN)
+        total = self.row_share.total()
+        new = SECOND_DECAY * state + (1.0 - SECOND_DECAY) * (total * (1.0 / D))
+        self.row_new[...] = new
+        self.new_rows[...] = exact(self.eye(count), new, NT)
+        self.col_part[count : count + 1, :] = jnp.sum(new, axis=0, keepdims=True)
+        self.col_share.start(self.col_part[...])
+
+    def update(self):
+        count = self.wg.shape[0]
+        total = self.col_share.total()
+        cols = SECOND_DECAY * self.col_state[...] + (1.0 - SECOND_DECAY) * (
+            total[0:count] * (1.0 / D)
+        )
+        self.new_cols[...] = cols
+        mean = total[count : count + 1] * (1.0 / D)
+        rows = self.row_new[...]
+        sums = jnp.zeros((1, LANES), F32)
+        for k in range(count):
+            r, m = rows[:, k : k + 1], mean[:, k : k + 1]
+            u = self.wg[k] * lax.rsqrt(r * cols[k : k + 1, :] / m)
+            self.upd[k] = u
+            s = jnp.sum(jnp.sum(u * u, axis=0, keepdims=True), axis=1, keepdims=True)
+            sums = self.lane(sums.shape, k, s, sums)
+        self.sq_dp.start(jnp.broadcast_to(sums, (SLOTS, LANES)))
+
+    def pass_on(self):
+        self.sq_head.start(self.sq_dp.total())
+
+    def apply(self):
+        count = self.wg.shape[0]
+        total = self.sq_head.total()[0:1]
+        rms = jnp.sqrt(total * (1.0 / (D * D)))
+        rate = STEP_RATE / jnp.maximum(1.0, rms)
+        for k in range(count):
+            new = self.weights[k] - rate[:, k : k + 1] * self.upd[k]
+            self.new_weights[k] = new
+            self.copy[k] = new.astype(BF16)
+            self.new_ema[k] = AVERAGE_KEEP * self.ema[k] + (1.0 - AVERAGE_KEEP) * new
+        lanes = lax.broadcasted_iota(jnp.int32, (1, LANES), 1)
+        clip = jnp.where(lanes < count, rms, self.small_clip[...])
+        self.clip[...] = clip[:, 0 : self.clip.shape[1]]
+
+    def small_step(self, full):
+        count = self.small.shape[0]
+        g = jnp.concatenate([full[b // 2, b % 2, 0:count, :] for b in range(D // LANES)], axis=1)
+        self.small_grads[...] = g
+        state = SECOND_DECAY * self.small_state[...] + (1.0 - SECOND_DECAY) * (
+            g * g + SQUARE_FLOOR
+        )
+        self.new_small_state[...] = state
+        u = g * lax.rsqrt(state)
+        rms = jnp.sqrt(jnp.sum(u * u, axis=1, keepdims=True) * (1.0 / D))
+        new = self.small[...] - SMALL_RATE * u / jnp.maximum(1.0, rms)
+        self.new_small[...] = new
+        self.new_small_ema[...] = AVERAGE_KEEP * self.small_ema[...] + (1.0 - AVERAGE_KEEP) * new
+        r = lax.broadcasted_iota(jnp.int32, (count, LANES), 0)
+        c = lax.broadcasted_iota(jnp.int32, (count, LANES), 1)
+        first = self.wg.shape[0]
+        picked = jnp.where(c == r + first, rms, 0.0)
+        self.small_clip[...] = jnp.sum(picked, axis=0, keepdims=True)
+
+
+class Inputs(NamedTuple):
+    cls: Any
+    img: Any
+    tokens: Any
+    cot: Any
+    weights: Any
+    row_state: Any
+    col_state: Any
+    ema: Any
+    small: Any
+    small_state: Any
+    small_ema: Any
+
+
+class Outputs(NamedTuple):
+    out: Any
+    grad_in: Any
+    wg: Any
+    new_rows: Any
+    new_cols: Any
+    new_weights: Any
+    copy: Any
+    new_ema: Any
+    small_grads: Any
+    new_small_state: Any
+    new_small: Any
+    new_small_ema: Any
+    clip: Any
+
+
+HEAD_ROWS = 320
+
+
+def shared_of(weights, parts, heads):
+    depth, (_, rows, _) = parts // 2, weights.shape
+    block = (rows, LANES)
+    dma = pltpu.SemaphoreType.DMA
+
+    def b(*lead):
+        return pltpu.VMEM((*lead, *block), BF16)
+
+    def f(*shape):
+        return pltpu.VMEM(shape, F32)
+
+    return dict(
+        w=b(2, 2, depth, 2, 12),
+        g=b(2, 2, depth, 2, 12),
+        box_c=b(12, 2, depth, 2),
+        box_y=b(6, 2, depth),
+        box_x=b(6, depth, 2),
+        box_early2=b(EARLY, depth - 1, 2),
+        box_early3=b(EARLY),
+        box_late2=b(12 - EARLY, depth),
+        box_late3=b(12 - EARLY, depth - 1),
+        out_rows=pltpu.VMEM((heads, HEAD_ROWS, D), BF16),
+        in_rows=pltpu.VMEM((heads, HEAD_ROWS, D), BF16),
+        sums=f(72, D),
+        parts=f(2, 2, 72, LANES),
+        in_c=f(2, 72, LANES),
+        in_x=f(72, LANES),
+        in_y=f(72, LANES),
+        in_z=f(depth, 72, LANES),
+        full=f(2, 2, 72, LANES),
+        row_box=f(heads, *block),
+        col_box=f(parts, 16, LANES),
+        sq_dp_box=f(parts, SLOTS, LANES),
+        sq_head_box=f(heads, SLOTS, LANES),
+        row_new=f(*block),
+        col_part=f(16, LANES),
+        upd=f(12, *block),
+        small_clip=f(1, LANES),
+        ag_send=dma((12, 4)),
+        ag_recv=dma((12, 4)),
+        rs_send=dma((12, 4)),
+        rs_recv=dma((12, 4)),
+        small_send=dma((6,)),
+        small_recv=dma((6,)),
+        out_send=dma((3,)),
+        out_recv=dma((3,)),
+        in_send=dma((3,)),
+        in_recv=dma((3,)),
+        opt_send=dma((4,)),
+        opt_recv=dma((4,)),
+    )
+
+
+def block_kernel(names, *refs):
+    r = types.SimpleNamespace(**dict(zip(names, refs, strict=True)))
+    at_head = lax.axis_index(HEAD)
+    r.out_own = r.out_rows.at[at_head]
+    r.in_own = r.in_rows.at[at_head]
+    own = r.cls.shape[1] * CELLS
+    blk = Block(vars(r))
     links = Links()
     at = links.at
+    gather = Gather(links, r.w, r.ag_send, r.ag_recv)
+    scatter = Scatter(links, r, r.rs_send, r.rs_recv)
+    small = Small(
+        links,
+        *(r.parts, r.in_c, r.in_x, r.in_y, r.in_z, r.full),
+        r.small_send,
+        r.small_recv,
+    )
+    out_rows = Rows(links, r.out_rows, r.out_send, r.out_recv)
+    in_rows = Rows(links, r.in_rows, r.in_send, r.in_recv)
+    boxes = dict(row_share=r.row_box, col_share=r.col_box, sq_dp=r.sq_dp_box, sq_head=r.sq_head_box)
+    shares = {}
+    for i, (name, box) in enumerate(boxes.items()):
+        axis = HEAD if i in (0, 3) else DP
+        shares[name] = Exchange(links, axis, box, r.opt_send.at[i], r.opt_recv.at[i])
+    opt = types.SimpleNamespace(**vars(r), **shares)
+    opt = Adafactor(vars(opt))
+
     for k in range(12):
-        w[at["x"], at["c"], at["z"], at["y"], SLOT_OF[k]] = weights[k].astype(BF16)
+        r.w[at["x"], at["c"], at["z"], at["y"], SLOT_OF[k]] = r.weights[k].astype(BF16)
     links.greet()
-    gather = Gather(links, w, ag_send, ag_recv)
     for slot in range(12):
         gather.start(slot, 0)
     blk.setup()
+    r.col_part[...] = jnp.zeros((16, LANES), F32)
     blk.read()
     blk.norm_one()
     blk.go_t[...] = blk.go[...].T
@@ -750,45 +1181,84 @@
     blk.attend()
     blk.norm_two()
     blk.n2_t[...] = blk.n2[...].T
-    for r in range(4):
-        gather.wave(6 + r)
-        blk.mlp(r)
+    for i in range(4):
+        gather.wave(6 + i)
+        blk.mlp(i)
+        scatter.start(4 + 2 * i, 0)
+        scatter.start(5 + 2 * i, 0)
+    for i in range(3):
+        scatter.tick(4 + 2 * i, 1)
+        scatter.tick(5 + 2 * i, 1)
     blk.finish_out()
+    scatter.tick(10, 1)
+    scatter.tick(11, 1)
     blk.back_two()
-    blk.back_attend()
+    blk.grad_proj()
+    scatter.start(3, 0)
+    for i in (4, 5, 6, 7):
+        scatter.tick(i, 2)
+    blk.back_heads()
+    for i in (8, 9, 10, 11):
+        scatter.tick(i, 2)
+    scatter.tick(3, 1)
+    out_rows.spread()
+    blk.back_window((0, 1, 2))
+    for i in (4, 5, 6, 7):
+        scatter.tick(i, 3)
+    blk.back_window((3,))
+    for i in (8, 9, 10, 11):
+        scatter.tick(i, 3)
+    scatter.tick(3, 2)
+    blk.back_qkv()
+    blk.grad_qkv()
+    for i in (0, 1, 2):
+        scatter.start(i, 0)
     blk.back_project()
+    for i in (0, 1, 2):
+        scatter.tick(i, 1)
     blk.back_one()
+    for i in (0, 1, 2):
+        scatter.tick(i, 2)
+    blk.back_first()
+    in_rows.spread()
+    for b in range(D // LANES):
+        r.parts[b // 2, b % 2] = r.sums[:, b * LANES : (b + 1) * LANES]
+    small.tick(0)
+    for i in (0, 1, 2):
+        scatter.tick(i, 3)
+    scatter.tick(3, 3)
+    out_rows.forward()
+    for i in range(4, 12):
+        scatter.tick(i, 4)
+    small.tick(1)
+    scatter.tick(3, 4)
+    for i in (0, 1, 2):
+        scatter.tick(i, 4)
+    opt.squares()
+    small.tick(2)
+    out_rows.arrive()
+    out_rows.join(own, r.out)
+    opt.rows()
+    small.tick(3)
+    in_rows.forward()
+    opt.update()
+    small.tick(4)
+    opt.pass_on()
+    small.tick(5)
+    in_rows.arrive()
+    in_rows.join(own, r.grad_in)
+    small.tick(6)
+    opt.small_step(r.full)
+    opt.apply()
     for slot in range(12):
         for phase in range(4):
             gather.sent(slot, phase)
-
-
-def block_call(cls, img, tokens, cot, weights, small):
-    own = cls.shape[1] * CELLS
-    smem = pl.BlockSpec(memory_space=pltpu.SMEM)
-    vmem = pl.BlockSpec(memory_space=pltpu.VMEM)
-    spread = (2, 2, lax.axis_size("dp") // 2, 2, *weights.shape)
-    return pl.pallas_call(
-        block_kernel,
-        out_shape=(
-            jax.ShapeDtypeStruct((own, D), BF16),
-            jax.ShapeDtypeStruct((own, D), BF16),
-            jax.ShapeDtypeStruct(spread, BF16),
-            jax.ShapeDtypeStruct(small.shape, F32),
-        ),
-        in_specs=[smem, smem, vmem, vmem, vmem, vmem],
-        out_specs=(vmem,) * 4,
-        scratch_shapes=[
-            pltpu.VMEM(spread, BF16),
-            pltpu.SemaphoreType.DMA((12, 4)),
-            pltpu.SemaphoreType.DMA((12, 4)),
-            *[pltpu.VMEM(*v) for v in scratch_of().values()],
-        ],
-        compiler_params=pltpu.CompilerParams(
-            collective_id=0, has_side_effects=True, vmem_limit_bytes=63 << 20
-        ),
-        name="block",
-    )(cls, img, tokens, cot, weights, small)
+            scatter.sent(slot, phase)
+    small.sent()
+    out_rows.sent()
+    in_rows.sent()
+    for share in shares.values():
+        share.sent()
 
 
 def local(
@@ -804,75 +1274,81 @@
     small_state,
     small_ema,
 ):
-    heads, parts = lax.axis_size("head"), lax.axis_size("dp")
-    both = ("head", "dp")
-    out, grad_in, g, sums = block_call(
-        crop_class, crop_image, tokens, cotangent, weights, small_params
+    parts, heads = lax.axis_size(DP), lax.axis_size(HEAD)
+    smem = pl.BlockSpec(memory_space=pltpu.SMEM)
+    vmem = pl.BlockSpec(memory_space=pltpu.VMEM)
+    shared = shared_of(weights, parts, heads)
+    own = scratch_of()
+
+    def like(x, dtype=None):
+        return jax.ShapeDtypeStruct(x.shape, dtype or x.dtype)
+
+    clips = weights.shape[0] + small_params.shape[0]
+    outs = (
+        like(tokens),
+        like(tokens),
+        like(weights),
+        like(row_state),
+        like(col_state),
+        like(weights),
+        like(weights, BF16),
+        like(weights),
+        like(small_params),
+        like(small_params),
+        like(small_params),
+        like(small_params),
+        jax.ShapeDtypeStruct((1, clips), F32),
     )
-    out = lax.all_gather(out, "head", axis=0, tiled=True)
-    grad_in = lax.all_gather(grad_in, "head", axis=0, tiled=True)
-    g = g.reshape(heads * parts, *weights.shape)
-    weight_grad = lax.all_to_all(g, both, split_axis=0, concat_axis=0, tiled=True)
-    weight_grad = weight_grad.astype(F32).sum(axis=0)[jnp.array(SLOT_OF)]
-    small_total = lax.psum(sums, ("dp", "head"))
-    squares = weight_grad * weight_grad + SQUARE_FLOOR
-    row_total = lax.psum(jnp.sum(squares, axis=2), "head")
-    new_rows = SECOND_DECAY * row_state + (1.0 - SECOND_DECAY) * (row_total / D)
-    col_total, row_mass = lax.psum((jnp.sum(squares, axis=1), jnp.sum(new_rows, axis=1)), "dp")
-    new_cols = SECOND_DECAY * col_state + (1.0 - SECOND_DECAY) * (col_total / D)
-    estimate = new_rows[:, :, None] * new_cols[:, None, :] / (row_mass / D)[:, None, None]
-    update = weight_grad * lax.rsqrt(estimate)
-    update_sq = lax.psum(jnp.sum(update * update, axis=(1, 2)), ("dp", "head"))
-    update_rms = jnp.sqrt(update_sq / (D * D))
-    new_weights = weights - STEP_RATE * update / jnp.maximum(1.0, update_rms)[:, None, None]
-    new_ema = AVERAGE_KEEP * weights_ema + (1.0 - AVERAGE_KEEP) * new_weights
-    new_small_state = SECOND_DECAY * small_state + (1.0 - SECOND_DECAY) * (
-        small_total * small_total + SQUARE_FLOOR
+    names = (*Inputs._fields, *Outputs._fields, *shared, *own)
+    res = pl.pallas_call(
+        functools.partial(block_kernel, names),
+        out_shape=outs,
+        in_specs=[smem, smem] + [vmem] * 9,
+        out_specs=(vmem,) * len(outs),
+        scratch_shapes=[*shared.values(), *[pltpu.VMEM(*v) for v in own.values()]],
+        compiler_params=pltpu.CompilerParams(
+            collective_id=0, has_side_effects=True, vmem_limit_bytes=63 << 20
+        ),
+        name="block",
+    )(
+        crop_class,
+        crop_image,
+        tokens,
+        cotangent,
+        weights,
+        row_state,
+        col_state,
+        weights_ema,
+        small_params,
+        small_state,
+        small_ema,
     )
-    small_update = small_total * lax.rsqrt(new_small_state)
-    small_rms = jnp.sqrt(jnp.mean(small_update * small_update, axis=1))
-    new_small = small_params - SMALL_RATE * small_update / jnp.maximum(1.0, small_rms)[:, None]
-    new_small_ema = AVERAGE_KEEP * small_ema + (1.0 - AVERAGE_KEEP) * new_small
-    return (
-        out,
-        grad_in,
-        weight_grad,
-        new_rows,
-        new_cols,
-        new_weights,
-        new_weights.astype(BF16),
-        new_ema,
-        small_total,
-        new_small_state,
-        new_small,
-        new_small_ema,
-        jnp.concatenate([update_rms, small_rms]),
-    )
+    return (*res[:-1], res[-1].reshape(clips))
 
 
 def solution(mesh):
     in_specs = (
-        P("dp", None),
-        P("dp", None),
-        P("dp", None),
-        P("dp", None),
-        P(None, "dp", "head"),
-        P(None, "dp"),
-        P(None, "head"),
-        P(None, "dp", "head"),
+        P(DP, None),
+        P(DP, None),
+        P(DP, None),
+        P(DP, None),
+        P(None, DP, HEAD),
+        P(None, DP),
+        P(None, HEAD),
+        P(None, DP, HEAD),
         P(),
         P(),
         P(),
     )
     out_specs = (
-        P("dp", None),
-        P("dp", None),
-        P(None, "dp", "head"),
-        P(None, "dp"),
-        P(None, "head"),
-        P(None, "dp", "head"),
-        P(None, "dp", "head"),
-        P(None, "dp", "head"),
+        P(DP, None),
+        P(DP, None),
+        P(None, DP, HEAD),
+        P(None, DP),
+        P(None, HEAD),
+        P(None, DP, HEAD),
+        P(None, DP, HEAD),
+        P(None, DP, HEAD),
         P(),
         P(),
         P(),

time: 386 us -> 143 us (0.37)
  waiting for transfers between devices: 199 us -> 0 us
  blocking collectives: 66.8 us -> 0 us
  Pallas kernels: 82.2 us -> 131 us
  between operations: 15.7 us -> 0.69 us
  other arithmetic: 10.1 us -> 0 us
  local copies, waits for them, and re-layouts: 6.62 us -> 10.9 us
  starting transfers between devices: 3.9 us -> 0 us
    psum x1 -> x0, waiting for transfers between devices: 197 us -> none  [local(): small_total = lax.psum(sums, ('dp', 'head'))]
    psum x3 -> x0, blocking collectives: 66.8 us -> none  [the longest x1 36.8 us: local(): update_sq = lax.psum(jnp.sum(update * update, axis=(1, 2)), ('dp', 'head'))]
    pallas_call x1, Pallas kernels: 82.2 us -> 131 us  [local(): pl.pallas_call(functools.partial(block_kernel, names), out_shape=outs, in...]
    reduce_sum x5 -> x0, other arithmetic: 5.98 us -> none  [the longest x1 4.32 us: local(): weight_grad = weight_grad.astype(F32).sum(axis=0)[jnp.array(SLOT_OF)]]
    unnamed x31 -> x37, local copies, waits for them, and re-layouts: 6.05 us -> 10.9 us
  transfers between devices with their start and end apart: 4 -> 0, of which waited for: 1 -> 0; matrix products, arithmetic and copies ran while one was open for 3% -> 0% of each run, Pallas kernels for 0% -> 0%
where the time goes in v3:
time: 143 us
  Pallas kernels  131 us (92%)
  local copies, waits for them, and re-layouts  10.9 us (8%)
    pallas_call x1, Pallas kernels, local(): pl.pallas_call(functools.partial(block_kernel, names), out_shape=outs, in...  131 us
    unnamed x37, local copies, waits for them, and re-layouts  10.9 us

profile of v3, /device:TPU:0, one launch (start us, length us, event | category | flops | bytes accessed | tf_op | source)
XLA Modules:
  0.0 142.8 jit_solution(13666622232492122118)
XLA Ops:
  0.6 131.2 %block.1 = (bf16[1176,512]{1,0:T(8,128)(2,1)}, bf16[1176,512]{1,0:T(8,128)(2,1)}, f32[12,64,128]{2,1,0:T(8,128)}, f32[12,64]{1,0:T(8,128)}, f32[12,128]{1,0:T(8,...) custom-call(s32[4,6]{1,0:T(4,128)} %refs_0_.1, ...), custom_call_target="tpu_custom_call" | custom-call | tf_op jit(solution)/shard_map/block/pallas_call | solution.py:1303
  131.8 0.0 copy-start
  131.8 2.5 %copy.37 = bf16[1176,512]{1,0:T(8,128)(2,1)} copy(bf16[1176,512]{1,0:T(8,128)(2,1)} %get-tuple-element.52) | data formatting | bytes 2408448
  134.3 0.0 copy-done
  134.3 0.0 copy-start.2
  134.3 1.0 copy.38
  135.3 0.1 copy-done.3
  135.5 0.7 copy.39
  136.2 0.0 copy-done.10
  136.2 0.6 copy.40
  136.8 0.0 copy-done.9
  136.8 0.6 copy.41
  137.4 0.0 copy-done.2
  137.5 0.7 copy.42
  138.2 0.0 copy-done.4
  138.2 0.7 copy.43
  138.9 0.0 copy-done.1
  138.9 0.7 copy.44
  139.6 0.0 copy-done.8
  139.6 0.7 copy.45
  140.3 0.7 copy.46
  141.0 0.7 copy.47
  141.6 0.7 copy.48
  142.3 0.5 copy.49
  (14 shorter events, 0.0 us)
Async XLA Ops:
  131.8 2.5 %copy-start = (bf16[1176,512]{1,0:T(8,128)(2,1)S(1)}, bf16[1176,512]{1,0:T(8,128)(2,1)}, u32[]{:S(2)}) copy-start(bf16[1176,512]{1,0:T(8,128)(2,1)} %get-tuple-element.53) | copy-start | bytes 3612676
  134.3 1.2 copy-start.3
  134.3 1.9 %copy-start.10 = (f32[12,64]{1,0:T(8,128)S(1)}, f32[12,64]{1,0:T(8,128)}, u32[]{:S(2)}) copy-start(f32[12,64]{1,0:T(8,128)} %get-tuple-element.55) | copy-start | bytes 9220
  134.3 2.5 %copy-start.9 = (f32[12,128]{1,0:T(8,128)S(1)}, f32[12,128]{1,0:T(8,128)}, u32[]{:S(2)}) copy-start(f32[12,128]{1,0:T(8,128)} %get-tuple-element.56) | copy-start | bytes 18436
  134.3 3.1 %copy-start.2 = (f32[12,64,128]{2,1,0:T(8,128)S(1)}, f32[12,64,128]{2,1,0:T(8,128)}, u32[]{:S(2)}) copy-start(f32[12,64,128]{2,1,0:T(8,128)} %get-tuple-element.57) | copy-start | bytes 1179652
  135.5 2.7 %copy-start.4 = (bf16[12,64,128]{2,1,0:T(8,128)(2,1)S(1)}, bf16[12,64,128]{2,1,0:T(8,128)(2,1)}, u32[]{:S(2)}) copy-start(bf16[12,64,128]{2,1,0:T(8,128)(2,1)} %get-tuple-element.58) | copy-start | bytes 589828
  135.5 3.4 %copy-start.1 = (f32[12,64,128]{2,1,0:T(8,128)S(1)}, f32[12,64,128]{2,1,0:T(8,128)}, u32[]{:S(2)}) copy-start(f32[12,64,128]{2,1,0:T(8,128)} %get-tuple-element.59) | copy-start | bytes 1179652
  135.5 4.1 %copy-start.8 = (f32[71,512]{1,0:T(8,128)S(1)}, f32[71,512]{1,0:T(8,128)}, u32[]{:S(2)}) copy-start(f32[71,512]{1,0:T(8,128)} %get-tuple-element.60) | copy-start | bytes 436228
  136.2 4.1 %copy-start.7 = (f32[71,512]{1,0:T(8,128)S(1)}, f32[71,512]{1,0:T(8,128)}, u32[]{:S(2)}) copy-start(f32[71,512]{1,0:T(8,128)} %get-tuple-element.61) | copy-start | bytes 436228
  137.4 3.5 %copy-start.6 = (f32[71,512]{1,0:T(8,128)S(1)}, f32[71,512]{1,0:T(8,128)}, u32[]{:S(2)}) copy-start(f32[71,512]{1,0:T(8,128)} %get-tuple-element.62) | copy-start | bytes 436228
  138.2 3.4 %copy-start.5 = (f32[71,512]{1,0:T(8,128)S(1)}, f32[71,512]{1,0:T(8,128)}, u32[]{:S(2)}) copy-start(f32[71,512]{1,0:T(8,128)} %get-tuple-element.63) | copy-start | bytes 436228
  138.2 4.1 %copy-start.11 = (f32[1,83]{1,0:T(1,128)S(1)}, f32[1,83]{1,0:T(1,128)}, u32[]{:S(2)}) copy-start(f32[1,83]{1,0:T(1,128)} %get-tuple-element.38) | copy-start | bytes 1000

commit v4 on v3

v4 whole, which is shorter than its diff:
```python
import functools
import math
import types
from typing import Any, NamedTuple

import jax
import jax.numpy as jnp
from jax import lax
from jax.experimental import pallas as pl
from jax.experimental.pallas import tpu as pltpu
from jax.sharding import PartitionSpec as P

DP, HEAD = "dp", "head"
D = 512
HEAD_DIM = 64
GRID = 7
SMALL_GRID = 3
WINDOW = 7
IMG_GROUP = 3
CELLS = GRID * GRID
SLOTS = 8
CELL_PAD = CELLS + 1
ROWS = CELL_PAD * SLOTS
LANES = 128
WIDE = 256
REACHES = (1, 2, 3, 3)
HALO = WINDOW // 2

NORM_EPS = 1e-06
SQUARE_FLOOR = 1e-30
SECOND_DECAY = 0.999
STEP_RATE = 0.02
SMALL_RATE = 0.05
AVERAGE_KEEP = 0.9
NEG_LARGE = -1e30
ROOT_HALF = 0.7071067811865476
INV_ROOT_TAU = 0.3989422804014327
INV_SCALE = 1.0 / math.sqrt(HEAD_DIM)

F32 = jnp.float32
BF16 = jnp.bfloat16
NN = (((1,), (0,)), ((), ()))
NT = (((1,), (1,)), ((), ()))
TN = (((0,), (0,)), ((), ()))


def dot(a, b, dims=NN):
    return lax.dot_general(a, b, dims, preferred_element_type=F32)


def lane_block(b):
    return slice(b * WIDE, (b + 1) * WIDE)


def wide(col):
    return jnp.concatenate([col] * (D // LANES), axis=1)


def rows_loop(count, size, body, init=None, unroll=1):
    def step(j, carry):
        return body(pl.multiple_of(j * size, size), carry)

    return lax.fori_loop(0, count // size, step, init, unroll=unroll)


def conv(src, halo, tap, reach, lanes, put):
    def line(y, _):
        sums = [jnp.zeros((SLOTS, LANES), F32) for _ in range(GRID)]
        for a in range(-reach, reach + 1):
            base = (y + (a + halo)) * GRID
            cells = [src[base + x, :, lanes] for x in range(GRID)]
            for b in range(-reach, reach + 1):
                t = tap(a, b)
                for x in range(GRID):
                    if 0 <= x + b < GRID:
                        sums[x] = sums[x] + t * cells[x + b]
        for x in range(GRID):
            put(y * GRID + x, sums[x])
        return 0

    lax.fori_loop(0, GRID, line, 0)


def tap_sums(up, src, halo, reach, lanes, put):
    for a in range(-reach, reach + 1):

        def line(y, sums):
            sums = list(sums)
            ups = [up(y * GRID + x) for x in range(GRID)]
            base = (y + (a + halo)) * GRID
            cells = [src[base + x, :, lanes] for x in range(GRID)]
            for i, b in enumerate(range(-reach, reach + 1)):
                for x in range(GRID):
                    if 0 <= x + b < GRID:
                        sums[i] = sums[i] + ups[x] * cells[x + b]
            return tuple(sums)

        start = tuple(jnp.zeros((SLOTS, LANES), F32) for _ in range(2 * reach + 1))
        sums = lax.fori_loop(0, GRID, line, start)
        for i, b in enumerate(range(-reach, reach + 1)):
            put(a, b, jnp.sum(sums[i], axis=0, keepdims=True))


def fold(x):
    return jnp.sum(x.reshape(x.shape[0] // SLOTS, SLOTS, x.shape[1]), axis=0)


def erf_parts(h):
    e = lax.erf(h * ROOT_HALF)
    half = 0.5 * (1.0 + e)
    return h * half, half + h * jnp.exp(-0.5 * h * h) * INV_ROOT_TAU


def norm_rows(v, gain, shift):
    centre = jnp.sum(v, axis=1, keepdims=True) * (1.0 / D)
    offset = v - centre
    spread = jnp.sum(offset * offset, axis=1, keepdims=True) * (1.0 / D)
    inverse = lax.rsqrt(spread + NORM_EPS)
    unit = offset * inverse
    return unit * gain + shift, unit, inverse


def norm_back(up, unit, inverse, gain):
    z = up * gain
    mean_z = jnp.sum(z, axis=1, keepdims=True) * (1.0 / D)
    mean_zu = jnp.sum(z * unit, axis=1, keepdims=True) * (1.0 / D)
    return inverse * (z - mean_z - unit * mean_zu)


class Block:
    def __init__(self, refs):
        self.__dict__.update(refs)

    def matrix(self, k, lo, hi):
        parts = []
        for h in range(lo, hi):
            part = self.w[h // 2, h % 2, :, :, :, k]
            if part.shape[-2] % 16:
                part = part.astype(F32).reshape(D, LANES).astype(BF16)
            else:
                part = part.reshape(D, LANES)
            parts.append(part)
        return jnp.concatenate(parts, axis=1)

    def times(self, lhs, k, b):
        return dot(lhs, self.matrix(k, 2 * b, 2 * b + 2))

    def times_t(self, lhs, k, b):
        return dot(lhs, self.matrix(k, 0, 4)[lane_block(b), :], NT)

    def put_grad(self, k, lhs_t, rhs):
        for b in range(2):
            g = dot(lhs_t, rhs[:, lane_block(b)])
            for i in range(2):
                piece = g[:, i * LANES : (i + 1) * LANES]
                place = self.g.shape[2:5]
                piece = piece.reshape(*place, self.g.shape[-2], LANES)
                self.g[b, i, :, :, :, k] = piece.astype(BF16)

    def row(self, j):
        return self.small[j : j + 1, :]

    def setup(self):
        head = lax.axis_index(HEAD)
        slots = self.cls.shape[1]
        self.sums[...] = jnp.zeros(self.sums.shape, F32)
        sub = lax.broadcasted_iota(jnp.int32, (SLOTS, LANES), 0)
        valid = jnp.where(sub < slots, 1.0, 0.0)
        full = jnp.zeros((SLOTS, LANES), F32)
        images = [jnp.zeros((SLOTS, LANES), F32) for _ in range(IMG_GROUP)]
        for s in range(slots):
            full = jnp.where(sub == s, jnp.where(self.cls[head, s] == 0, 1.0, 0.0), full)
            for i in range(IMG_GROUP):
                images[i] = jnp.where(
                    sub == s, jnp.where(self.img[head, s] == i, 1.0, 0.0), images[i]
                )
        for cell in range(CELLS):
            small = cell // GRID < SMALL_GRID and cell % GRID < SMALL_GRID
            self.live[cell * SLOTS : (cell + 1) * SLOTS, :] = valid if small else full
        self.live[CELLS * SLOTS :, :] = jnp.zeros((SLOTS, LANES), F32)
        for i in range(IMG_GROUP):
            self.im8[i] = images[i]
            self.im16[i] = jnp.concatenate([images[i], images[i]], axis=0).astype(BF16)
        self.pos_src[0:GRID] = jnp.zeros((GRID, SLOTS, D), F32)
        self.pos_src[GRID + CELLS :] = jnp.zeros((GRID, SLOTS, D), F32)
        for pad in (self.rel_src, self.dq_src):
            pad[0 : HALO * GRID] = jnp.zeros((HALO * GRID, SLOTS, D), F32)
            pad[HALO * GRID + CELLS :] = jnp.zeros((HALO * GRID, SLOTS, D), F32)
        tap = lax.broadcasted_iota(jnp.int32, (WINDOW * WINDOW, 1), 0)
        row_off = jnp.abs(tap // WINDOW - HALO)
        col_off = jnp.abs(tap % WINDOW - HALO)
        off = jnp.maximum(row_off, col_off)
        heads = lax.broadcasted_iota(jnp.int32, (1, D), 1) // HEAD_DIM
        reach = jnp.where(heads < 2, 1, jnp.where(heads < 5, 2, 3))
        mask = jnp.where(off <= reach, 1.0, 0.0)
        self.window[...] = mask
        self.rel_taps[...] = self.small[22 : 22 + WINDOW * WINDOW, :] * mask

    def place(self, rows_ref, first, r0, size):
        count = rows_ref.shape[0]
        r = r0 + lax.broadcasted_iota(jnp.int32, (size, 1), 0)
        cell, slot = r >> 3, r & 7
        want = first + slot * CELLS + cell
        want = jnp.where((slot < self.cls.shape[1]) & (cell < CELLS), want, -1)
        col = lax.broadcasted_iota(jnp.int32, (size, count), 1)
        pick = jnp.where(col == want, 1.0, 0.0).astype(BF16)
        return dot(pick, rows_ref[...])

    def unplace(self, src_ref, out_ref):
        count = out_ref.shape[0]
        own = self.cls.shape[1] * CELLS
        lead = lax.rem(lax.axis_index(HEAD) * own, 16)
        r = lax.broadcasted_iota(jnp.int32, (1, ROWS), 1)
        cell, slot = r >> 3, r & 7
        target = lead + slot * CELLS + cell
        target = jnp.where((slot < self.cls.shape[1]) & (cell < CELLS), target, -1)
        t = lax.broadcasted_iota(jnp.int32, (count, ROWS), 0)
        pick = jnp.where(t == target, 1.0, 0.0).astype(BF16)
        out_ref[...] = dot(pick, src_ref[...]).astype(BF16)

    def read_tokens(self):
        first = lax.axis_index(HEAD) * (self.cls.shape[1] * CELLS)
        size = 80

        def body(r0, _):
            live = wide(self.live[pl.ds(r0, size), :])
            x = self.place(self.tokens, first, r0, size)
            self.first[pl.ds(r0, size), :] = x
            c0 = r0 // SLOTS
            self.pos_src[pl.ds(GRID + c0, size // SLOTS)] = (x * live).reshape(-1, SLOTS, D)
            return 0

        rows_loop(ROWS, size, body, 0)

    def read_cotangent(self):
        first = lax.axis_index(HEAD) * (self.cls.shape[1] * CELLS)
        size = 80

        def body(r0, _):
            live = wide(self.live[pl.ds(r0, size), :])
            c = self.place(self.cot, first, r0, size)
            self.go[pl.ds(r0, size), :] = (c * live).astype(BF16)
            return 0

        rows_loop(ROWS, size, body, 0)
        self.go_t[...] = self.go[...].T
        self.back[...] = jnp.zeros((ROWS, D), F32)

    def norm_one(self):
        for c in range(D // LANES):
            lanes = slice(c * LANES, (c + 1) * LANES)

            def put(cell, value):
                rows = pl.ds(pl.multiple_of(cell * SLOTS, SLOTS), SLOTS)
                self.first[rows, lanes] = self.first[rows, lanes] + value + self.small[8:9, lanes]

            def tap(a, b):
                t = 13 + (a + 1) * 3 + b + 1
                return self.small[t : t + 1, lanes]

            conv(self.pos_src, 1, tap, 1, lanes, put)

        def body(r0, _):
            rows = pl.ds(r0, 16)
            n, u, inv = norm_rows(self.first[rows, :], self.row(0), self.row(1))
            self.n1[rows, :] = n.astype(BF16)
            self.u1[rows, :] = u
            self.inv1[rows, :] = jnp.broadcast_to(inv, (16, LANES))
            return 0

        rows_loop(ROWS, 16, body, 0, unroll=5)
        self.n1_t[...] = self.n1[...].T

    def project(self, k):
        low = (self.q, self.k, self.v)[k]
        for b in range(2):
            cols = lane_block(b)
            p = self.times(self.n1[...], k, b)
            if k != 1:
                p = p + self.small[2 + k // 2 : 3 + k // 2, cols]
            low[:, cols] = p.astype(BF16)

    def image_sum(self, x):
        total = jnp.zeros((SLOTS, D), F32)
        for i in range(IMG_GROUP):
            im = wide(self.im8[i])
            total = total + im * jnp.sum(im * x, axis=0, keepdims=True)
        return total

    def softmax(self):
        def top(r0, best):
            live = wide(self.live[pl.ds(r0, 16), :])
            keys = jnp.where(live > 0, self.k[pl.ds(r0, 16), :].astype(F32), NEG_LARGE)
            return jnp.maximum(best, jnp.max(keys.reshape(2, SLOTS, D), axis=0))

        best = rows_loop(ROWS, 16, top, jnp.full((SLOTS, D), NEG_LARGE, F32), unroll=5)
        shift = jnp.zeros((SLOTS, D), F32)
        for i in range(IMG_GROUP):
            im = wide(self.im8[i])
            most = jnp.max(jnp.where(im > 0, best, NEG_LARGE), axis=0, keepdims=True)
            shift = jnp.where(im > 0, most, shift)
        shift2 = jnp.concatenate([shift, shift], axis=0)

        def raise_(r0, total):
            rows = pl.ds(r0, 16)
            live = wide(self.live[rows, :])
            keys = self.k[rows, :].astype(F32)
            e = jnp.where(live > 0, jnp.exp(jnp.where(live > 0, keys - shift2, 0.0)), 0.0)
            self.soft[rows, :] = e
            return total + fold(e)

        total = self.image_sum(
            rows_loop(ROWS, 16, raise_, jnp.zeros((SLOTS, D), F32), unroll=5)
        )
        scale = 1.0 / jnp.where(total > 0, total, 1.0)
        scale2 = jnp.concatenate([scale, scale], axis=0)

        def divide(r0, _):
            rows = pl.ds(r0, 16)
            soft = self.soft[rows, :] * scale2
            self.soft[rows, :] = soft
            self.soft_low[rows, :] = soft.astype(BF16)
            return 0

        rows_loop(ROWS, 16, divide, 0, unroll=5)

    def by_image(self, x):
        tiles = x.reshape(ROWS // 16, 16, WIDE)
        parts = []
        for i in range(IMG_GROUP):
            im = jnp.concatenate([self.im16[i]] * (WIDE // LANES), axis=1)
            parts.append((tiles * im[None]).reshape(ROWS, WIDE))
        return jnp.concatenate(parts, axis=1)

    def head_blocks(self, x):
        r = lax.broadcasted_iota(jnp.int32, x.shape, 0) // HEAD_DIM
        c = (lax.broadcasted_iota(jnp.int32, x.shape, 1) % WIDE) // HEAD_DIM
        return jnp.where(r == c, x, 0.0).astype(BF16)

    def stacked(self, x):
        return jnp.concatenate([x[:, lane_block(i)] for i in range(IMG_GROUP)], axis=0)

    def contexts(self):
        for b in range(2):
            cols = lane_block(b)
            ctx = dot(self.soft_low[:, cols], self.by_image(self.v[:, cols]), TN)
            ctx = self.head_blocks(ctx)
            self.ctx[b] = ctx
            self.factor[:, cols] = dot(self.by_image(self.q[:, cols]), self.stacked(ctx))

    def fill_window(self):
        def fill(r0, _):
            rows = pl.ds(r0, 16)
            v = self.v[rows, :].astype(F32) * wide(self.live[rows, :])
            c0 = r0 // SLOTS
            self.rel_src[pl.ds(HALO * GRID + c0, 2)] = v.reshape(2, SLOTS, D)
            return 0

        rows_loop(ROWS, 16, fill, 0, unroll=5)
        self.rel[CELLS * SLOTS :, :] = jnp.zeros((SLOTS, D), F32)

    def window_sum(self, c):
        lanes = slice(c * LANES, (c + 1) * LANES)

        def put(cell, value):
            rows = pl.ds(pl.multiple_of(cell * SLOTS, SLOTS), SLOTS)
            self.rel[rows, lanes] = value

        def tap(a, b):
            t = (a + HALO) * WINDOW + b + HALO
            return self.rel_taps[t : t + 1, lanes]

        conv(self.rel_src, HALO, tap, REACHES[c], lanes, put)

    def mix(self):
        def mix(r0, _):
            rows = pl.ds(r0, 16)
            m = self.factor[rows, :] * INV_SCALE + self.q[rows, :].astype(F32) * self.rel[rows, :]
            self.mixed[rows, :] = (m * wide(self.live[rows, :])).astype(BF16)
            return 0

        rows_loop(ROWS, 16, mix, 0, unroll=5)

    def norm_two(self):
        for b in range(2):
            cols = lane_block(b)
            p = self.times_t(self.mixed[...], 3, b)
            self.second[:, cols] = self.first[:, cols] + p + self.small[4:5, cols]

        def body(r0, _):
            rows = pl.ds(r0, 16)
            n, u, inv = norm_rows(self.second[rows, :], self.row(5), self.row(6))
            self.n2[rows, :] = n.astype(BF16)
            self.u2[rows, :] = u
            self.inv2[rows, :] = jnp.broadcast_to(inv, (16, LANES))
            return 0

        rows_loop(ROWS, 16, body, 0, unroll=5)
        self.n2_t[...] = self.n2[...].T

    def hidden_block(self, r):
        up, down = 4 + 2 * r, 5 + 2 * r
        for b in range(2):
            cols = lane_block(b)
            h = self.times(self.n2[...], up, b) + self.small[pl.ds(9 + r, 1), cols]
            self.hidden[:, cols] = h
            self.factor[:, cols] = self.times(self.go[...], down, b)

        def body(r0, total):
            rows = pl.ds(r0, 16)
            act, slope = erf_parts(self.hidden[rows, :])
            g = self.factor[rows, :] * slope
            self.active[rows, :] = act.astype(BF16)
            self.low[rows, :] = g.astype(BF16)
            return total + fold(g)

        total = rows_loop(ROWS, 16, body, jnp.zeros((SLOTS, D), F32), unroll=5)
        self.sums[pl.ds(9 + r, 1), :] = jnp.sum(total, axis=0, keepdims=True)

    def hidden_grads(self, r):
        up, down = 4 + 2 * r, 5 + 2 * r
        self.put_grad(down, self.go_t[...], self.active)
        self.put_grad(up, self.n2_t[...], self.low)
        for b in range(2):
            cols = lane_block(b)
            self.second[:, cols] += self.times_t(self.active[...], down, b)
            self.back[:, cols] += self.times_t(self.low[...], up, b)

    def finish_out(self):
        def body(r0, _):
            rows = pl.ds(r0, 16)
            self.out_low[rows, :] = (self.second[rows, :] + self.row(7)).astype(BF16)
            return 0

        rows_loop(ROWS, 16, body, 0, unroll=5)
        self.unplace(self.out_low, self.out_own)

    def back_two(self):
        zero = jnp.zeros((SLOTS, D), F32)

        def body(r0, sums):
            rows = pl.ds(r0, 16)
            back, u = self.back[rows, :], self.u2[rows, :]
            go = self.go[rows, :].astype(F32)
            gs = go + norm_back(back, u, wide(self.inv2[rows, :]), self.row(5))
            self.gs[rows, :] = gs
            self.gs_low[rows, :] = gs.astype(BF16)
            new = (gs, back * u, back, go)
            return tuple(s + fold(n) for s, n in zip(sums, new, strict=True))

        sums = rows_loop(ROWS, 16, body, (zero,) * 4, unroll=5)
        for j, s in zip((4, 5, 6, 7), sums, strict=True):
            self.sums[j : j + 1, :] = jnp.sum(s, axis=0, keepdims=True)

    def grad_proj(self):
        self.put_grad(3, self.gs_low[...].T, self.mixed)

    def back_heads(self):
        for b in range(2):
            cols = lane_block(b)
            self.d[:, cols] = self.times(self.gs_low[...], 3, b)

        def fill(r0, _):
            rows = pl.ds(r0, 16)
            d = self.d[rows, :] * wide(self.live[rows, :])
            self.d[rows, :] = d
            self.f[rows, :] = (d * INV_SCALE).astype(BF16)
            c0 = r0 // SLOTS
            dq = d * self.q[rows, :].astype(F32)
            self.dq_src[pl.ds(HALO * GRID + c0, 2)] = dq.reshape(2, SLOTS, D)
            return 0

        rows_loop(ROWS, 16, fill, 0, unroll=5)
        for b in range(2):
            cols = lane_block(b)
            f3 = self.by_image(self.f[:, cols])
            g = self.head_blocks(dot(self.q[:, cols], f3, TN))
            self.gq[:, cols] = dot(f3, self.ctx[b], NT)
            self.gk[:, cols] = dot(self.by_image(self.v[:, cols]), g, NT)
            self.gv[:, cols] = dot(self.by_image(self.soft_low[:, cols]), self.stacked(g))

    def back_window(self, c):
        lanes = slice(c * LANES, (c + 1) * LANES)

        def put(cell, value):
            rows = pl.ds(pl.multiple_of(cell * SLOTS, SLOTS), SLOTS)
            self.gv[rows, lanes] = self.gv[rows, lanes] + value * self.live[rows, :]

        def tap(a, b):
            t = (HALO - a) * WINDOW + HALO - b
            return self.rel_taps[t : t + 1, lanes]

        conv(self.dq_src, HALO, tap, REACHES[c], lanes, put)

    def window_taps(self, c):
        lanes = slice(c * LANES, (c + 1) * LANES)

        def up(cell):
            return self.dq_src[HALO * GRID + cell, :, lanes]

        def put_tap(a, b, value):
            t = (a + HALO) * WINDOW + b + HALO
            keep = self.window[t : t + 1, lanes]
            self.sums[22 + t : 23 + t, lanes] = value * keep

        tap_sums(up, self.rel_src, HALO, REACHES[c], lanes, put_tap)

    def back_query_key(self):
        zero = jnp.zeros((SLOTS, D), F32)

        def inner(r0, total):
            rows = pl.ds(r0, 16)
            return total + fold(self.soft[rows, :] * self.gk[rows, :])

        shared = self.image_sum(rows_loop(ROWS, 16, inner, zero, unroll=5))
        shared2 = jnp.concatenate([shared, shared], axis=0)

        def low(r0, total):
            rows = pl.ds(r0, 16)
            gq = self.gq[rows, :] + self.d[rows, :] * self.rel[rows, :]
            gk = self.soft[rows, :] * (self.gk[rows, :] - shared2)
            self.gl[0, rows, :] = gq.astype(BF16)
            self.gl[1, rows, :] = gk.astype(BF16)
            return total + fold(gq)

        total = rows_loop(ROWS, 16, low, zero, unroll=5)
        self.sums[2:3, :] = jnp.sum(total, axis=0, keepdims=True)

    def back_value(self):
        def low(r0, total):
            rows = pl.ds(r0, 16)
            gv = self.gv[rows, :]
            self.gl[2, rows, :] = gv.astype(BF16)
            return total + fold(gv)

        total = rows_loop(ROWS, 16, low, jnp.zeros((SLOTS, D), F32), unroll=5)
        self.sums[3:4, :] = jnp.sum(total, axis=0, keepdims=True)
        self.grad_of(2)

    def grad_of(self, k):
        self.put_grad(k, self.n1_t[...], self.gl.at[k])

    def back_project(self):
        for b in range(2):
            cols = lane_block(b)
            back = self.times_t(self.gl[0], 0, b)
            back = back + self.times_t(self.gl[1], 1, b)
            self.back[:, cols] = back + self.times_t(self.gl[2], 2, b)

    def back_one(self):
        zero = jnp.zeros((SLOTS, D), F32)
        self.pos_up[0:GRID] = jnp.zeros((GRID, SLOTS, D), F32)
        self.pos_up[GRID + CELLS :] = jnp.zeros((GRID, SLOTS, D), F32)

        def body(r0, sums):
            rows = pl.ds(r0, 16)
            back, u = self.back[rows, :], self.u1[rows, :]
            gf = self.gs[rows, :] + norm_back(back, u, wide(self.inv1[rows, :]), self.row(0))
            c0 = r0 // SLOTS
            self.pos_up[pl.ds(GRID + c0, 2)] = gf.reshape(2, SLOTS, D)
            new = (back * u, back, gf)
            return tuple(s + fold(n) for s, n in zip(sums, new, strict=True))

        sums = rows_loop(ROWS, 16, body, (zero,) * 3, unroll=5)
        for j, s in zip((0, 1, 8), sums, strict=True):
            self.sums[j : j + 1, :] = jnp.sum(s, axis=0, keepdims=True)

    def back_position(self):
        for c in range(D // LANES):
            lanes = slice(c * LANES, (c + 1) * LANES)

            def put(cell, value):
                rows = pl.ds(pl.multiple_of(cell * SLOTS, SLOTS), SLOTS)
                gf = self.pos_up[GRID + cell, :, lanes]
                self.first[rows, lanes] = gf + value * self.live[rows, :]

            def tap(a, b):
                t = 13 + (1 - a) * 3 + 1 - b
                return self.small[t : t + 1, lanes]

            conv(self.pos_up, 1, tap, 1, lanes, put)

    def position_taps(self):
        for c in range(D // LANES):
            lanes = slice(c * LANES, (c + 1) * LANES)

            def up(cell):
                return self.pos_up[GRID + cell, :, lanes]

            def put_tap(a, b, value):
                t = 13 + (a + 1) * 3 + b + 1
                self.sums[t : t + 1, lanes] = value

            tap_sums(up, self.pos_src, 1, 1, lanes, put_tap)

    def finish_in(self):
        def down(r0, _):
            rows = pl.ds(r0, 16)
            self.in_low[rows, :] = self.first[rows, :].astype(BF16)
            return 0

        rows_loop(ROWS, 16, down, 0, unroll=5)
        self.unplace(self.in_low, self.in_own)


SLOT_OF = (0, 1, 2, 3, 4, 6, 8, 10, 5, 7, 9, 11)
MATS = len(SLOT_OF)
AXES = "xchly"
HEAD_ROWS = 320
SMALL_ROWS = 72
AG_ROUTES = ("hlxyc", "lyhxc", "hlxyc", "hlyxc", "xyhlc", "xhlyc", "yhlxc", "lyhxc", "hlxyc", "xhylc", "hlxyc", "lxyhc")
RS_ROUTES = ("cylhx", "clyxh", "cyxlh", "clxyh", "cyxhl", "cxylh", "clhxy", "cxylh", "cylxh", "cxylh", "cyxlh", "cxylh")
ORDER = (
    30, 6, 12, 0, 18, 24, 36, 42, 48, 54, 60, 66, 144, 145, 31, 7, 146, 13, 1, 19,
    8, 25, 49, 37, 43, 55, 61, 67, 147, 32, 14, 26, 2, 44, 68, 20, 9, 50, 15, 38,
    69, 3, 62, 56, 21, 33, 10, 27, 16, 51, 11, 149, 151, 4, 45, 39, 17, 150, 153, 157,
    22, 156, 5, 148, 152, 34, 155, 28, 57, 23, 63, 46, 70, 154, 158, 159, 29, 52, 40, 47,
    35, 160, 161, 58, 53, 64, 71, 102, 96, 41, 162, 163, 59, 164, 65, 108, 103, 97, 114, 165,
    166, 120, 167, 132, 126, 138, 109, 115, 168, 121, 133, 98, 127, 104, 139, 189, 169, 171, 177, 178,
    176, 172, 175, 170, 179, 184, 84, 173, 174, 90, 72, 78, 122, 185, 85, 187, 91, 73, 183, 79,
    181, 180, 128, 123, 110, 134, 140, 99, 186, 86, 105, 188, 92, 192, 116, 182, 74, 195, 135, 124,
    80, 129, 87, 190, 196, 141, 111, 93, 106, 117, 100, 191, 75, 81, 136, 94, 125, 130, 88, 142,
    107, 118, 101, 193, 197, 76, 112, 137, 82, 95, 194, 131, 77, 89, 198, 113, 143, 119, 83, 204,
    199, 205, 200, 201, 206, 202, 203, 207,
)


def scratch_of():
    f, h, low = (ROWS, D), (ROWS, LANES), pltpu.VMEM((ROWS, D), BF16)
    halo3 = pltpu.VMEM(((GRID + 2 * HALO) * GRID, SLOTS, D), F32)
    halo1 = pltpu.VMEM(((GRID + 2) * GRID, SLOTS, D), F32)
    high, column, turned = pltpu.VMEM(f, F32), pltpu.VMEM(h, F32), pltpu.VMEM((D, ROWS), BF16)
    taps = pltpu.VMEM((WINDOW * WINDOW, D), F32)
    return dict(
        live=column,
        im8=pltpu.VMEM((IMG_GROUP, SLOTS, LANES), F32),
        im16=pltpu.VMEM((IMG_GROUP, 16, LANES), BF16),
        window=taps,
        rel_taps=taps,
        pos_src=halo1,
        pos_up=halo1,
        rel_src=halo3,
        dq_src=halo3,
        first=high,
        u1=high,
        inv1=column,
        second=high,
        u2=high,
        inv2=column,
        n1=low,
        n1_t=turned,
        n2=low,
        n2_t=turned,
        go=low,
        go_t=turned,
        q=low,
        k=low,
        v=low,
        soft=high,
        soft_low=low,
        ctx=pltpu.VMEM((2, WIDE, IMG_GROUP * WIDE), BF16),
        factor=high,
        rel=high,
        mixed=low,
        hidden=high,
        active=low,
        low=low,
        out_low=low,
        back=high,
        gs=high,
        gs_low=low,
        d=high,
        f=low,
        gq=high,
        gk=high,
        gv=high,
        gl=pltpu.VMEM((3, ROWS, D), BF16),
        in_low=low,
    )


class Links:
    def __init__(self):
        dp, head = lax.axis_index(DP), lax.axis_index(HEAD)
        self.far = lax.axis_size(DP) // 4
        self.at = dict(x=head // 2, c=head % 2, h=dp // 4, l=dp // 2 % 2, y=dp % 2)

    def count(self, axis):
        return self.far if axis == "h" else 2

    def peer(self, axis, step):
        return lax.rem(self.at[axis] + step, self.count(axis))

    def device(self, axis, step):
        at = {**self.at, axis: self.peer(axis, step)}
        return (at["h"] * 4 + at["l"] * 2 + at["y"], at["x"] * 2 + at["c"])

    def steps(self, axis, do):
        self.repeat(self.count(axis), do)

    def repeat(self, size, do):
        if size <= 8:
            for step in range(1, size):
                do(step)
        else:

            def body(step, _):
                do(step)
                return 0

            lax.fori_loop(1, size, body, 0)

    def others(self, name, do):
        index = {DP: lax.axis_index(DP), HEAD: lax.axis_index(HEAD)}

        def one(step):
            at = {**index, name: lax.rem(index[name] + step, lax.axis_size(name))}
            do(step, (at[DP], at[HEAD]))

        self.repeat(lax.axis_size(name), one)

    def greet(self):
        barrier = pltpu.get_barrier_semaphore()

        def signal(step, device):
            pl.semaphore_signal(
                barrier, inc=1, device_id=device, device_id_type=pl.DeviceIdType.MESH
            )

        self.others(HEAD, signal)
        self.others(DP, signal)
        pl.semaphore_wait(barrier, lax.axis_size(HEAD) + lax.axis_size(DP) - 2)

    def copy(self, src, dst, send, recv, device):
        return pltpu.make_async_remote_copy(
            src_ref=src,
            dst_ref=dst,
            send_sem=send,
            recv_sem=recv,
            device_id=device,
            device_id_type=pl.DeviceIdType.MESH,
        )

    def region(self, blocks, slot, whole, **at):
        at = {**self.at, **at}
        place = [slice(None) if axis in whole else at[axis] for axis in AXES]
        return blocks.at[(*place, slot)]


class Gather:
    def __init__(self, links, w, send, recv):
        self.links, self.w, self.send, self.recv = links, w, send, recv

    def start(self, slot, phase):
        path = AG_ROUTES[slot]
        part = self.links.region(self.w, slot, path[:phase])
        sems = self.send.at[slot, phase], self.recv.at[slot, phase]

        def go(step):
            self.links.copy(part, part, *sems, self.links.device(path[phase], step)).start()

        self.links.steps(path[phase], go)

    def descriptor(self, slot, phase):
        path = AG_ROUTES[slot]
        at = {"h": pl.ds(0, self.links.far - 1)} if path[phase] == "h" else {}
        part = self.links.region(self.w, slot, path[:phase], **at)
        sems = self.send.at[slot, phase], self.recv.at[slot, phase]
        return self.links.copy(part, part, *sems, self.links.device(path[phase], 1))

    def tick(self, slot, phase):
        if phase:
            self.descriptor(slot, phase - 1).wait_recv()
        if phase < len(AXES):
            self.start(slot, phase)

    def sent(self):
        for slot in range(MATS):
            for phase in range(len(AXES)):
                self.descriptor(slot, phase).wait_send()


class Scatter:
    def __init__(self, links, g, boxes, total, send, recv):
        self.links, self.g, self.boxes, self.total = links, g, boxes, total
        self.send, self.recv = send, recv

    def descriptor(self, slot, phase):
        box = self.boxes[slot * len(AXES) + phase]
        sems = self.send.at[slot, phase], self.recv.at[slot, phase]
        return self.links.copy(box, box, *sems, self.links.device(RS_ROUTES[slot][phase], 1))

    def take(self, slot, phase):
        path = RS_ROUTES[slot]
        self.descriptor(slot, phase).wait_recv()
        own = self.links.region(self.g, slot, path[phase + 1 :])
        box = self.boxes[slot * len(AXES) + phase]
        if path[phase] == "h" and box.shape[0] == 1:
            box = box.at[0]
        elif path[phase] == "h":
            value = own[...].astype(F32)
            return own, value + jnp.sum(box[...].astype(F32), axis=0)
        return own, own[...] + box[...] if phase + 1 < len(AXES) else (
            own[...].astype(F32) + box[...].astype(F32)
        )

    def start(self, slot, phase):
        path = RS_ROUTES[slot]
        axis, rest = path[phase], path[phase + 1 :]
        box = self.boxes[slot * len(AXES) + phase]
        sems = self.send.at[slot, phase], self.recv.at[slot, phase]

        def go(step):
            at = {axis: self.links.peer(axis, step)}
            part = self.links.region(self.g, slot, rest, **at)
            into = box.at[step - 1] if axis == "h" else box
            self.links.copy(part, into, *sems, self.links.device(axis, step)).start()

        self.links.steps(axis, go)

    def tick(self, slot, phase):
        if phase:
            own, value = self.take(slot, phase - 1)
            if phase == len(AXES):
                self.total[SLOT_OF.index(slot)] = value
                return
            own[...] = value.astype(BF16)
        self.start(slot, phase)

    def sent(self):
        for slot in range(MATS):
            for phase in range(len(AXES)):
                self.descriptor(slot, phase).wait_send()


class Small:
    def __init__(self, links, sums, parts, in_c, in_x, in_y, in_h, in_l, full, send, recv):
        self.links, self.sums, self.parts, self.full = links, sums, parts, full
        self.in_c, self.in_x, self.in_y, self.in_h, self.in_l = in_c, in_x, in_y, in_h, in_l
        self.send, self.recv = send, recv

    def go(self, stage, src, dst, axis):
        sems = (self.send.at[stage], self.recv.at[stage])
        self.links.steps(
            axis, lambda step: self.links.copy(src, dst, *sems, self.links.device(axis, step)).start()
        )

    def wait(self, stage):
        x, c = self.links.at["x"], self.links.at["c"]
        ref = (
            self.in_c,
            self.in_x,
            self.in_y,
            self.in_h.at[pl.ds(0, self.links.far - 1)],
            self.in_l,
            self.full.at[c, x],
            self.full.at[c],
        )[stage]
        sems = (self.send.at[stage], self.recv.at[stage])
        return self.links.copy(ref, ref, *sems, self.links.device("cxyhlxc"[stage], 1))

    def tick(self, stage):
        at = self.links.at
        x, c, h = at["x"], at["c"], at["h"]
        mine = self.parts.at[c, x]
        if stage:
            self.wait(stage - 1).wait_recv()
        if stage == 0:
            for b in range(D // LANES):
                self.parts[b // 2, b % 2] = self.sums[:, b * LANES : (b + 1) * LANES]
            self.go(0, self.parts.at[1 - c], self.in_c, "c")
        if stage == 1:
            self.parts[c] = self.parts[c] + self.in_c[...]
            self.go(1, self.parts.at[c, 1 - x], self.in_x, "x")
        if stage == 2:
            mine[...] = mine[...] + self.in_x[...]
            self.go(2, mine, self.in_y, "y")
        if stage == 3:
            self.in_h[h] = mine[...] + self.in_y[...]
            self.go(3, self.in_h.at[h], self.in_h.at[h], "h")
        if stage == 4:
            total = self.in_h[0]
            for i in range(1, self.links.far):
                total = total + self.in_h[i]
            self.sums[:, 0:LANES] = total
            self.go(4, self.sums.at[:, pl.ds(0, LANES)], self.in_l, "l")
        if stage == 5:
            self.full[c, x] = self.sums[:, 0:LANES] + self.in_l[...]
            self.go(5, self.full.at[c, x], self.full.at[c, x], "x")
        if stage == 6:
            self.go(6, self.full.at[c], self.full.at[c], "c")

    def sent(self):
        for stage in range(7):
            self.wait(stage).wait_send()


class Rows:
    def __init__(self, links, blocks, out, own, send, recv):
        self.links, self.blocks, self.out, self.own = links, blocks, out, own
        self.send, self.recv = send, recv

    def hop(self, i):
        x, c = self.links.at["x"], self.links.at["c"]
        x, axis = ((x, "x"), (x, "c"), (1 - x, "c"))[i]
        block = self.blocks.at[2 * x + c]
        return self.links.copy(
            block, block, self.send.at[i], self.recv.at[i], self.links.device(axis, 1)
        )

    def tick(self, stage):
        if stage == 0:
            self.hop(0).start()
            self.hop(1).start()
        if stage == 1:
            self.hop(0).wait_recv()
            self.hop(2).start()
        if stage == 2:
            self.hop(1).wait_recv()
            self.hop(2).wait_recv()
            self.join()

    def sent(self):
        for i in range(3):
            self.hop(i).wait_send()

    def join(self):
        heads, end, own = self.blocks.shape[0], self.out.shape[0], self.own
        for h in range(heads):
            lo, hi = h * own, (h + 1) * own
            base = lo // 16 * 16
            first = base + 16 if lo % 16 else base
            last = hi // 16 * 16 if h + 1 < heads else end
            self.out[first:last, :] = self.blocks[h, first - base : last - base, :]
            if lo % 16:
                before = (lo - own) // 16 * 16
                tail = self.blocks[h - 1, base - before : base - before + 16, :]
                self.out[base : base + 16, :] = tail + self.blocks[h, 0:16, :]


class Exchange:
    def __init__(self, links, name, buffer, send, recv):
        self.links, self.name, self.buffer, self.send, self.recv = links, name, buffer, send, recv

    def start(self, value):
        own = lax.axis_index(self.name)
        self.buffer[own] = value
        mine = self.buffer.at[own]
        self.links.others(
            self.name,
            lambda step, device: self.links.copy(mine, mine, self.send, self.recv, device).start(),
        )

    def descriptor(self):
        ref = self.buffer.at[pl.ds(0, self.buffer.shape[0] - 1)]
        return self.links.copy(ref, ref, self.send, self.recv, self.links.device("c", 1))

    def total(self):
        self.descriptor().wait_recv()
        return jnp.sum(self.buffer[...], axis=0)

    def sent(self):
        self.descriptor().wait_send()


def exact(a, b, dims):
    return lax.dot_general(
        a, b, dims, precision=lax.Precision.HIGHEST, preferred_element_type=F32
    )


class Adafactor:
    def __init__(self, refs, row_share, col_share, sq_dp, sq_head):
        self.__dict__.update(refs)
        self.row_share, self.col_share = row_share, col_share
        self.sq_dp, self.sq_head = sq_dp, sq_head

    def eye(self, count):
        r = lax.broadcasted_iota(jnp.int32, (count, LANES), 0)
        c = lax.broadcasted_iota(jnp.int32, (count, LANES), 1)
        return jnp.where(r == c, 1.0, 0.0)

    def lane(self, k, value, rest):
        lanes = lax.broadcasted_iota(jnp.int32, rest.shape, 1)
        return jnp.where(lanes == k, value, rest)

    def squares(self):
        rows = self.wg.shape[1]
        by_row = jnp.zeros((rows, LANES), F32)
        by_col = []
        for k in range(MATS):
            g = self.wg[k]
            s = g * g + SQUARE_FLOOR
            by_row = self.lane(k, jnp.sum(s, axis=1, keepdims=True), by_row)
            by_col.append(jnp.sum(s, axis=0, keepdims=True))
        self.col_share.start(jnp.concatenate([*by_col, jnp.zeros((4, LANES), F32)], axis=0))
        turned = exact(self.eye(16), by_row, NT)
        if rows < LANES:
            turned = jnp.concatenate([turned, jnp.zeros((16, LANES - rows), F32)], axis=1)
        self.row_share.start(turned)

    def scale(self):
        rows = self.wg.shape[1]
        total = self.row_share.total()[0:MATS, 0:rows]
        new_rows = SECOND_DECAY * self.row_state[...] + (1.0 - SECOND_DECAY) * (total * (1.0 / D))
        self.new_rows[...] = new_rows
        row = exact(new_rows, self.eye(MATS), TN)
        total = self.col_share.total()[0:MATS]
        cols = SECOND_DECAY * self.col_state[...] + (1.0 - SECOND_DECAY) * (total * (1.0 / D))
        self.new_cols[...] = cols
        sums = jnp.zeros((1, LANES), F32)
        for k in range(MATS):
            u = self.wg[k] * lax.rsqrt(row[:, k : k + 1] * cols[k : k + 1, :])
            self.upd[k] = u
            s = jnp.sum(jnp.sum(u * u, axis=0, keepdims=True), axis=1, keepdims=True)
            sums = self.lane(k, s, sums)
        mass = jnp.sum(row, axis=0, keepdims=True)
        self.sq_dp.start(jnp.concatenate([sums, mass, jnp.zeros((6, LANES), F32)], axis=0))

    def pass_on(self):
        self.sq_head.start(self.sq_dp.total())

    def apply(self):
        heads = self.sq_head.buffer.shape[0]
        total = self.sq_head.total()
        mean = total[1:2] * (1.0 / (D * heads))
        rms = jnp.sqrt(total[0:1] * mean * (1.0 / (D * D)))
        rate = STEP_RATE * jnp.sqrt(mean) / jnp.maximum(1.0, rms)
        for k in range(MATS):
            new = self.weights[k] - rate[:, k : k + 1] * self.upd[k]
            self.new_weights[k] = new
            self.copy[k] = new.astype(BF16)
            self.new_ema[k] = AVERAGE_KEEP * self.ema[k] + (1.0 - AVERAGE_KEEP) * new
        lanes = lax.broadcasted_iota(jnp.int32, (1, LANES), 1)
        clip = jnp.where(lanes < MATS, rms, self.small_clip[...])
        self.clip[...] = clip[:, 0 : self.clip.shape[1]]

    def small_step(self):
        count, full = self.small.shape[0], self.full
        g = jnp.concatenate([full[b // 2, b % 2, 0:count, :] for b in range(D // LANES)], axis=1)
        self.small_grads[...] = g
        state = SECOND_DECAY * self.small_state[...] + (1.0 - SECOND_DECAY) * (
            g * g + SQUARE_FLOOR
        )
        self.new_small_state[...] = state
        u = g * lax.rsqrt(state)
        rms = jnp.sqrt(jnp.sum(u * u, axis=1, keepdims=True) * (1.0 / D))
        new = self.small[...] - SMALL_RATE * u / jnp.maximum(1.0, rms)
        self.new_small[...] = new
        self.new_small_ema[...] = AVERAGE_KEEP * self.small_ema[...] + (1.0 - AVERAGE_KEEP) * new
        r = lax.broadcasted_iota(jnp.int32, (count, LANES), 0)
        c = lax.broadcasted_iota(jnp.int32, (count, LANES), 1)
        picked = jnp.where(c == r + MATS, rms, 0.0)
        self.small_clip[...] = jnp.sum(picked, axis=0, keepdims=True)


class Inputs(NamedTuple):
    cls: Any
    img: Any
    tokens: Any
    cot: Any
    weights: Any
    row_state: Any
    col_state: Any
    ema: Any
    small: Any
    small_state: Any
    small_ema: Any


class Outputs(NamedTuple):
    out: Any
    grad_in: Any
    wg: Any
    new_rows: Any
    new_cols: Any
    new_weights: Any
    copy: Any
    new_ema: Any
    small_grads: Any
    new_small_state: Any
    new_small: Any
    new_small_ema: Any
    clip: Any


def box_shapes(links, block):
    for slot in range(MATS):
        path = RS_ROUTES[slot]
        for phase, axis in enumerate(path):
            lead = [links.count(a) for a in AXES if a in path[phase + 1 :]]
            if axis == "h":
                lead = [links.far - 1, *lead]
            yield pltpu.VMEM((*lead, *block), BF16)


def shared_of(weights, parts, heads):
    links, (_, rows, _) = Links(), weights.shape
    block = (rows, LANES)
    every = pltpu.VMEM((2, 2, links.far, 2, 2, MATS, *block), BF16)
    out_rows = pltpu.VMEM((heads, HEAD_ROWS, D), BF16)
    dma = pltpu.SemaphoreType.DMA

    def f(*shape):
        return pltpu.VMEM(shape, F32)

    part = f(SMALL_ROWS, LANES)
    return dict(
        w=every,
        g=every,
        out_rows=out_rows,
        in_rows=out_rows,
        sums=f(SMALL_ROWS, D),
        parts=f(2, 2, SMALL_ROWS, LANES),
        in_c=f(2, SMALL_ROWS, LANES),
        in_x=part,
        in_y=part,
        in_h=f(links.far, SMALL_ROWS, LANES),
        in_l=part,
        full=f(2, 2, SMALL_ROWS, LANES),
        row_box=f(heads, 16, LANES),
        col_box=f(parts, 16, LANES),
        sq_dp_box=f(parts, SLOTS, LANES),
        sq_head_box=f(heads, SLOTS, LANES),
        upd=f(MATS, *block),
        small_clip=f(1, LANES),
        ag_send=dma((MATS, len(AXES))),
        ag_recv=dma((MATS, len(AXES))),
        rs_send=dma((MATS, len(AXES))),
        rs_recv=dma((MATS, len(AXES))),
        small_send=dma((7,)),
        small_recv=dma((7,)),
        out_send=dma((3,)),
        out_recv=dma((3,)),
        in_send=dma((3,)),
        in_recv=dma((3,)),
        opt_send=dma((4,)),
        opt_recv=dma((4,)),
    )


def block_kernel(names, *refs):
    r = types.SimpleNamespace(**dict(zip(names, refs)))
    boxes = refs[len(names) :]
    r.out_own = r.out_rows.at[lax.axis_index(HEAD)]
    r.in_own = r.in_rows.at[lax.axis_index(HEAD)]
    own = r.cls.shape[1] * CELLS
    blk = Block(vars(r))
    links = Links()
    gather = Gather(links, r.w, r.ag_send, r.ag_recv)
    scatter = Scatter(links, r.g, boxes, r.wg, r.rs_send, r.rs_recv)
    small = Small(
        links,
        *(r.sums, r.parts, r.in_c, r.in_x, r.in_y, r.in_h, r.in_l, r.full),
        r.small_send,
        r.small_recv,
    )
    out_rows = Rows(links, r.out_rows, r.out, own, r.out_send, r.out_recv)
    in_rows = Rows(links, r.in_rows, r.grad_in, own, r.in_send, r.in_recv)
    shares = [
        Exchange(links, axis, box, r.opt_send.at[i], r.opt_recv.at[i])
        for i, (axis, box) in enumerate(
            ((HEAD, r.row_box), (DP, r.col_box), (DP, r.sq_dp_box), (HEAD, r.sq_head_box))
        )
    ]
    opt = Adafactor(vars(r), *shares)

    for k in range(MATS):
        mine = links.region(r.w, SLOT_OF[k], "")
        mine[...] = r.weights[k].astype(BF16)
    links.greet()

    ops = []
    for tick in (gather.tick, scatter.tick):
        ops += [
            functools.partial(tick, slot, phase)
            for slot in range(MATS)
            for phase in range(len(AXES) + 1)
        ]
    ops += [blk.setup, blk.read_tokens, blk.norm_one, blk.read_cotangent]
    ops += [functools.partial(blk.project, k) for k in range(3)]
    ops += [blk.softmax, blk.contexts, blk.fill_window]
    ops += [functools.partial(blk.window_sum, c) for c in range(D // LANES)]
    ops += [blk.mix, blk.norm_two]
    for i in range(4):
        ops += [functools.partial(blk.hidden_block, i), functools.partial(blk.hidden_grads, i)]
    ops += [blk.finish_out, blk.back_two, blk.grad_proj, blk.back_heads, blk.back_query_key]
    ops += [functools.partial(blk.grad_of, k) for k in range(2)]
    ops += [functools.partial(blk.back_window, c) for c in range(D // LANES)]
    ops += [blk.back_value]
    ops += [functools.partial(blk.window_taps, c) for c in range(D // LANES)]
    ops += [blk.back_project, blk.back_one, blk.back_position, blk.position_taps, blk.finish_in]
    for rows in (out_rows, in_rows):
        ops += [functools.partial(rows.tick, stage) for stage in range(3)]
    ops += [functools.partial(small.tick, stage) for stage in range(8)]
    ops += [opt.small_step, opt.squares, opt.scale, opt.pass_on, opt.apply]
    for i in ORDER:
        ops[i]()
    for transfer in (gather, scatter, small, out_rows, in_rows, *shares):
        transfer.sent()


def local(
    tokens,
    cotangent,
    crop_image,
    crop_class,
    weights,
    row_state,
    col_state,
    weights_ema,
    small_params,
    small_state,
    small_ema,
):
    parts, heads = lax.axis_size(DP), lax.axis_size(HEAD)
    smem = pl.BlockSpec(memory_space=pltpu.SMEM)
    vmem = pl.BlockSpec(memory_space=pltpu.VMEM)
    shared = shared_of(weights, parts, heads)
    own = scratch_of()

    def like(x, dtype=None):
        return jax.ShapeDtypeStruct(x.shape, dtype or x.dtype)

    clips = weights.shape[0] + small_params.shape[0]
    outs = (
        like(tokens),
        like(tokens),
        like(weights),
        like(row_state),
        like(col_state),
        like(weights),
        like(weights, BF16),
        like(weights),
        like(small_params),
        like(small_params),
        like(small_params),
        like(small_params),
        jax.ShapeDtypeStruct((1, clips), F32),
    )
    names = (*Inputs._fields, *Outputs._fields, *shared, *own)
    res = pl.pallas_call(
        functools.partial(block_kernel, names),
        out_shape=outs,
        in_specs=[smem, smem] + [vmem] * 9,
        out_specs=(vmem,) * len(outs),
        scratch_shapes=[
            *shared.values(),
            *own.values(),
            *box_shapes(Links(), weights.shape[1:]),
        ],
        compiler_params=pltpu.CompilerParams(
            collective_id=0, has_side_effects=True, vmem_limit_bytes=63 << 20
        ),
        name="block",
    )(
        crop_class,
        crop_image,
        tokens,
        cotangent,
        weights,
        row_state,
        col_state,
        weights_ema,
        small_params,
        small_state,
        small_ema,
    )
    return (*res[:-1], res[-1].reshape(clips))


def solution(mesh):
    in_specs = (
        P(DP, None),
        P(DP, None),
        P(DP, None),
        P(DP, None),
        P(None, DP, HEAD),
        P(None, DP),
        P(None, HEAD),
        P(None, DP, HEAD),
        P(),
        P(),
        P(),
    )
    out_specs = (
        P(DP, None),
        P(DP, None),
        P(None, DP, HEAD),
        P(None, DP),
        P(None, HEAD),
        P(None, DP, HEAD),
        P(None, DP, HEAD),
        P(None, DP, HEAD),
        P(),
        P(),
        P(),
        P(),
        P(),
    )
    return jax.shard_map(local, mesh=mesh, in_specs=in_specs, out_specs=out_specs, check_vma=False)
```

time: 143 us -> 110 us (0.77)
  Pallas kernels: 131 us -> 98.1 us
    pallas_call x1, Pallas kernels: 131 us -> 98.1 us  [local(): pl.pallas_call(functools.partial(block_kernel, names), out_shape=outs, in...]
where the time goes in v4:
time: 110 us
  Pallas kernels  98.1 us (89%)
  local copies, waits for them, and re-layouts  10.9 us (10%)
    pallas_call x1, Pallas kernels, local(): pl.pallas_call(functools.partial(block_kernel, names), out_shape=outs, in...  98.1 us
    unnamed x37, local copies, waits for them, and re-layouts  10.9 us

profile of v4, /device:TPU:0, one launch (start us, length us, event | category | flops | bytes accessed | tf_op | source)
XLA Modules:
  0.0 109.7 jit_solution(6952761596625149488)
XLA Ops:
  0.6 98.1 %block.1 = (bf16[1176,512]{1,0:T(8,128)(2,1)}, bf16[1176,512]{1,0:T(8,128)(2,1)}, f32[12,64,128]{2,1,0:T(8,128)}, f32[12,64]{1,0:T(8,128)}, f32[12,128]{1,0:T(8,...) custom-call(s32[4,6]{1,0:T(4,128)} %refs_0_.1, ...), custom_call_target="tpu_custom_call" | custom-call | tf_op jit(solution)/shard_map/block/pallas_call | solution.py:1242
  98.7 0.0 copy-start
  98.8 2.5 %copy.37 = bf16[1176,512]{1,0:T(8,128)(2,1)} copy(bf16[1176,512]{1,0:T(8,128)(2,1)} %get-tuple-element.52) | data formatting | bytes 2408448
  101.2 0.0 copy-done
  101.2 0.0 copy-start.2
  101.2 1.0 copy.38
  102.3 0.1 copy-done.3
  102.4 0.7 copy.39
  103.2 0.0 copy-done.10
  103.2 0.6 copy.40
  103.8 0.0 copy-done.9
  103.8 0.6 copy.41
  104.4 0.7 copy.42
  105.1 0.0 copy-done.4
  105.1 0.7 copy.43
  105.8 0.7 copy.44
  106.6 0.0 copy-done.8
  106.6 0.7 copy.45
  107.2 0.7 copy.46
  107.9 0.0 copy-done.6
  107.9 0.7 copy.47
  108.6 0.7 copy.48
  109.2 0.0 copy-done.11
  109.2 0.5 copy.49
  (14 shorter events, 0.0 us)
Async XLA Ops:
  98.7 2.5 %copy-start = (bf16[1176,512]{1,0:T(8,128)(2,1)S(1)}, bf16[1176,512]{1,0:T(8,128)(2,1)}, u32[]{:S(2)}) copy-start(bf16[1176,512]{1,0:T(8,128)(2,1)} %get-tuple-element.53) | copy-start | bytes 3612676
  101.2 1.2 %copy-start.3 = (f32[12,64,128]{2,1,0:T(8,128)S(1)}, f32[12,64,128]{2,1,0:T(8,128)}, u32[]{:S(2)}) copy-start(f32[12,64,128]{2,1,0:T(8,128)} %get-tuple-element.54) | copy-start | bytes 1179652
  101.2 1.9 %copy-start.10 = (f32[12,64]{1,0:T(8,128)S(1)}, f32[12,64]{1,0:T(8,128)}, u32[]{:S(2)}) copy-start(f32[12,64]{1,0:T(8,128)} %get-tuple-element.55) | copy-start | bytes 9220
  101.2 2.5 %copy-start.9 = (f32[12,128]{1,0:T(8,128)S(1)}, f32[12,128]{1,0:T(8,128)}, u32[]{:S(2)}) copy-start(f32[12,128]{1,0:T(8,128)} %get-tuple-element.56) | copy-start | bytes 18436
  101.2 3.1 %copy-start.2 = (f32[12,64,128]{2,1,0:T(8,128)S(1)}, f32[12,64,128]{2,1,0:T(8,128)}, u32[]{:S(2)}) copy-start(f32[12,64,128]{2,1,0:T(8,128)} %get-tuple-element.57) | copy-start | bytes 1179652
  102.4 2.7 %copy-start.4 = (bf16[12,64,128]{2,1,0:T(8,128)(2,1)S(1)}, bf16[12,64,128]{2,1,0:T(8,128)(2,1)}, u32[]{:S(2)}) copy-start(bf16[12,64,128]{2,1,0:T(8,128)(2,1)} %get-tuple-element.58) | copy-start | bytes 589828
  102.4 3.4 %copy-start.1 = (f32[12,64,128]{2,1,0:T(8,128)S(1)}, f32[12,64,128]{2,1,0:T(8,128)}, u32[]{:S(2)}) copy-start(f32[12,64,128]{2,1,0:T(8,128)} %get-tuple-element.59) | copy-start | bytes 1179652
  102.4 4.1 %copy-start.8 = (f32[71,512]{1,0:T(8,128)S(1)}, f32[71,512]{1,0:T(8,128)}, u32[]{:S(2)}) copy-start(f32[71,512]{1,0:T(8,128)} %get-tuple-element.60) | copy-start | bytes 436228
  103.2 4.1 %copy-start.7 = (f32[71,512]{1,0:T(8,128)S(1)}, f32[71,512]{1,0:T(8,128)}, u32[]{:S(2)}) copy-start(f32[71,512]{1,0:T(8,128)} %get-tuple-element.61) | copy-start | bytes 436228
  104.4 3.5 %copy-start.6 = (f32[71,512]{1,0:T(8,128)S(1)}, f32[71,512]{1,0:T(8,128)}, u32[]{:S(2)}) copy-start(f32[71,512]{1,0:T(8,128)} %get-tuple-element.62) | copy-start | bytes 436228
  105.1 3.4 %copy-start.5 = (f32[71,512]{1,0:T(8,128)S(1)}, f32[71,512]{1,0:T(8,128)}, u32[]{:S(2)}) copy-start(f32[71,512]{1,0:T(8,128)} %get-tuple-element.63) | copy-start | bytes 436228
  105.1 4.1 %copy-start.11 = (f32[1,83]{1,0:T(1,128)S(1)}, f32[1,83]{1,0:T(1,128)}, u32[]{:S(2)}) copy-start(f32[1,83]{1,0:T(1,128)} %get-tuple-element.38) | copy-start | bytes 1000

commit v5 on v4

--- a/solution.py
+++ b/solution.py
@@ -11,6 +11,7 @@
 from jax.sharding import PartitionSpec as P
 
 DP, HEAD = "dp", "head"
+ALL = (DP, HEAD)
 D = 512
 HEAD_DIM = 64
 GRID = 7
@@ -608,20 +609,20 @@
 AXES = "xchly"
 HEAD_ROWS = 320
 SMALL_ROWS = 72
-AG_ROUTES = ("hlxyc", "lyhxc", "hlxyc", "hlyxc", "xyhlc", "xhlyc", "yhlxc", "lyhxc", "hlxyc", "xhylc", "hlxyc", "lxyhc")
-RS_ROUTES = ("cylhx", "clyxh", "cyxlh", "clxyh", "cyxhl", "cxylh", "clhxy", "cxylh", "cylxh", "cxylh", "cyxlh", "cxylh")
+AG_ROUTES = ("lhyxc", "hlxyc", "lhyxc", "hxlyc", "hlxyc", "xylhc", "hylxc", "hylxc", "lxhyc", "xyhlc", "lhxyc", "xylhc")
+RS_ROUTES = ("cxylh", "clyhx", "cxylh", "cyhlx", "cxyhl", "clhyx", "cylxh", "cxylh", "cyxhl", "chlyx", "clyxh", "cylhx")
 ORDER = (
-    30, 6, 12, 0, 18, 24, 36, 42, 48, 54, 60, 66, 144, 145, 31, 7, 146, 13, 1, 19,
-    8, 25, 49, 37, 43, 55, 61, 67, 147, 32, 14, 26, 2, 44, 68, 20, 9, 50, 15, 38,
-    69, 3, 62, 56, 21, 33, 10, 27, 16, 51, 11, 149, 151, 4, 45, 39, 17, 150, 153, 157,
-    22, 156, 5, 148, 152, 34, 155, 28, 57, 23, 63, 46, 70, 154, 158, 159, 29, 52, 40, 47,
-    35, 160, 161, 58, 53, 64, 71, 102, 96, 41, 162, 163, 59, 164, 65, 108, 103, 97, 114, 165,
-    166, 120, 167, 132, 126, 138, 109, 115, 168, 121, 133, 98, 127, 104, 139, 189, 169, 171, 177, 178,
-    176, 172, 175, 170, 179, 184, 84, 173, 174, 90, 72, 78, 122, 185, 85, 187, 91, 73, 183, 79,
-    181, 180, 128, 123, 110, 134, 140, 99, 186, 86, 105, 188, 92, 192, 116, 182, 74, 195, 135, 124,
-    80, 129, 87, 190, 196, 141, 111, 93, 106, 117, 100, 191, 75, 81, 136, 94, 125, 130, 88, 142,
-    107, 118, 101, 193, 197, 76, 112, 137, 82, 95, 194, 131, 77, 89, 198, 113, 143, 119, 83, 204,
-    199, 205, 200, 201, 206, 202, 203, 207,
+    6, 12, 0, 66, 18, 30, 42, 48, 36, 60, 54, 24, 144, 147, 145, 13, 31, 7, 55, 1,
+    146, 19, 25, 49, 37, 43, 61, 67, 32, 8, 56, 14, 2, 20, 26, 38, 50, 44, 62, 68,
+    9, 33, 15, 27, 57, 3, 21, 63, 39, 10, 16, 51, 45, 11, 149, 151, 69, 17, 4, 150,
+    153, 154, 156, 155, 22, 28, 157, 5, 34, 148, 152, 40, 158, 23, 159, 46, 29, 64, 58, 35,
+    160, 161, 52, 96, 102, 41, 47, 162, 70, 163, 108, 59, 65, 114, 53, 164, 97, 165, 126, 120,
+    103, 71, 166, 109, 115, 167, 127, 132, 138, 168, 189, 121, 169, 133, 98, 170, 90, 171, 139, 172,
+    173, 72, 110, 181, 174, 78, 91, 177, 180, 183, 128, 134, 104, 73, 175, 79, 99, 176, 111, 116,
+    122, 178, 179, 84, 140, 184, 185, 129, 186, 85, 92, 190, 187, 105, 182, 135, 195, 112, 74, 188,
+    80, 191, 130, 117, 196, 123, 192, 100, 106, 141, 86, 75, 136, 93, 131, 118, 113, 81, 197, 101,
+    124, 87, 76, 142, 94, 137, 198, 119, 125, 88, 82, 77, 193, 107, 199, 143, 95, 83, 89, 204,
+    194, 200, 205, 201, 202, 203, 206, 207,
 )
 
 
@@ -699,7 +700,7 @@
         self.repeat(self.count(axis), do)
 
     def repeat(self, size, do):
-        if size <= 8:
+        if size <= 32:
             for step in range(1, size):
                 do(step)
         else:
@@ -711,25 +712,32 @@
             lax.fori_loop(1, size, body, 0)
 
     def others(self, name, do):
-        index = {DP: lax.axis_index(DP), HEAD: lax.axis_index(HEAD)}
+        dp, head, heads = lax.axis_index(DP), lax.axis_index(HEAD), lax.axis_size(HEAD)
 
         def one(step):
-            at = {**index, name: lax.rem(index[name] + step, lax.axis_size(name))}
-            do(step, (at[DP], at[HEAD]))
+            if name == ALL:
+                i = lax.rem(dp * heads + head + step, lax.axis_size(ALL))
+                do((i // heads, lax.rem(i, heads)))
+            elif name == DP:
+                do((lax.rem(dp + step, lax.axis_size(DP)), head))
+            else:
+                do((dp, lax.rem(head + step, heads)))
 
         self.repeat(lax.axis_size(name), one)
 
-    def greet(self):
-        barrier = pltpu.get_barrier_semaphore()
-
-        def signal(step, device):
+    def signal(self):
+        def one(device):
             pl.semaphore_signal(
-                barrier, inc=1, device_id=device, device_id_type=pl.DeviceIdType.MESH
+                pltpu.get_barrier_semaphore(),
+                inc=1,
+                device_id=device,
+                device_id_type=pl.DeviceIdType.MESH,
             )
 
-        self.others(HEAD, signal)
-        self.others(DP, signal)
-        pl.semaphore_wait(barrier, lax.axis_size(HEAD) + lax.axis_size(DP) - 2)
+        self.others(ALL, one)
+
+    def meet(self):
+        pl.semaphore_wait(pltpu.get_barrier_semaphore(), lax.axis_size(ALL) - 1)
 
     def copy(self, src, dst, send, recv, device):
         return pltpu.make_async_remote_copy(
@@ -948,7 +956,7 @@
         mine = self.buffer.at[own]
         self.links.others(
             self.name,
-            lambda step, device: self.links.copy(mine, mine, self.send, self.recv, device).start(),
+            lambda device: self.links.copy(mine, mine, self.send, self.recv, device).start(),
         )
 
     def descriptor(self):
@@ -970,10 +978,9 @@
 
 
 class Adafactor:
-    def __init__(self, refs, row_share, col_share, sq_dp, sq_head):
+    def __init__(self, refs, row_share, col_share, sq_share):
         self.__dict__.update(refs)
-        self.row_share, self.col_share = row_share, col_share
-        self.sq_dp, self.sq_head = sq_dp, sq_head
+        self.row_share, self.col_share, self.sq_share = row_share, col_share, sq_share
 
     def eye(self, count):
         r = lax.broadcasted_iota(jnp.int32, (count, LANES), 0)
@@ -1015,15 +1022,11 @@
             s = jnp.sum(jnp.sum(u * u, axis=0, keepdims=True), axis=1, keepdims=True)
             sums = self.lane(k, s, sums)
         mass = jnp.sum(row, axis=0, keepdims=True)
-        self.sq_dp.start(jnp.concatenate([sums, mass, jnp.zeros((6, LANES), F32)], axis=0))
-
-    def pass_on(self):
-        self.sq_head.start(self.sq_dp.total())
+        self.sq_share.start(jnp.concatenate([sums, mass], axis=0))
 
     def apply(self):
-        heads = self.sq_head.buffer.shape[0]
-        total = self.sq_head.total()
-        mean = total[1:2] * (1.0 / (D * heads))
+        total = self.sq_share.total()
+        mean = total[1:2] * (1.0 / (D * lax.axis_size(HEAD)))
         rms = jnp.sqrt(total[0:1] * mean * (1.0 / (D * D)))
         rate = STEP_RATE * jnp.sqrt(mean) / jnp.maximum(1.0, rms)
         for k in range(MATS):
@@ -1031,8 +1034,11 @@
             self.new_weights[k] = new
             self.copy[k] = new.astype(BF16)
             self.new_ema[k] = AVERAGE_KEEP * self.ema[k] + (1.0 - AVERAGE_KEEP) * new
+        self.rms[...] = rms
+
+    def clips(self):
         lanes = lax.broadcasted_iota(jnp.int32, (1, LANES), 1)
-        clip = jnp.where(lanes < MATS, rms, self.small_clip[...])
+        clip = jnp.where(lanes < MATS, self.rms[...], self.small_clip[...])
         self.clip[...] = clip[:, 0 : self.clip.shape[1]]
 
     def small_step(self):
@@ -1120,10 +1126,10 @@
         full=f(2, 2, SMALL_ROWS, LANES),
         row_box=f(heads, 16, LANES),
         col_box=f(parts, 16, LANES),
-        sq_dp_box=f(parts, SLOTS, LANES),
-        sq_head_box=f(heads, SLOTS, LANES),
+        sq_box=f(parts * heads, 2, LANES),
         upd=f(MATS, *block),
         small_clip=f(1, LANES),
+        rms=f(1, LANES),
         ag_send=dma((MATS, len(AXES))),
         ag_recv=dma((MATS, len(AXES))),
         rs_send=dma((MATS, len(AXES))),
@@ -1134,19 +1140,53 @@
         out_recv=dma((3,)),
         in_send=dma((3,)),
         in_recv=dma((3,)),
-        opt_send=dma((4,)),
-        opt_recv=dma((4,)),
+        opt_send=dma((3,)),
+        opt_recv=dma((3,)),
+        fetched=dma((len(Inputs._fields),)),
+        stored=dma((len(Outputs._fields),)),
     )
 
 
+class Ready:
+    def __init__(self, src, dst, sem):
+        self.copy = pltpu.make_async_copy(src, dst, sem)
+        self.start, self.wait = self.copy.start, self.copy.wait
+
+
+def then(*steps):
+    def run():
+        for step in steps:
+            step()
+
+    return run
+
+
 def block_kernel(names, *refs):
+    n_in, n_out = len(Inputs._fields), len(Outputs._fields)
+    ins, outs, refs = Inputs(*refs[:n_in]), Outputs(*refs[n_in : n_in + n_out]), refs[n_in + n_out :]
     r = types.SimpleNamespace(**dict(zip(names, refs)))
+    r.cls, r.img = ins.cls, ins.img
+    fetch = Inputs(
+        *[
+            None if i < 2 else Ready(ref, getattr(r, name), r.fetched.at[i])
+            for i, (name, ref) in enumerate(zip(Inputs._fields, ins))
+        ]
+    )
+    store = Outputs(
+        *[
+            Ready(getattr(r, name), ref, r.stored.at[i])
+            for i, (name, ref) in enumerate(zip(Outputs._fields, outs))
+        ]
+    )
     boxes = refs[len(names) :]
+    links = Links()
+    links.signal()
+    for one in (fetch.weights, fetch.small, fetch.tokens, fetch.cot, *fetch[5:8], *fetch[9:]):
+        one.start()
     r.out_own = r.out_rows.at[lax.axis_index(HEAD)]
     r.in_own = r.in_rows.at[lax.axis_index(HEAD)]
     own = r.cls.shape[1] * CELLS
     blk = Block(vars(r))
-    links = Links()
     gather = Gather(links, r.w, r.ag_send, r.ag_recv)
     scatter = Scatter(links, r.g, boxes, r.wg, r.rs_send, r.rs_recv)
     small = Small(
@@ -1159,16 +1199,15 @@
     in_rows = Rows(links, r.in_rows, r.grad_in, own, r.in_send, r.in_recv)
     shares = [
         Exchange(links, axis, box, r.opt_send.at[i], r.opt_recv.at[i])
-        for i, (axis, box) in enumerate(
-            ((HEAD, r.row_box), (DP, r.col_box), (DP, r.sq_dp_box), (HEAD, r.sq_head_box))
-        )
+        for i, (axis, box) in enumerate(((HEAD, r.row_box), (DP, r.col_box), (ALL, r.sq_box)))
     ]
     opt = Adafactor(vars(r), *shares)
 
+    fetch.weights.wait()
     for k in range(MATS):
         mine = links.region(r.w, SLOT_OF[k], "")
         mine[...] = r.weights[k].astype(BF16)
-    links.greet()
+    links.meet()
 
     ops = []
     for tick in (gather.tick, scatter.tick):
@@ -1177,7 +1216,12 @@
             for slot in range(MATS)
             for phase in range(len(AXES) + 1)
         ]
-    ops += [blk.setup, blk.read_tokens, blk.norm_one, blk.read_cotangent]
+    ops += [
+        then(fetch.small.wait, blk.setup),
+        then(fetch.tokens.wait, blk.read_tokens),
+        blk.norm_one,
+        then(fetch.cot.wait, blk.read_cotangent),
+    ]
     ops += [functools.partial(blk.project, k) for k in range(3)]
     ops += [blk.softmax, blk.contexts, blk.fill_window]
     ops += [functools.partial(blk.window_sum, c) for c in range(D // LANES)]
@@ -1190,14 +1234,53 @@
     ops += [blk.back_value]
     ops += [functools.partial(blk.window_taps, c) for c in range(D // LANES)]
     ops += [blk.back_project, blk.back_one, blk.back_position, blk.position_taps, blk.finish_in]
-    for rows in (out_rows, in_rows):
-        ops += [functools.partial(rows.tick, stage) for stage in range(3)]
+    for rows, done in ((out_rows, store.out), (in_rows, store.grad_in)):
+        ops += [functools.partial(rows.tick, stage) for stage in range(2)]
+        ops += [then(functools.partial(rows.tick, 2), done.start)]
     ops += [functools.partial(small.tick, stage) for stage in range(8)]
-    ops += [opt.small_step, opt.squares, opt.scale, opt.pass_on, opt.apply]
+    ops += [
+        then(
+            fetch.small_state.wait,
+            fetch.small_ema.wait,
+            opt.small_step,
+            store.small_grads.start,
+            store.new_small_state.start,
+            store.new_small.start,
+            store.new_small_ema.start,
+        ),
+        then(store.wg.start, opt.squares),
+        then(
+            fetch.row_state.wait,
+            fetch.col_state.wait,
+            opt.scale,
+            store.new_rows.start,
+            store.new_cols.start,
+        ),
+        then(
+            fetch.ema.wait,
+            opt.apply,
+            store.new_weights.start,
+            store.copy.start,
+            store.new_ema.start,
+        ),
+        then(opt.clips, store.clip.start),
+    ]
     for i in ORDER:
         ops[i]()
     for transfer in (gather, scatter, small, out_rows, in_rows, *shares):
         transfer.sent()
+    for one in store:
+        one.wait()
+
+
+def finish_kernel(count, *refs):
+    copies = [
+        pltpu.make_async_copy(refs[i], refs[count + i], refs[-1].at[i]) for i in range(count)
+    ]
+    for one in copies:
+        one.start()
+    for one in copies:
+        one.wait()
 
 
 def local(
@@ -1215,7 +1298,6 @@
 ):
     parts, heads = lax.axis_size(DP), lax.axis_size(HEAD)
     smem = pl.BlockSpec(memory_space=pltpu.SMEM)
-    vmem = pl.BlockSpec(memory_space=pltpu.VMEM)
     shared = shared_of(weights, parts, heads)
     own = scratch_of()
 
@@ -1238,22 +1320,7 @@
         like(small_params),
         jax.ShapeDtypeStruct((1, clips), F32),
     )
-    names = (*Inputs._fields, *Outputs._fields, *shared, *own)
-    res = pl.pallas_call(
-        functools.partial(block_kernel, names),
-        out_shape=outs,
-        in_specs=[smem, smem] + [vmem] * 9,
-        out_specs=(vmem,) * len(outs),
-        scratch_shapes=[
-            *shared.values(),
-            *own.values(),
-            *box_shapes(Links(), weights.shape[1:]),
-        ],
-        compiler_params=pltpu.CompilerParams(
-            collective_id=0, has_side_effects=True, vmem_limit_bytes=63 << 20
-        ),
-        name="block",
-    )(
+    args = Inputs(
         crop_class,
         crop_image,
         tokens,
@@ -1266,6 +1333,33 @@
         small_state,
         small_ema,
     )
+    staged = [pltpu.VMEM(x.shape, x.dtype) for x in (*args[2:], *outs)]
+    names = (*shared, *own, *Inputs._fields[2:], *Outputs._fields)
+    far = pl.BlockSpec(memory_space=pl.ANY)
+    res = pl.pallas_call(
+        functools.partial(block_kernel, names),
+        out_shape=outs,
+        in_specs=[smem, smem] + [far] * 9,
+        out_specs=(far,) * len(outs),
+        scratch_shapes=[
+            *shared.values(),
+            *own.values(),
+            *staged,
+            *box_shapes(Links(), weights.shape[1:]),
+        ],
+        compiler_params=pltpu.CompilerParams(
+            collective_id=0, has_side_effects=True, vmem_limit_bytes=63 << 20
+        ),
+        name="block",
+    )(*args)
+    res = pl.pallas_call(
+        functools.partial(finish_kernel, len(outs)),
+        out_shape=outs,
+        in_specs=[far] * len(outs),
+        out_specs=(far,) * len(outs),
+        scratch_shapes=[pltpu.SemaphoreType.DMA((len(outs),))],
+        name="finish",
+    )(*res)
     return (*res[:-1], res[-1].reshape(clips))
 
 

time: 110 us -> 225 us (2.05)
  Pallas kernels: 98.1 us -> 224 us
  local copies, waits for them, and re-layouts: 10.9 us -> 0 us
    pallas_call x0 -> x1, Pallas kernels: none -> 134 us  [local(): pl.pallas_call(functools.partial(finish_kernel, len(outs)), out_shape=out...]
    unnamed x37 -> x0, local copies, waits for them, and re-layouts: 10.9 us -> none
    pallas_call x1, Pallas kernels: 98.1 us -> 90 us  [local(): pl.pallas_call(functools.partial(block_kernel, names), out_shape=outs, in...]
where the time goes in v5:
time: 225 us
  Pallas kernels  224 us (100%)
    pallas_call x1, Pallas kernels, local(): pl.pallas_call(functools.partial(finish_kernel, len(outs)), out_shape=out...  134 us
    pallas_call x1, Pallas kernels, local(): pl.pallas_call(functools.partial(block_kernel, names), out_shape=outs, in...  90 us

profile of v5, /device:TPU:0, one launch (start us, length us, event | category | flops | bytes accessed | tf_op | source)
XLA Modules:
  0.0 224.9 jit_solution(17647769774560313895)
XLA Ops:
  0.6 90.0 %block.1 = (bf16[1176,512]{1,0:T(8,128)(2,1)}, bf16[1176,512]{1,0:T(8,128)(2,1)}, f32[12,64,128]{2,1,0:T(8,128)}, f32[12,64]{1,0:T(8,128)}, f32[12,128]{1,0:T(8,...) custom-call(s32[4,6]{1,0:T(4,128)} %refs_0_.1, ...), custom_call_target="tpu_custom_call" | custom-call | tf_op jit(solution)/shard_map/block/pallas_call | solution.py:1339
  90.6 134.1 %finish.1 = (bf16[1176,512]{1,0:T(8,128)(2,1)}, bf16[1176,512]{1,0:T(8,128)(2,1)}, f32[12,64,128]{2,1,0:T(8,128)}, f32[12,64]{1,0:T(8,128)}, f32[12,128]{1,0:T(8...) custom-call(bf16[1176,512]{1,0:T(8,128)(2,1)} %get-tuple-element.39., ...), custom_call_target="tpu_custom_call" | custom-call | tf_op jit(solution)/shard_map/finish/pallas_call | solution.py:1355

commit v6 on v5

--- a/solution.py
+++ b/solution.py
@@ -1274,12 +1274,16 @@
 
 
 def finish_kernel(count, *refs):
-    copies = [
-        pltpu.make_async_copy(refs[i], refs[count + i], refs[-1].at[i]) for i in range(count)
-    ]
-    for one in copies:
+    ins, outs, held = refs[:count], refs[count : 2 * count], refs[2 * count : 3 * count]
+    took, gave = refs[3 * count :]
+    come = [pltpu.make_async_copy(a, b, took.at[i]) for i, (a, b) in enumerate(zip(ins, held))]
+    leave = [pltpu.make_async_copy(a, b, gave.at[i]) for i, (a, b) in enumerate(zip(held, outs))]
+    for one in come:
         one.start()
-    for one in copies:
+    for one, other in zip(come, leave):
+        one.wait()
+        other.start()
+    for one in leave:
         one.wait()
 
 
@@ -1357,7 +1361,12 @@
         out_shape=outs,
         in_specs=[far] * len(outs),
         out_specs=(far,) * len(outs),
-        scratch_shapes=[pltpu.SemaphoreType.DMA((len(outs),))],
+        scratch_shapes=[
+            *[pltpu.VMEM(x.shape, x.dtype) for x in outs],
+            pltpu.SemaphoreType.DMA((len(outs),)),
+            pltpu.SemaphoreType.DMA((len(outs),)),
+        ],
+        compiler_params=pltpu.CompilerParams(vmem_limit_bytes=32 << 20),
         name="finish",
     )(*res)
     return (*res[:-1], res[-1].reshape(clips))

time: 225 us -> 108 us (0.48)
  Pallas kernels: 224 us -> 94.7 us
  local copies, waits for them, and re-layouts: 0 us -> 12.1 us
    pallas_call x1, Pallas kernels: 134 us -> 4.73 us  [local(): pl.pallas_call(functools.partial(finish_kernel, len(outs)), out_shape=out...]
    unnamed x0 -> x26, local copies, waits for them, and re-layouts: none -> 12.1 us
where the time goes in v6:
time: 108 us
  Pallas kernels  94.7 us (88%)
  local copies, waits for them, and re-layouts  12.1 us (11%)
    pallas_call x1, Pallas kernels, local(): pl.pallas_call(functools.partial(block_kernel, names), out_shape=outs, in...  90 us
    unnamed x26, local copies, waits for them, and re-layouts  12.1 us
    pallas_call x1, Pallas kernels, local(): pl.pallas_call(functools.partial(finish_kernel, len(outs)), out_shape=out...  4.73 us

profile of v6, /device:TPU:0, one launch (start us, length us, event | category | flops | bytes accessed | tf_op | source)
XLA Modules:
  0.0 107.7 jit_solution(2138880241245607056)
XLA Ops:
  0.6 90.0 %block.1 = (bf16[1176,512]{1,0:T(8,128)(2,1)}, bf16[1176,512]{1,0:T(8,128)(2,1)}, f32[12,64,128]{2,1,0:T(8,128)}, f32[12,64]{1,0:T(8,128)}, f32[12,128]{1,0:T(8,...) custom-call(s32[4,6]{1,0:T(4,128)} %refs_0_.1, ...), custom_call_target="tpu_custom_call" | custom-call | tf_op jit(solution)/shard_map/block/pallas_call | solution.py:1343
  90.6 0.0 copy-start
  90.7 1.3 %copy-done = bf16[1176,512]{1,0:T(8,128)(2,1)S(1)} copy-done((bf16[1176,512]{1,0:T(8,128)(2,1)S(1)}, bf16[1176,512]{1,0:T(8,128)(2,1)}, u32[]{:S(2)}) %copy-start) | copy-done | bytes 1204248
  91.9 0.0 copy-start.1
  91.9 1.3 %copy-done.1 = bf16[1176,512]{1,0:T(8,128)(2,1)S(1)} copy-done((bf16[1176,512]{1,0:T(8,128)(2,1)S(1)}, bf16[1176,512]{1,0:T(8,128)(2,1)}, u32[]{:S(2)}) %copy-start.1) | copy-done | bytes 1204248
  93.2 0.0 copy-start.2
  93.2 1.0 copy-done.2
  94.2 0.0 copy-start.3
  94.2 1.0 copy-done.3
  95.2 0.0 copy-start.4
  95.2 1.0 copy-done.4
  96.2 0.0 copy-start.5
  96.2 0.9 copy-done.5
  97.1 0.0 copy-start.6
  97.1 0.9 copy-done.6
  98.0 0.0 copy-start.7
  98.0 0.9 copy-done.7
  98.9 0.0 copy-start.8
  98.9 0.9 copy-done.8
  99.8 0.9 copy-done.9
  100.8 0.7 copy-done.10
  101.5 0.7 copy-done.11
  102.2 0.6 copy-done.12
  102.8 4.7 %finish.1 = (bf16[1176,512]{1,0:T(8,128)(2,1)}, bf16[1176,512]{1,0:T(8,128)(2,1)}, f32[12,64,128]{2,1,0:T(8,128)}, f32[12,64]{1,0:T(8,128)}, f32[12,128]{1,0:T(8...) custom-call(bf16[1176,512]{1,0:T(8,128)(2,1)S(1)} %copy-done, ...), custom_call_target="tpu_custom_call" | custom-call | tf_op jit(solution)/shard_map/finish/pallas_call | solution.py:1359
  (4 shorter events, 0.0 us)
Async XLA Ops:
  90.6 1.3 %copy-start = (bf16[1176,512]{1,0:T(8,128)(2,1)S(1)}, bf16[1176,512]{1,0:T(8,128)(2,1)}, u32[]{:S(2)}) copy-start(bf16[1176,512]{1,0:T(8,128)(2,1)} %get-tuple-element.39.refs_0_) | copy-start | bytes 3612676
  91.9 1.3 %copy-start.1 = (bf16[1176,512]{1,0:T(8,128)(2,1)S(1)}, bf16[1176,512]{1,0:T(8,128)(2,1)}, u32[]{:S(2)}) copy-start(bf16[1176,512]{1,0:T(8,128)(2,1)} %get-tuple-element.40.refs_1_) | copy-start | bytes 3612676
  93.2 1.0 copy-start.2
  94.2 1.0 copy-start.3
  95.2 1.0 copy-start.4
  96.2 0.9 copy-start.5
  97.1 0.9 copy-start.6
  98.0 0.9 copy-start.7
  98.9 0.9 copy-start.8
  99.8 0.9 copy-start.9
  100.8 0.7 copy-start.10
  101.5 0.7 copy-start.11
  102.2 0.6 copy-start.12

commit v7 on v6

--- a/solution.py
+++ b/solution.py
@@ -1339,7 +1339,7 @@
     )
     staged = [pltpu.VMEM(x.shape, x.dtype) for x in (*args[2:], *outs)]
     names = (*shared, *own, *Inputs._fields[2:], *Outputs._fields)
-    far = pl.BlockSpec(memory_space=pl.ANY)
+    far = pl.BlockSpec(memory_space=pltpu.HBM)
     res = pl.pallas_call(
         functools.partial(block_kernel, names),
         out_shape=outs,

time: 108 us -> 108 us (level)
  no operation moved by 1% of the time
where the time goes in v7:
time: 108 us
  Pallas kernels  94.7 us (88%)
  local copies, waits for them, and re-layouts  12.1 us (11%)
    pallas_call x1, Pallas kernels, local(): pl.pallas_call(functools.partial(block_kernel, names), out_shape=outs, in...  90 us
    unnamed x26, local copies, waits for them, and re-layouts  12.1 us
    pallas_call x1, Pallas kernels, local(): pl.pallas_call(functools.partial(finish_kernel, len(outs)), out_shape=out...  4.73 us

profile of v7, /device:TPU:0, one launch (start us, length us, event | category | flops | bytes accessed | tf_op | source)
XLA Modules:
  0.0 107.7 jit_solution(2138880241245607056)
XLA Ops:
  0.6 90.0 %block.1 = (bf16[1176,512]{1,0:T(8,128)(2,1)}, bf16[1176,512]{1,0:T(8,128)(2,1)}, f32[12,64,128]{2,1,0:T(8,128)}, f32[12,64]{1,0:T(8,128)}, f32[12,128]{1,0:T(8,...) custom-call(s32[4,6]{1,0:T(4,128)} %refs_0_.1, ...), custom_call_target="tpu_custom_call" | custom-call | tf_op jit(solution)/shard_map/block/pallas_call | solution.py:1343
  90.6 0.0 copy-start
  90.7 1.3 %copy-done = bf16[1176,512]{1,0:T(8,128)(2,1)S(1)} copy-done((bf16[1176,512]{1,0:T(8,128)(2,1)S(1)}, bf16[1176,512]{1,0:T(8,128)(2,1)}, u32[]{:S(2)}) %copy-start) | copy-done | bytes 1204248
  91.9 0.0 copy-start.1
  91.9 1.3 %copy-done.1 = bf16[1176,512]{1,0:T(8,128)(2,1)S(1)} copy-done((bf16[1176,512]{1,0:T(8,128)(2,1)S(1)}, bf16[1176,512]{1,0:T(8,128)(2,1)}, u32[]{:S(2)}) %copy-start.1) | copy-done | bytes 1204248
  93.2 0.0 copy-start.2
  93.2 1.0 copy-done.2
  94.2 0.0 copy-start.3
  94.2 1.0 copy-done.3
  95.2 0.0 copy-start.4
  95.2 1.0 copy-done.4
  96.2 0.0 copy-start.5
  96.2 0.9 copy-done.5
  97.1 0.0 copy-start.6
  97.1 0.9 copy-done.6
  98.0 0.0 copy-start.7
  98.0 0.9 copy-done.7
  98.9 0.0 copy-start.8
  98.9 0.9 copy-done.8
  99.8 0.9 copy-done.9
  100.8 0.7 copy-done.10
  101.5 0.7 copy-done.11
  102.2 0.6 copy-done.12
  102.8 4.7 %finish.1 = (bf16[1176,512]{1,0:T(8,128)(2,1)}, bf16[1176,512]{1,0:T(8,128)(2,1)}, f32[12,64,128]{2,1,0:T(8,128)}, f32[12,64]{1,0:T(8,128)}, f32[12,128]{1,0:T(8...) custom-call(bf16[1176,512]{1,0:T(8,128)(2,1)S(1)} %copy-done, ...), custom_call_target="tpu_custom_call" | custom-call | tf_op jit(solution)/shard_map/finish/pallas_call | solution.py:1359
  (4 shorter events, 0.0 us)
Async XLA Ops:
  90.6 1.3 %copy-start = (bf16[1176,512]{1,0:T(8,128)(2,1)S(1)}, bf16[1176,512]{1,0:T(8,128)(2,1)}, u32[]{:S(2)}) copy-start(bf16[1176,512]{1,0:T(8,128)(2,1)} %get-tuple-element.39.refs_0_) | copy-start | bytes 3612676
  91.9 1.3 %copy-start.1 = (bf16[1176,512]{1,0:T(8,128)(2,1)S(1)}, bf16[1176,512]{1,0:T(8,128)(2,1)}, u32[]{:S(2)}) copy-start(bf16[1176,512]{1,0:T(8,128)(2,1)} %get-tuple-element.40.refs_1_) | copy-start | bytes 3612676
  93.2 1.0 copy-start.2
  94.2 1.0 copy-start.3
  95.2 1.0 copy-start.4
  96.2 0.9 copy-start.5
  97.1 0.9 copy-start.6
  98.0 0.9 copy-start.7
  98.9 0.9 copy-start.8
  99.8 0.9 copy-start.9
  100.8 0.7 copy-start.10
  101.5 0.7 copy-start.11
  102.2 0.6 copy-start.12

commit v8 on v7

--- a/solution.py
+++ b/solution.py
@@ -1366,7 +1366,7 @@
             pltpu.SemaphoreType.DMA((len(outs),)),
             pltpu.SemaphoreType.DMA((len(outs),)),
         ],
-        compiler_params=pltpu.CompilerParams(vmem_limit_bytes=32 << 20),
+        compiler_params=pltpu.CompilerParams(vmem_limit_bytes=63 << 20),
         name="finish",
     )(*res)
     return (*res[:-1], res[-1].reshape(clips))

time: 108 us -> 94.6 us (0.88)
  local copies, waits for them, and re-layouts: 12.1 us -> 0 us
  Pallas kernels: 94.7 us -> 93.6 us
    unnamed x26 -> x0, local copies, waits for them, and re-layouts: 12.1 us -> none
    pallas_call x1, Pallas kernels: 4.73 us -> 3.58 us  [local(): pl.pallas_call(functools.partial(finish_kernel, len(outs)), out_shape=out...]
where the time goes in v8:
time: 94.6 us; the launch traced here: 94.4 us
  Pallas kernels  93.6 us (99%)
    pallas_call x1, Pallas kernels, local(): pl.pallas_call(functools.partial(block_kernel, names), out_shape=outs, in...  90 us
    pallas_call x1, Pallas kernels, local(): pl.pallas_call(functools.partial(finish_kernel, len(outs)), out_shape=out...  3.58 us

profile of v8, /device:TPU:0, one launch (start us, length us, event | category | flops | bytes accessed | tf_op | source)
XLA Modules:
  0.0 94.4 jit_solution(7005860926536063569)
XLA Ops:
  0.6 90.0 %block.1 = (bf16[1176,512]{1,0:T(8,128)(2,1)}, bf16[1176,512]{1,0:T(8,128)(2,1)}, f32[12,64,128]{2,1,0:T(8,128)}, f32[12,64]{1,0:T(8,128)}, f32[12,128]{1,0:T(8,...) custom-call(s32[4,6]{1,0:T(4,128)} %refs_0_.1, ...), custom_call_target="tpu_custom_call" | custom-call | tf_op jit(solution)/shard_map/block/pallas_call | solution.py:1343
  90.6 3.6 %finish.1 = (bf16[1176,512]{1,0:T(8,128)(2,1)}, bf16[1176,512]{1,0:T(8,128)(2,1)}, f32[12,64,128]{2,1,0:T(8,128)}, f32[12,64]{1,0:T(8,128)}, f32[12,128]{1,0:T(8...) custom-call(bf16[1176,512]{1,0:T(8,128)(2,1)} %get-tuple-element.39., ...), custom_call_target="tpu_custom_call" | custom-call | tf_op jit(solution)/shard_map/finish/pallas_call | solution.py:1359

commit v9 on v8

--- a/solution.py
+++ b/solution.py
@@ -606,23 +606,41 @@
 
 SLOT_OF = (0, 1, 2, 3, 4, 6, 8, 10, 5, 7, 9, 11)
 MATS = len(SLOT_OF)
+EARLY = 4
 AXES = "xchly"
 HEAD_ROWS = 320
 SMALL_ROWS = 72
-AG_ROUTES = ("lhyxc", "hlxyc", "lhyxc", "hxlyc", "hlxyc", "xylhc", "hylxc", "hylxc", "lxhyc", "xyhlc", "lhxyc", "xylhc")
-RS_ROUTES = ("cxylh", "clyhx", "cxylh", "cyhlx", "cxyhl", "clhyx", "cylxh", "cxylh", "cyxhl", "chlyx", "clyxh", "cylhx")
+AG_ROUTES = ("lhyxc", "hlxyc", "lhxyc", "hylxc", "hyxlc", "hxylc", "lhxyc", "lhyxc", "hyxlc", "hylxc", "lhxyc", "hxlyc")
+RS_ROUTES = ("cxylh", "cyxhl", "cylhx", "cylhx", "clxhy", "cxhyl", "clxyh", "cxyhl", "cylhx", "cylxh", "chxyl", "clxhy")
 ORDER = (
-    6, 12, 0, 66, 18, 30, 42, 48, 36, 60, 54, 24, 144, 147, 145, 13, 31, 7, 55, 1,
-    146, 19, 25, 49, 37, 43, 61, 67, 32, 8, 56, 14, 2, 20, 26, 38, 50, 44, 62, 68,
-    9, 33, 15, 27, 57, 3, 21, 63, 39, 10, 16, 51, 45, 11, 149, 151, 69, 17, 4, 150,
-    153, 154, 156, 155, 22, 28, 157, 5, 34, 148, 152, 40, 158, 23, 159, 46, 29, 64, 58, 35,
-    160, 161, 52, 96, 102, 41, 47, 162, 70, 163, 108, 59, 65, 114, 53, 164, 97, 165, 126, 120,
-    103, 71, 166, 109, 115, 167, 127, 132, 138, 168, 189, 121, 169, 133, 98, 170, 90, 171, 139, 172,
-    173, 72, 110, 181, 174, 78, 91, 177, 180, 183, 128, 134, 104, 73, 175, 79, 99, 176, 111, 116,
-    122, 178, 179, 84, 140, 184, 185, 129, 186, 85, 92, 190, 187, 105, 182, 135, 195, 112, 74, 188,
-    80, 191, 130, 117, 196, 123, 192, 100, 106, 141, 86, 75, 136, 93, 131, 118, 113, 81, 197, 101,
-    124, 87, 76, 142, 94, 137, 198, 119, 125, 88, 82, 77, 193, 107, 199, 143, 95, 83, 89, 204,
-    194, 200, 205, 201, 202, 203, 206, 207,
+    480, 482, 483, 481, 40, 20, 43, 63, 46, 70, 6, 60, 50, 41, 3, 0, 1, 26, 110, 66,
+    23, 21, 103, 10, 30, 81, 83, 80, 61, 86, 90, 484, 55, 47, 44, 42, 51, 106, 100, 186,
+    166, 101, 121, 163, 120, 123, 221, 161, 190, 181, 210, 130, 150, 226, 126, 485, 15, 75, 62, 71,
+    35, 24, 22, 27, 64, 67, 4, 31, 2, 11, 7, 183, 203, 180, 140, 206, 160, 170, 200, 201,
+    223, 230, 146, 141, 220, 143, 95, 82, 84, 87, 91, 56, 45, 52, 48, 76, 72, 65, 68, 115,
+    104, 111, 102, 107, 135, 122, 127, 124, 131, 36, 32, 25, 28, 96, 92, 88, 85, 16, 5, 8,
+    12, 57, 49, 53, 155, 151, 142, 147, 144, 195, 182, 191, 184, 187, 215, 211, 202, 204, 207, 175,
+    162, 164, 167, 171, 116, 105, 108, 112, 37, 33, 29, 17, 9, 13, 97, 89, 93, 235, 224, 231,
+    227, 222, 77, 69, 73, 58, 54, 136, 128, 125, 132, 196, 185, 188, 192, 176, 168, 165, 172, 156,
+    152, 148, 145, 59, 488, 491, 493, 18, 14, 494, 38, 34, 117, 113, 109, 492, 236, 232, 228, 216,
+    212, 205, 208, 225, 495, 19, 98, 78, 74, 94, 486, 137, 133, 129, 157, 153, 149, 197, 189, 193,
+    39, 487, 489, 490, 79, 118, 114, 99, 177, 169, 173, 217, 209, 213, 496, 237, 229, 233, 497, 138,
+    134, 158, 154, 119, 498, 198, 194, 499, 322, 324, 320, 178, 323, 342, 321, 340, 174, 343, 344, 341,
+    139, 159, 218, 214, 500, 501, 381, 384, 382, 383, 380, 335, 327, 328, 360, 362, 326, 364, 325, 363,
+    361, 199, 238, 234, 355, 348, 347, 345, 346, 179, 502, 395, 386, 387, 385, 388, 219, 503, 400, 401,
+    422, 403, 404, 375, 365, 366, 368, 367, 402, 423, 421, 420, 424, 239, 504, 505, 461, 464, 462, 443,
+    460, 463, 442, 415, 408, 441, 407, 444, 440, 405, 336, 331, 329, 330, 406, 356, 351, 350, 349, 506,
+    376, 370, 369, 371, 527, 435, 425, 426, 428, 427, 507, 475, 467, 468, 465, 396, 391, 389, 455, 446,
+    445, 466, 447, 390, 448, 508, 300, 301, 303, 304, 509, 519, 510, 511, 512, 315, 515, 476, 471, 470,
+    469, 260, 307, 377, 262, 242, 337, 333, 305, 416, 409, 411, 410, 308, 241, 261, 244, 302, 243, 240,
+    516, 397, 392, 393, 264, 263, 332, 372, 306, 521, 275, 265, 266, 268, 267, 513, 357, 352, 520, 456,
+    451, 450, 449, 255, 248, 246, 247, 353, 245, 373, 436, 430, 429, 431, 518, 514, 517, 282, 280, 281,
+    283, 528, 284, 417, 412, 316, 311, 309, 310, 378, 413, 374, 522, 523, 295, 287, 285, 286, 398, 394,
+    288, 477, 473, 472, 276, 269, 270, 271, 525, 457, 452, 453, 533, 529, 358, 338, 334, 437, 433, 354,
+    432, 524, 534, 418, 414, 317, 312, 313, 526, 256, 249, 251, 250, 530, 277, 296, 289, 290, 291, 273,
+    272, 399, 379, 438, 458, 454, 434, 359, 478, 474, 339, 535, 419, 318, 257, 314, 252, 253, 297, 293,
+    292, 479, 459, 536, 278, 274, 258, 254, 439, 542, 298, 294, 279, 531, 537, 319, 259, 299, 543, 544,
+    532, 538, 545, 539, 546, 540, 541, 547, 548,
 )
 
 
@@ -697,10 +715,10 @@
         return (at["h"] * 4 + at["l"] * 2 + at["y"], at["x"] * 2 + at["c"])
 
     def steps(self, axis, do):
-        self.repeat(self.count(axis), do)
-
-    def repeat(self, size, do):
-        if size <= 32:
+        self.repeat(self.count(axis), do, 8)
+
+    def repeat(self, size, do, most):
+        if size <= most:
             for step in range(1, size):
                 do(step)
         else:
@@ -723,7 +741,7 @@
             else:
                 do((dp, lax.rem(head + step, heads)))
 
-        self.repeat(lax.axis_size(name), one)
+        self.repeat(lax.axis_size(name), one, 32)
 
     def signal(self):
         def one(device):
@@ -757,88 +775,122 @@
 
 class Gather:
     def __init__(self, links, w, send, recv):
-        self.links, self.w, self.send, self.recv = links, w, send, recv
-
-    def start(self, slot, phase):
+        self.links, self.w, self.sems = links, w, (send, recv)
+
+    def start(self, slot, i, j):
+        path, links = AG_ROUTES[slot], self.links
+
+        def along(**at):
+            part = links.region(self.w, slot, path[: max(i, 0)], **at)
+            sems = [s.at[slot, j] for s in self.sems]
+            links.steps(
+                path[j],
+                lambda step: links.copy(part, part, *sems, links.device(path[j], step)).start(),
+            )
+
+        if i < 0:
+            along()
+        else:
+            links.steps(path[i], lambda step: along(**{path[i]: links.peer(path[i], step)}))
+
+    def descriptor(self, slot, j):
         path = AG_ROUTES[slot]
-        part = self.links.region(self.w, slot, path[:phase])
-        sems = self.send.at[slot, phase], self.recv.at[slot, phase]
-
-        def go(step):
-            self.links.copy(part, part, *sems, self.links.device(path[phase], step)).start()
-
-        self.links.steps(path[phase], go)
-
-    def descriptor(self, slot, phase):
-        path = AG_ROUTES[slot]
-        at = {"h": pl.ds(0, self.links.far - 1)} if path[phase] == "h" else {}
-        part = self.links.region(self.w, slot, path[:phase], **at)
-        sems = self.send.at[slot, phase], self.recv.at[slot, phase]
-        return self.links.copy(part, part, *sems, self.links.device(path[phase], 1))
-
-    def tick(self, slot, phase):
-        if phase:
-            self.descriptor(slot, phase - 1).wait_recv()
-        if phase < len(AXES):
-            self.start(slot, phase)
+        at = {"h": pl.ds(0, self.links.far - 1)} if path[j] == "h" else {}
+        part = self.links.region(self.w, slot, path[:j], **at)
+        sems = [s.at[slot, j] for s in self.sems]
+        return self.links.copy(part, part, *sems, self.links.device(path[j], 1))
+
+    def arrive(self, slot, j):
+        self.descriptor(slot, j).wait_recv()
 
     def sent(self):
         for slot in range(MATS):
-            for phase in range(len(AXES)):
-                self.descriptor(slot, phase).wait_send()
+            for j in range(len(AXES)):
+                self.descriptor(slot, j).wait_send()
+
+    def steps(self):
+        for slot in range(MATS):
+            for j in range(len(AXES)):
+                for i in range(-1, j):
+                    yield functools.partial(self.start, slot, i, j)
+            for j in range(len(AXES)):
+                yield functools.partial(self.arrive, slot, j)
 
 
 class Scatter:
     def __init__(self, links, g, boxes, total, send, recv):
         self.links, self.g, self.boxes, self.total = links, g, boxes, total
-        self.send, self.recv = send, recv
-
-    def descriptor(self, slot, phase):
-        box = self.boxes[slot * len(AXES) + phase]
-        sems = self.send.at[slot, phase], self.recv.at[slot, phase]
-        return self.links.copy(box, box, *sems, self.links.device(RS_ROUTES[slot][phase], 1))
-
-    def take(self, slot, phase):
-        path = RS_ROUTES[slot]
-        self.descriptor(slot, phase).wait_recv()
-        own = self.links.region(self.g, slot, path[phase + 1 :])
-        box = self.boxes[slot * len(AXES) + phase]
-        if path[phase] == "h" and box.shape[0] == 1:
-            box = box.at[0]
-        elif path[phase] == "h":
+        self.sems = (send, recv)
+
+    def box(self, slot, j):
+        return self.boxes[slot * len(AXES) + j - 1]
+
+    def start(self, slot, i, j):
+        path, links = RS_ROUTES[slot], self.links
+        first = sum(links.count(a) - 1 for a in path[:i]) - 1
+        sems = self.sems[0].at[slot, i], self.sems[1].at[slot, j - 1]
+
+        def go(step):
+            at = {path[i]: links.peer(path[i], step)}
+            into = self.box(slot, j).at[first + step]
+            device = links.device(path[i], step)
+
+            def part(into, **more):
+                src = links.region(self.g, slot, path[j + 1 :], **at, **more)
+                links.copy(src, into, *sems, device).start()
+
+            if j == len(AXES):
+                part(into)
+            else:
+                links.steps(
+                    path[j], lambda n: part(into.at[n - 1], **{path[j]: links.peer(path[j], n)})
+                )
+
+        links.steps(path[i], go)
+
+    def add(self, slot, j):
+        path, links = RS_ROUTES[slot], self.links
+        box = self.box(slot, j)
+        self.arrived(slot, j).wait_recv()
+
+        def total(own, pick):
             value = own[...].astype(F32)
-            return own, value + jnp.sum(box[...].astype(F32), axis=0)
-        return own, own[...] + box[...] if phase + 1 < len(AXES) else (
-            own[...].astype(F32) + box[...].astype(F32)
-        )
-
-    def start(self, slot, phase):
-        path = RS_ROUTES[slot]
-        axis, rest = path[phase], path[phase + 1 :]
-        box = self.boxes[slot * len(AXES) + phase]
-        sems = self.send.at[slot, phase], self.recv.at[slot, phase]
-
-        def go(step):
-            at = {axis: self.links.peer(axis, step)}
-            part = self.links.region(self.g, slot, rest, **at)
-            into = box.at[step - 1] if axis == "h" else box
-            self.links.copy(part, into, *sems, self.links.device(axis, step)).start()
-
-        self.links.steps(axis, go)
-
-    def tick(self, slot, phase):
-        if phase:
-            own, value = self.take(slot, phase - 1)
-            if phase == len(AXES):
-                self.total[SLOT_OF.index(slot)] = value
-                return
-            own[...] = value.astype(BF16)
-        self.start(slot, phase)
+            for e in range(box.shape[0]):
+                value = value + pick(box.at[e])[...].astype(F32)
+            return value
+
+        if j == len(AXES):
+            own = links.region(self.g, slot, "")
+            self.total[SLOT_OF.index(slot)] = total(own, lambda b: b)
+            return
+
+        def one(n):
+            own = links.region(self.g, slot, path[j + 1 :], **{path[j]: links.peer(path[j], n)})
+            own[...] = total(own, lambda b: b.at[n - 1]).astype(BF16)
+
+        links.steps(path[j], one)
+
+    def arrived(self, slot, j):
+        box = self.box(slot, j)
+        sems = self.sems[0].at[slot, j - 1], self.sems[1].at[slot, j - 1]
+        return self.links.copy(box, box, *sems, self.links.device("c", 1))
 
     def sent(self):
         for slot in range(MATS):
-            for phase in range(len(AXES)):
-                self.descriptor(slot, phase).wait_send()
+            path = RS_ROUTES[slot]
+            for i in range(len(AXES)):
+                at = {"h": pl.ds(0, self.links.far - 1)} if path[i] == "h" else {}
+                part = self.links.region(self.g, slot, path[i + 1 :], **at)
+                sems = [s.at[slot, i] for s in self.sems]
+                self.links.copy(part, part, *sems, self.links.device(path[i], 1)).wait_send()
+
+    def steps(self):
+        for slot in range(MATS):
+            for i in range(len(AXES)):
+                for j in range(i + 1, len(AXES) + 1):
+                    yield functools.partial(self.start, slot, i, j)
+            for j in range(1, len(AXES) + 1):
+                yield functools.partial(self.add, slot, j)
 
 
 class Small:
@@ -978,46 +1030,52 @@
 
 
 class Adafactor:
-    def __init__(self, refs, row_share, col_share, sq_share):
+    def __init__(self, refs, lo, hi, row_share, col_share, sq_share):
         self.__dict__.update(refs)
+        self.lo, self.hi = lo, hi
         self.row_share, self.col_share, self.sq_share = row_share, col_share, sq_share
 
-    def eye(self, count):
+    def eye(self, count, first):
         r = lax.broadcasted_iota(jnp.int32, (count, LANES), 0)
         c = lax.broadcasted_iota(jnp.int32, (count, LANES), 1)
-        return jnp.where(r == c, 1.0, 0.0)
+        return jnp.where(c == r + first, 1.0, 0.0)
 
     def lane(self, k, value, rest):
         lanes = lax.broadcasted_iota(jnp.int32, rest.shape, 1)
         return jnp.where(lanes == k, value, rest)
 
     def squares(self):
-        rows = self.wg.shape[1]
+        rows, count = self.wg.shape[1], self.hi - self.lo
         by_row = jnp.zeros((rows, LANES), F32)
         by_col = []
-        for k in range(MATS):
+        for k in range(self.lo, self.hi):
             g = self.wg[k]
             s = g * g + SQUARE_FLOOR
             by_row = self.lane(k, jnp.sum(s, axis=1, keepdims=True), by_row)
             by_col.append(jnp.sum(s, axis=0, keepdims=True))
-        self.col_share.start(jnp.concatenate([*by_col, jnp.zeros((4, LANES), F32)], axis=0))
-        turned = exact(self.eye(16), by_row, NT)
+        rest = jnp.zeros((SLOTS - count, LANES), F32)
+        self.col_share.start(jnp.concatenate([*by_col, rest] if count < SLOTS else by_col, axis=0))
+        turned = exact(self.eye(SLOTS, self.lo), by_row, NT)
         if rows < LANES:
-            turned = jnp.concatenate([turned, jnp.zeros((16, LANES - rows), F32)], axis=1)
+            turned = jnp.concatenate([turned, jnp.zeros((SLOTS, LANES - rows), F32)], axis=1)
         self.row_share.start(turned)
 
     def scale(self):
-        rows = self.wg.shape[1]
-        total = self.row_share.total()[0:MATS, 0:rows]
-        new_rows = SECOND_DECAY * self.row_state[...] + (1.0 - SECOND_DECAY) * (total * (1.0 / D))
-        self.new_rows[...] = new_rows
-        row = exact(new_rows, self.eye(MATS), TN)
-        total = self.col_share.total()[0:MATS]
-        cols = SECOND_DECAY * self.col_state[...] + (1.0 - SECOND_DECAY) * (total * (1.0 / D))
-        self.new_cols[...] = cols
+        rows, lo, hi = self.wg.shape[1], self.lo, self.hi
+        total = self.row_share.total()[0 : hi - lo, 0:rows]
+        new_rows = SECOND_DECAY * self.row_state[lo:hi, :] + (1.0 - SECOND_DECAY) * (
+            total * (1.0 / D)
+        )
+        self.new_rows[lo:hi, :] = new_rows
+        row = exact(new_rows, self.eye(hi - lo, lo), TN)
+        total = self.col_share.total()[0 : hi - lo]
+        cols = SECOND_DECAY * self.col_state[lo:hi, :] + (1.0 - SECOND_DECAY) * (
+            total * (1.0 / D)
+        )
+        self.new_cols[lo:hi, :] = cols
         sums = jnp.zeros((1, LANES), F32)
-        for k in range(MATS):
-            u = self.wg[k] * lax.rsqrt(row[:, k : k + 1] * cols[k : k + 1, :])
+        for k in range(lo, hi):
+            u = self.wg[k] * lax.rsqrt(row[:, k : k + 1] * cols[k - lo : k - lo + 1, :])
             self.upd[k] = u
             s = jnp.sum(jnp.sum(u * u, axis=0, keepdims=True), axis=1, keepdims=True)
             sums = self.lane(k, s, sums)
@@ -1029,16 +1087,22 @@
         mean = total[1:2] * (1.0 / (D * lax.axis_size(HEAD)))
         rms = jnp.sqrt(total[0:1] * mean * (1.0 / (D * D)))
         rate = STEP_RATE * jnp.sqrt(mean) / jnp.maximum(1.0, rms)
-        for k in range(MATS):
+        for k in range(self.lo, self.hi):
             new = self.weights[k] - rate[:, k : k + 1] * self.upd[k]
             self.new_weights[k] = new
             self.copy[k] = new.astype(BF16)
             self.new_ema[k] = AVERAGE_KEEP * self.ema[k] + (1.0 - AVERAGE_KEEP) * new
-        self.rms[...] = rms
+        self.rms[self.lo // 4 : self.lo // 4 + 1, :] = rms
+
+
+class SmallStep:
+    def __init__(self, refs):
+        self.__dict__.update(refs)
 
     def clips(self):
         lanes = lax.broadcasted_iota(jnp.int32, (1, LANES), 1)
-        clip = jnp.where(lanes < MATS, self.rms[...], self.small_clip[...])
+        clip = jnp.where(lanes < EARLY, self.rms[0:1, :], self.rms[1:2, :])
+        clip = jnp.where(lanes < MATS, clip, self.small_clip[...])
         self.clip[...] = clip[:, 0 : self.clip.shape[1]]
 
     def small_step(self):
@@ -1091,13 +1155,12 @@
 
 
 def box_shapes(links, block):
-    for slot in range(MATS):
-        path = RS_ROUTES[slot]
-        for phase, axis in enumerate(path):
-            lead = [links.count(a) for a in AXES if a in path[phase + 1 :]]
-            if axis == "h":
-                lead = [links.far - 1, *lead]
-            yield pltpu.VMEM((*lead, *block), BF16)
+    for path in RS_ROUTES:
+        for j in range(1, len(AXES) + 1):
+            entries = sum(links.count(a) - 1 for a in path[:j])
+            ways = [links.count(path[j]) - 1] if j < len(AXES) else []
+            rest = [links.count(a) for a in AXES if a in path[j + 1 :]]
+            yield pltpu.VMEM((entries, *ways, *rest, *block), BF16)
 
 
 def shared_of(weights, parts, heads):
@@ -1124,12 +1187,12 @@
         in_h=f(links.far, SMALL_ROWS, LANES),
         in_l=part,
         full=f(2, 2, SMALL_ROWS, LANES),
-        row_box=f(heads, 16, LANES),
-        col_box=f(parts, 16, LANES),
-        sq_box=f(parts * heads, 2, LANES),
+        row_box=f(2, heads, SLOTS, LANES),
+        col_box=f(2, parts, SLOTS, LANES),
+        sq_box=f(2, parts * heads, 2, LANES),
         upd=f(MATS, *block),
         small_clip=f(1, LANES),
-        rms=f(1, LANES),
+        rms=f(2, LANES),
         ag_send=dma((MATS, len(AXES))),
         ag_recv=dma((MATS, len(AXES))),
         rs_send=dma((MATS, len(AXES))),
@@ -1140,8 +1203,8 @@
         out_recv=dma((3,)),
         in_send=dma((3,)),
         in_recv=dma((3,)),
-        opt_send=dma((3,)),
-        opt_recv=dma((3,)),
+        opt_send=dma((2, 3)),
+        opt_recv=dma((2, 3)),
         fetched=dma((len(Inputs._fields),)),
         stored=dma((len(Outputs._fields),)),
     )
@@ -1165,10 +1228,9 @@
     n_in, n_out = len(Inputs._fields), len(Outputs._fields)
     ins, outs, refs = Inputs(*refs[:n_in]), Outputs(*refs[n_in : n_in + n_out]), refs[n_in + n_out :]
     r = types.SimpleNamespace(**dict(zip(names, refs)))
-    r.cls, r.img = ins.cls, ins.img
     fetch = Inputs(
         *[
-            None if i < 2 else Ready(ref, getattr(r, name), r.fetched.at[i])
+            Ready(ref, getattr(r, name), r.fetched.at[i])
             for i, (name, ref) in enumerate(zip(Inputs._fields, ins))
         ]
     )
@@ -1181,7 +1243,7 @@
     boxes = refs[len(names) :]
     links = Links()
     links.signal()
-    for one in (fetch.weights, fetch.small, fetch.tokens, fetch.cot, *fetch[5:8], *fetch[9:]):
+    for one in (fetch.weights, *fetch[0:2], fetch.small, *fetch[2:4], *fetch[5:8], *fetch[9:]):
         one.start()
     r.out_own = r.out_rows.at[lax.axis_index(HEAD)]
     r.in_own = r.in_rows.at[lax.axis_index(HEAD)]
@@ -1197,27 +1259,25 @@
     )
     out_rows = Rows(links, r.out_rows, r.out, own, r.out_send, r.out_recv)
     in_rows = Rows(links, r.in_rows, r.grad_in, own, r.in_send, r.in_recv)
-    shares = [
-        Exchange(links, axis, box, r.opt_send.at[i], r.opt_recv.at[i])
-        for i, (axis, box) in enumerate(((HEAD, r.row_box), (DP, r.col_box), (ALL, r.sq_box)))
-    ]
-    opt = Adafactor(vars(r), *shares)
-
-    fetch.weights.wait()
-    for k in range(MATS):
-        mine = links.region(r.w, SLOT_OF[k], "")
-        mine[...] = r.weights[k].astype(BF16)
-    links.meet()
-
-    ops = []
-    for tick in (gather.tick, scatter.tick):
-        ops += [
-            functools.partial(tick, slot, phase)
-            for slot in range(MATS)
-            for phase in range(len(AXES) + 1)
+    shares, opts = [], []
+    for part, (lo, hi) in enumerate(((0, EARLY), (EARLY, MATS))):
+        boxes = (HEAD, r.row_box), (DP, r.col_box), (ALL, r.sq_box)
+        shares += [
+            Exchange(links, axis, box.at[part], r.opt_send.at[part, i], r.opt_recv.at[part, i])
+            for i, (axis, box) in enumerate(boxes)
         ]
+        opts.append(Adafactor(vars(r), lo, hi, *shares[-3:]))
+    step = SmallStep(vars(r))
+
+    def round_weights():
+        for k in range(MATS):
+            mine = links.region(r.w, SLOT_OF[k], "")
+            mine[...] = r.weights[k].astype(BF16)
+
+    ops = [*gather.steps(), *scatter.steps()]
+    ops += [then(fetch.weights.wait, round_weights), links.meet]
     ops += [
-        then(fetch.small.wait, blk.setup),
+        then(fetch.small.wait, fetch.cls.wait, fetch.img.wait, blk.setup),
         then(fetch.tokens.wait, blk.read_tokens),
         blk.norm_one,
         then(fetch.cot.wait, blk.read_cotangent),
@@ -1242,28 +1302,21 @@
         then(
             fetch.small_state.wait,
             fetch.small_ema.wait,
-            opt.small_step,
+            step.small_step,
             store.small_grads.start,
             store.new_small_state.start,
             store.new_small.start,
             store.new_small_ema.start,
         ),
-        then(store.wg.start, opt.squares),
+        opts[1].squares,
+        then(store.wg.start, opts[0].squares),
+        then(fetch.row_state.wait, fetch.col_state.wait, opts[1].scale),
+        then(opts[0].scale, store.new_rows.start, store.new_cols.start),
+        then(fetch.ema.wait, opts[1].apply),
         then(
-            fetch.row_state.wait,
-            fetch.col_state.wait,
-            opt.scale,
-            store.new_rows.start,
-            store.new_cols.start,
+            opts[0].apply, store.new_weights.start, store.copy.start, store.new_ema.start
         ),
-        then(
-            fetch.ema.wait,
-            opt.apply,
-            store.new_weights.start,
-            store.copy.start,
-            store.new_ema.start,
-        ),
-        then(opt.clips, store.clip.start),
+        then(step.clips, store.clip.start),
     ]
     for i in ORDER:
         ops[i]()
@@ -1301,7 +1354,6 @@
     small_ema,
 ):
     parts, heads = lax.axis_size(DP), lax.axis_size(HEAD)
-    smem = pl.BlockSpec(memory_space=pltpu.SMEM)
     shared = shared_of(weights, parts, heads)
     own = scratch_of()
 
@@ -1337,13 +1389,14 @@
         small_state,
         small_ema,
     )
-    staged = [pltpu.VMEM(x.shape, x.dtype) for x in (*args[2:], *outs)]
-    names = (*shared, *own, *Inputs._fields[2:], *Outputs._fields)
+    staged = [pltpu.SMEM(x.shape, x.dtype) for x in args[:2]]
+    staged += [pltpu.VMEM(x.shape, x.dtype) for x in (*args[2:], *outs)]
+    names = (*shared, *own, *Inputs._fields, *Outputs._fields)
     far = pl.BlockSpec(memory_space=pltpu.HBM)
     res = pl.pallas_call(
         functools.partial(block_kernel, names),
         out_shape=outs,
-        in_specs=[smem, smem] + [far] * 9,
+        in_specs=[far] * len(args),
         out_specs=(far,) * len(outs),
         scratch_shapes=[
             *shared.values(),

time: 94.6 us -> 87.3 us (0.923)
  Pallas kernels: 93.6 us -> 86.3 us
    pallas_call x1, Pallas kernels: 90 us -> 82.7 us  [local(): pl.pallas_call(functools.partial(block_kernel, names), out_shape=outs, in...]
where the time goes in v9:
time: 87.3 us; the launch traced here: 87.1 us
  Pallas kernels  86.3 us (99%)
    pallas_call x1, Pallas kernels, local(): pl.pallas_call(functools.partial(block_kernel, names), out_shape=outs, in...  82.7 us
    pallas_call x1, Pallas kernels, local(): pl.pallas_call(functools.partial(finish_kernel, len(outs)), out_shape=out...  3.58 us

profile of v9, /device:TPU:0, one launch (start us, length us, event | category | flops | bytes accessed | tf_op | source)
XLA Modules:
  0.0 87.1 jit_solution(15611339500491846742)
XLA Ops:
  0.6 82.7 %block.1 = (bf16[1176,512]{1,0:T(8,128)(2,1)}, bf16[1176,512]{1,0:T(8,128)(2,1)}, f32[12,64,128]{2,1,0:T(8,128)}, f32[12,64]{1,0:T(8,128)}, f32[12,128]{1,0:T(8,...) custom-call(s32[4,6]{1,0:T(4,128)} %refs_0_.1, ...), custom_call_target="tpu_custom_call" | custom-call | tf_op jit(solution)/shard_map/block/pallas_call | solution.py:1396
  83.4 3.6 %finish.1 = (bf16[1176,512]{1,0:T(8,128)(2,1)}, bf16[1176,512]{1,0:T(8,128)(2,1)}, f32[12,64,128]{2,1,0:T(8,128)}, f32[12,64]{1,0:T(8,128)}, f32[12,128]{1,0:T(8...) custom-call(bf16[1176,512]{1,0:T(8,128)(2,1)} %get-tuple-element.39., ...), custom_call_target="tpu_custom_call" | custom-call | tf_op jit(solution)/shard_map/finish/pallas_call | solution.py:1412

commit v10 on v9

--- a/solution.py
+++ b/solution.py
@@ -1,4 +1,5 @@
 import functools
+import itertools
 import math
 import types
 from typing import Any, NamedTuple
@@ -22,6 +23,8 @@
 SLOTS = 8
 CELL_PAD = CELLS + 1
 ROWS = CELL_PAD * SLOTS
+PIECES = 5
+PIECE = ROWS // PIECES
 LANES = 128
 WIDE = 256
 REACHES = (1, 2, 3, 3)
@@ -62,6 +65,14 @@
         return body(pl.multiple_of(j * size, size), carry)
 
     return lax.fori_loop(0, count // size, step, init, unroll=unroll)
+
+
+def piece_loop(piece, body):
+    def step(j, carry):
+        body(pl.multiple_of(piece * PIECE + j * 16, 16))
+        return carry
+
+    lax.fori_loop(0, PIECE // 16, step, 0, unroll=5)
 
 
 def conv(src, halo, tap, reach, lanes, put):
@@ -219,67 +230,57 @@
         pick = jnp.where(t == target, 1.0, 0.0).astype(BF16)
         out_ref[...] = dot(pick, src_ref[...]).astype(BF16)
 
-    def read_tokens(self):
+    def read_tokens(self, piece):
         first = lax.axis_index(HEAD) * (self.cls.shape[1] * CELLS)
-        size = 80
-
-        def body(r0, _):
-            live = wide(self.live[pl.ds(r0, size), :])
-            x = self.place(self.tokens, first, r0, size)
-            self.first[pl.ds(r0, size), :] = x
-            c0 = r0 // SLOTS
-            self.pos_src[pl.ds(GRID + c0, size // SLOTS)] = (x * live).reshape(-1, SLOTS, D)
-            return 0
-
-        rows_loop(ROWS, size, body, 0)
-
-    def read_cotangent(self):
+        r0 = piece * PIECE
+        rows = slice(r0, r0 + PIECE)
+        x = self.place(self.tokens, first, r0, PIECE)
+        self.first[rows, :] = x
+        cells = slice(GRID + r0 // SLOTS, GRID + (r0 + PIECE) // SLOTS)
+        self.pos_src[cells] = (x * wide(self.live[rows, :])).reshape(-1, SLOTS, D)
+
+    def read_cotangent(self, piece):
         first = lax.axis_index(HEAD) * (self.cls.shape[1] * CELLS)
-        size = 80
-
-        def body(r0, _):
-            live = wide(self.live[pl.ds(r0, size), :])
-            c = self.place(self.cot, first, r0, size)
-            self.go[pl.ds(r0, size), :] = (c * live).astype(BF16)
-            return 0
-
-        rows_loop(ROWS, size, body, 0)
+        rows = slice(piece * PIECE, (piece + 1) * PIECE)
+        c = self.place(self.cot, first, piece * PIECE, PIECE)
+        self.go[rows, :] = (c * wide(self.live[rows, :])).astype(BF16)
+
+    def turn_cotangent(self):
         self.go_t[...] = self.go[...].T
         self.back[...] = jnp.zeros((ROWS, D), F32)
 
-    def norm_one(self):
-        for c in range(D // LANES):
-            lanes = slice(c * LANES, (c + 1) * LANES)
-
-            def put(cell, value):
-                rows = pl.ds(pl.multiple_of(cell * SLOTS, SLOTS), SLOTS)
-                self.first[rows, lanes] = self.first[rows, lanes] + value + self.small[8:9, lanes]
-
-            def tap(a, b):
-                t = 13 + (a + 1) * 3 + b + 1
-                return self.small[t : t + 1, lanes]
-
-            conv(self.pos_src, 1, tap, 1, lanes, put)
-
-        def body(r0, _):
+    def position(self, c):
+        lanes = slice(c * LANES, (c + 1) * LANES)
+
+        def put(cell, value):
+            rows = pl.ds(pl.multiple_of(cell * SLOTS, SLOTS), SLOTS)
+            self.first[rows, lanes] = self.first[rows, lanes] + value + self.small[8:9, lanes]
+
+        def tap(a, b):
+            t = 13 + (a + 1) * 3 + b + 1
+            return self.small[t : t + 1, lanes]
+
+        conv(self.pos_src, 1, tap, 1, lanes, put)
+
+    def norm_one(self, piece):
+        def body(r0):
             rows = pl.ds(r0, 16)
             n, u, inv = norm_rows(self.first[rows, :], self.row(0), self.row(1))
             self.n1[rows, :] = n.astype(BF16)
             self.u1[rows, :] = u
             self.inv1[rows, :] = jnp.broadcast_to(inv, (16, LANES))
-            return 0
-
-        rows_loop(ROWS, 16, body, 0, unroll=5)
+
+        piece_loop(piece, body)
+
+    def turn_one(self):
         self.n1_t[...] = self.n1[...].T
 
-    def project(self, k):
-        low = (self.q, self.k, self.v)[k]
-        for b in range(2):
-            cols = lane_block(b)
-            p = self.times(self.n1[...], k, b)
-            if k != 1:
-                p = p + self.small[2 + k // 2 : 3 + k // 2, cols]
-            low[:, cols] = p.astype(BF16)
+    def project(self, k, b):
+        low, cols = (self.q, self.k, self.v)[k], lane_block(b)
+        p = self.times(self.n1[...], k, b)
+        if k != 1:
+            p = p + self.small[2 + k // 2 : 3 + k // 2, cols]
+        low[:, cols] = p.astype(BF16)
 
     def image_sum(self, x):
         total = jnp.zeros((SLOTS, D), F32)
@@ -288,7 +289,7 @@
             total = total + im * jnp.sum(im * x, axis=0, keepdims=True)
         return total
 
-    def softmax(self):
+    def key_tops(self):
         def top(r0, best):
             live = wide(self.live[pl.ds(r0, 16), :])
             keys = jnp.where(live > 0, self.k[pl.ds(r0, 16), :].astype(F32), NEG_LARGE)
@@ -300,9 +301,12 @@
             im = wide(self.im8[i])
             most = jnp.max(jnp.where(im > 0, best, NEG_LARGE), axis=0, keepdims=True)
             shift = jnp.where(im > 0, most, shift)
-        shift2 = jnp.concatenate([shift, shift], axis=0)
-
-        def raise_(r0, total):
+        self.soft_acc[0:SLOTS, :] = shift
+
+    def key_powers(self):
+        shift2 = jnp.concatenate([self.soft_acc[0:SLOTS, :]] * 2, axis=0)
+
+        def power(r0, total):
             rows = pl.ds(r0, 16)
             live = wide(self.live[rows, :])
             keys = self.k[rows, :].astype(F32)
@@ -310,11 +314,12 @@
             self.soft[rows, :] = e
             return total + fold(e)
 
-        total = self.image_sum(
-            rows_loop(ROWS, 16, raise_, jnp.zeros((SLOTS, D), F32), unroll=5)
-        )
-        scale = 1.0 / jnp.where(total > 0, total, 1.0)
-        scale2 = jnp.concatenate([scale, scale], axis=0)
+        total = rows_loop(ROWS, 16, power, jnp.zeros((SLOTS, D), F32), unroll=5)
+        total = self.image_sum(total)
+        self.soft_acc[SLOTS : 2 * SLOTS, :] = 1.0 / jnp.where(total > 0, total, 1.0)
+
+    def key_shares(self):
+        scale2 = jnp.concatenate([self.soft_acc[SLOTS : 2 * SLOTS, :]] * 2, axis=0)
 
         def divide(r0, _):
             rows = pl.ds(r0, 16)
@@ -341,13 +346,12 @@
     def stacked(self, x):
         return jnp.concatenate([x[:, lane_block(i)] for i in range(IMG_GROUP)], axis=0)
 
-    def contexts(self):
-        for b in range(2):
-            cols = lane_block(b)
-            ctx = dot(self.soft_low[:, cols], self.by_image(self.v[:, cols]), TN)
-            ctx = self.head_blocks(ctx)
-            self.ctx[b] = ctx
-            self.factor[:, cols] = dot(self.by_image(self.q[:, cols]), self.stacked(ctx))
+    def contexts(self, b):
+        cols = lane_block(b)
+        ctx = dot(self.soft_low[:, cols], self.by_image(self.v[:, cols]), TN)
+        ctx = self.head_blocks(ctx)
+        self.ctx[b] = ctx
+        self.factor[:, cols] = dot(self.by_image(self.q[:, cols]), self.stacked(ctx))
 
     def fill_window(self):
         def fill(r0, _):
@@ -382,31 +386,32 @@
 
         rows_loop(ROWS, 16, mix, 0, unroll=5)
 
-    def norm_two(self):
-        for b in range(2):
-            cols = lane_block(b)
-            p = self.times_t(self.mixed[...], 3, b)
-            self.second[:, cols] = self.first[:, cols] + p + self.small[4:5, cols]
-
-        def body(r0, _):
+    def attend(self, b):
+        cols = lane_block(b)
+        p = self.times_t(self.mixed[...], 3, b)
+        self.second[:, cols] = self.first[:, cols] + p + self.small[4:5, cols]
+
+    def norm_two(self, piece):
+        def body(r0):
             rows = pl.ds(r0, 16)
             n, u, inv = norm_rows(self.second[rows, :], self.row(5), self.row(6))
             self.n2[rows, :] = n.astype(BF16)
             self.u2[rows, :] = u
             self.inv2[rows, :] = jnp.broadcast_to(inv, (16, LANES))
-            return 0
-
-        rows_loop(ROWS, 16, body, 0, unroll=5)
+
+        piece_loop(piece, body)
+
+    def turn_two(self):
         self.n2_t[...] = self.n2[...].T
 
-    def hidden_block(self, r):
-        up, down = 4 + 2 * r, 5 + 2 * r
+    def hidden_in(self, r):
         for b in range(2):
             cols = lane_block(b)
-            h = self.times(self.n2[...], up, b) + self.small[pl.ds(9 + r, 1), cols]
+            h = self.times(self.n2[...], 4 + 2 * r, b) + self.small[9 + r : 10 + r, cols]
             self.hidden[:, cols] = h
-            self.factor[:, cols] = self.times(self.go[...], down, b)
-
+            self.factor[:, cols] = self.times(self.go[...], 5 + 2 * r, b)
+
+    def hidden_out(self, r):
         def body(r0, total):
             rows = pl.ds(r0, 16)
             act, slope = erf_parts(self.hidden[rows, :])
@@ -416,16 +421,21 @@
             return total + fold(g)
 
         total = rows_loop(ROWS, 16, body, jnp.zeros((SLOTS, D), F32), unroll=5)
-        self.sums[pl.ds(9 + r, 1), :] = jnp.sum(total, axis=0, keepdims=True)
-
-    def hidden_grads(self, r):
-        up, down = 4 + 2 * r, 5 + 2 * r
-        self.put_grad(down, self.go_t[...], self.active)
-        self.put_grad(up, self.n2_t[...], self.low)
+        self.sums[9 + r : 10 + r, :] = jnp.sum(total, axis=0, keepdims=True)
+
+    def grad_down(self, r):
+        self.put_grad(5 + 2 * r, self.go_t[...], self.active)
+
+    def grad_up(self, r):
+        self.put_grad(4 + 2 * r, self.n2_t[...], self.low)
+
+    def add_down(self, r):
         for b in range(2):
-            cols = lane_block(b)
-            self.second[:, cols] += self.times_t(self.active[...], down, b)
-            self.back[:, cols] += self.times_t(self.low[...], up, b)
+            self.second[:, lane_block(b)] += self.times_t(self.active[...], 5 + 2 * r, b)
+
+    def add_back(self, r):
+        for b in range(2):
+            self.back[:, lane_block(b)] += self.times_t(self.low[...], 4 + 2 * r, b)
 
     def finish_out(self):
         def body(r0, _):
@@ -456,11 +466,11 @@
     def grad_proj(self):
         self.put_grad(3, self.gs_low[...].T, self.mixed)
 
-    def back_heads(self):
+    def back_mixed(self):
         for b in range(2):
-            cols = lane_block(b)
-            self.d[:, cols] = self.times(self.gs_low[...], 3, b)
-
+            self.d[:, lane_block(b)] = self.times(self.gs_low[...], 3, b)
+
+    def back_fill(self):
         def fill(r0, _):
             rows = pl.ds(r0, 16)
             d = self.d[rows, :] * wide(self.live[rows, :])
@@ -472,13 +482,13 @@
             return 0
 
         rows_loop(ROWS, 16, fill, 0, unroll=5)
-        for b in range(2):
-            cols = lane_block(b)
-            f3 = self.by_image(self.f[:, cols])
-            g = self.head_blocks(dot(self.q[:, cols], f3, TN))
-            self.gq[:, cols] = dot(f3, self.ctx[b], NT)
-            self.gk[:, cols] = dot(self.by_image(self.v[:, cols]), g, NT)
-            self.gv[:, cols] = dot(self.by_image(self.soft_low[:, cols]), self.stacked(g))
+    def back_heads(self, b):
+        cols = lane_block(b)
+        f3 = self.by_image(self.f[:, cols])
+        g = self.head_blocks(dot(self.q[:, cols], f3, TN))
+        self.gq[:, cols] = dot(f3, self.ctx[b], NT)
+        self.gk[:, cols] = dot(self.by_image(self.v[:, cols]), g, NT)
+        self.gv[:, cols] = dot(self.by_image(self.soft_low[:, cols]), self.stacked(g))
 
     def back_window(self, c):
         lanes = slice(c * LANES, (c + 1) * LANES)
@@ -506,15 +516,17 @@
 
         tap_sums(up, self.rel_src, HALO, REACHES[c], lanes, put_tap)
 
-    def back_query_key(self):
-        zero = jnp.zeros((SLOTS, D), F32)
-
+    def back_inner(self):
         def inner(r0, total):
             rows = pl.ds(r0, 16)
             return total + fold(self.soft[rows, :] * self.gk[rows, :])
 
-        shared = self.image_sum(rows_loop(ROWS, 16, inner, zero, unroll=5))
-        shared2 = jnp.concatenate([shared, shared], axis=0)
+        total = rows_loop(ROWS, 16, inner, jnp.zeros((SLOTS, D), F32), unroll=5)
+        self.soft_acc[0:SLOTS, :] = self.image_sum(total)
+
+    def back_query_key(self):
+        zero = jnp.zeros((SLOTS, D), F32)
+        shared2 = jnp.concatenate([self.soft_acc[0:SLOTS, :]] * 2, axis=0)
 
         def low(r0, total):
             rows = pl.ds(r0, 16)
@@ -536,17 +548,14 @@
 
         total = rows_loop(ROWS, 16, low, jnp.zeros((SLOTS, D), F32), unroll=5)
         self.sums[3:4, :] = jnp.sum(total, axis=0, keepdims=True)
-        self.grad_of(2)
 
     def grad_of(self, k):
         self.put_grad(k, self.n1_t[...], self.gl.at[k])
 
-    def back_project(self):
-        for b in range(2):
-            cols = lane_block(b)
-            back = self.times_t(self.gl[0], 0, b)
-            back = back + self.times_t(self.gl[1], 1, b)
-            self.back[:, cols] = back + self.times_t(self.gl[2], 2, b)
+    def back_project(self, b):
+        back = self.times_t(self.gl[0], 0, b)
+        back = back + self.times_t(self.gl[1], 1, b)
+        self.back[:, lane_block(b)] = back + self.times_t(self.gl[2], 2, b)
 
     def back_one(self):
         zero = jnp.zeros((SLOTS, D), F32)
@@ -608,39 +617,38 @@
 MATS = len(SLOT_OF)
 EARLY = 4
 AXES = "xchly"
+WAYS, ENTRIES = 3, 6
 HEAD_ROWS = 320
 SMALL_ROWS = 72
-AG_ROUTES = ("lhyxc", "hlxyc", "lhxyc", "hylxc", "hyxlc", "hxylc", "lhxyc", "lhyxc", "hyxlc", "hylxc", "lhxyc", "hxlyc")
-RS_ROUTES = ("cxylh", "cyxhl", "cylhx", "cylhx", "clxhy", "cxhyl", "clxyh", "cxyhl", "cylhx", "cylxh", "chxyl", "clxhy")
+AG_ROUTES = ("zyxc", "zyxc", "zxyc", "zxyc", "zxyc", "zyxc", "yhxlc", "xylhc", "xhylc", "hlyxc", "hxlyc", "hlyxc")
+RS_ROUTES = ("cyxz", "cxyz", "cyxz", "cyxz", "cxhyl", "cyhlx", "cxlhy", "cyhlx", "cylxh", "clyxh", "cyxhl", "chlxy")
 ORDER = (
-    480, 482, 483, 481, 40, 20, 43, 63, 46, 70, 6, 60, 50, 41, 3, 0, 1, 26, 110, 66,
-    23, 21, 103, 10, 30, 81, 83, 80, 61, 86, 90, 484, 55, 47, 44, 42, 51, 106, 100, 186,
-    166, 101, 121, 163, 120, 123, 221, 161, 190, 181, 210, 130, 150, 226, 126, 485, 15, 75, 62, 71,
-    35, 24, 22, 27, 64, 67, 4, 31, 2, 11, 7, 183, 203, 180, 140, 206, 160, 170, 200, 201,
-    223, 230, 146, 141, 220, 143, 95, 82, 84, 87, 91, 56, 45, 52, 48, 76, 72, 65, 68, 115,
-    104, 111, 102, 107, 135, 122, 127, 124, 131, 36, 32, 25, 28, 96, 92, 88, 85, 16, 5, 8,
-    12, 57, 49, 53, 155, 151, 142, 147, 144, 195, 182, 191, 184, 187, 215, 211, 202, 204, 207, 175,
-    162, 164, 167, 171, 116, 105, 108, 112, 37, 33, 29, 17, 9, 13, 97, 89, 93, 235, 224, 231,
-    227, 222, 77, 69, 73, 58, 54, 136, 128, 125, 132, 196, 185, 188, 192, 176, 168, 165, 172, 156,
-    152, 148, 145, 59, 488, 491, 493, 18, 14, 494, 38, 34, 117, 113, 109, 492, 236, 232, 228, 216,
-    212, 205, 208, 225, 495, 19, 98, 78, 74, 94, 486, 137, 133, 129, 157, 153, 149, 197, 189, 193,
-    39, 487, 489, 490, 79, 118, 114, 99, 177, 169, 173, 217, 209, 213, 496, 237, 229, 233, 497, 138,
-    134, 158, 154, 119, 498, 198, 194, 499, 322, 324, 320, 178, 323, 342, 321, 340, 174, 343, 344, 341,
-    139, 159, 218, 214, 500, 501, 381, 384, 382, 383, 380, 335, 327, 328, 360, 362, 326, 364, 325, 363,
-    361, 199, 238, 234, 355, 348, 347, 345, 346, 179, 502, 395, 386, 387, 385, 388, 219, 503, 400, 401,
-    422, 403, 404, 375, 365, 366, 368, 367, 402, 423, 421, 420, 424, 239, 504, 505, 461, 464, 462, 443,
-    460, 463, 442, 415, 408, 441, 407, 444, 440, 405, 336, 331, 329, 330, 406, 356, 351, 350, 349, 506,
-    376, 370, 369, 371, 527, 435, 425, 426, 428, 427, 507, 475, 467, 468, 465, 396, 391, 389, 455, 446,
-    445, 466, 447, 390, 448, 508, 300, 301, 303, 304, 509, 519, 510, 511, 512, 315, 515, 476, 471, 470,
-    469, 260, 307, 377, 262, 242, 337, 333, 305, 416, 409, 411, 410, 308, 241, 261, 244, 302, 243, 240,
-    516, 397, 392, 393, 264, 263, 332, 372, 306, 521, 275, 265, 266, 268, 267, 513, 357, 352, 520, 456,
-    451, 450, 449, 255, 248, 246, 247, 353, 245, 373, 436, 430, 429, 431, 518, 514, 517, 282, 280, 281,
-    283, 528, 284, 417, 412, 316, 311, 309, 310, 378, 413, 374, 522, 523, 295, 287, 285, 286, 398, 394,
-    288, 477, 473, 472, 276, 269, 270, 271, 525, 457, 452, 453, 533, 529, 358, 338, 334, 437, 433, 354,
-    432, 524, 534, 418, 414, 317, 312, 313, 526, 256, 249, 251, 250, 530, 277, 296, 289, 290, 291, 273,
-    272, 399, 379, 438, 458, 454, 434, 359, 478, 474, 339, 535, 419, 318, 257, 314, 252, 253, 297, 293,
-    292, 479, 459, 536, 278, 274, 258, 254, 439, 542, 298, 294, 279, 531, 537, 319, 259, 299, 543, 544,
-    532, 538, 545, 539, 546, 540, 541, 547, 548,
+    390, 392, 393, 399, 397, 394, 395, 391, 11, 66, 129, 152, 136, 76, 156, 106, 132, 116, 109, 169,
+    396, 22, 69, 87, 96, 398, 403, 401, 72, 400, 147, 412, 0, 414, 172, 411, 127, 81, 77, 70,
+    121, 110, 117, 410, 73, 86, 176, 402, 33, 406, 404, 407, 18, 12, 15, 13, 149, 408, 44, 405,
+    409, 413, 415, 29, 24, 23, 26, 101, 97, 88, 167, 55, 7, 4, 1, 2, 89, 126, 113, 19,
+    16, 14, 67, 40, 37, 35, 90, 108, 112, 30, 27, 25, 34, 68, 102, 98, 51, 48, 91, 46,
+    94, 45, 8, 5, 62, 59, 146, 56, 141, 137, 128, 20, 17, 3, 166, 107, 130, 41, 38, 36,
+    57, 92, 21, 418, 31, 28, 82, 78, 103, 99, 419, 74, 422, 423, 52, 133, 49, 47, 424, 71,
+    95, 142, 138, 32, 420, 421, 161, 157, 427, 148, 9, 6, 150, 131, 430, 63, 60, 58, 153, 181,
+    168, 177, 428, 431, 170, 93, 134, 122, 118, 111, 114, 429, 10, 417, 42, 39, 426, 83, 75, 79,
+    162, 158, 154, 173, 416, 425, 53, 50, 151, 182, 174, 171, 178, 43, 432, 64, 61, 143, 135, 434,
+    139, 433, 437, 436, 435, 54, 104, 438, 123, 119, 115, 100, 439, 65, 441, 84, 80, 445, 449, 252,
+    250, 251, 163, 155, 461, 253, 254, 159, 105, 457, 144, 140, 183, 175, 440, 453, 230, 85, 232, 231,
+    442, 265, 256, 258, 255, 234, 233, 124, 120, 179, 446, 450, 293, 290, 291, 292, 145, 458, 257, 294,
+    245, 237, 235, 454, 270, 271, 274, 272, 462, 273, 164, 160, 125, 443, 305, 297, 296, 298, 295, 236,
+    184, 180, 447, 455, 311, 314, 313, 312, 310, 285, 276, 459, 277, 165, 463, 278, 451, 332, 334, 266,
+    261, 260, 333, 330, 331, 275, 185, 444, 259, 448, 460, 325, 318, 317, 316, 315, 246, 456, 352, 351,
+    353, 350, 345, 335, 238, 465, 338, 354, 492, 452, 336, 373, 306, 372, 464, 370, 466, 337, 301, 374,
+    371, 468, 365, 358, 355, 286, 300, 469, 357, 281, 483, 299, 485, 267, 356, 385, 467, 346, 339, 262,
+    219, 221, 220, 482, 263, 471, 326, 340, 341, 375, 477, 319, 226, 222, 476, 366, 320, 223, 470, 360,
+    268, 264, 376, 474, 475, 347, 342, 343, 307, 302, 303, 478, 361, 378, 481, 208, 210, 209, 359, 279,
+    472, 473, 327, 322, 323, 377, 480, 197, 198, 199, 321, 241, 227, 224, 269, 479, 215, 211, 212, 348,
+    344, 187, 186, 386, 381, 188, 484, 308, 379, 493, 487, 304, 239, 486, 204, 200, 367, 488, 328, 287,
+    362, 193, 189, 380, 490, 201, 324, 190, 498, 494, 216, 363, 309, 228, 213, 282, 489, 349, 387, 283,
+    499, 491, 205, 202, 247, 243, 280, 225, 242, 368, 382, 364, 383, 194, 240, 329, 191, 217, 214, 495,
+    288, 284, 500, 388, 384, 206, 203, 369, 229, 195, 192, 289, 248, 244, 501, 389, 218, 207, 249, 507,
+    196, 508, 502, 496, 503, 509, 510, 497, 504, 505, 506, 511, 512, 513,
 )
 
 
@@ -677,6 +685,7 @@
         v=low,
         soft=high,
         soft_low=low,
+        soft_acc=pltpu.VMEM((2 * SLOTS, D), F32),
         ctx=pltpu.VMEM((2, WIDE, IMG_GROUP * WIDE), BF16),
         factor=high,
         rel=high,
@@ -705,13 +714,19 @@
         self.at = dict(x=head // 2, c=head % 2, h=dp // 4, l=dp // 2 % 2, y=dp % 2)
 
     def count(self, axis):
-        return self.far if axis == "h" else 2
+        return dict(h=self.far, z=2 * self.far, d=4).get(axis, 2)
 
     def peer(self, axis, step):
+        if axis in "zd":
+            one, two = "hl" if axis == "z" else "xy"
+            return {one: self.next(one, step // 2), two: self.next(two, step % 2)}
+        return {axis: self.next(axis, step)}
+
+    def next(self, axis, step):
         return lax.rem(self.at[axis] + step, self.count(axis))
 
     def device(self, axis, step):
-        at = {**self.at, axis: self.peer(axis, step)}
+        at = {**self.at, **self.peer(axis, step)}
         return (at["h"] * 4 + at["l"] * 2 + at["y"], at["x"] * 2 + at["c"])
 
     def steps(self, axis, do):
@@ -769,6 +784,7 @@
 
     def region(self, blocks, slot, whole, **at):
         at = {**self.at, **at}
+        whole = whole.replace("z", "hl").replace("d", "xy")
         place = [slice(None) if axis in whole else at[axis] for axis in AXES]
         return blocks.at[(*place, slot)]
 
@@ -780,40 +796,47 @@
     def start(self, slot, i, j):
         path, links = AG_ROUTES[slot], self.links
 
-        def along(**at):
-            part = links.region(self.w, slot, path[: max(i, 0)], **at)
-            sems = [s.at[slot, j] for s in self.sems]
-            links.steps(
-                path[j],
-                lambda step: links.copy(part, part, *sems, links.device(path[j], step)).start(),
-            )
+        def along(whole, at):
+            part = links.region(self.w, slot, whole, **at)
+
+            def go(step):
+                sems = [s.at[slot, j, (step - 1) % WAYS] for s in self.sems]
+                links.copy(part, part, *sems, links.device(path[j], step)).start()
+
+            links.steps(path[j], go)
 
         if i < 0:
-            along()
+            along("", {})
+        elif path[i] == "z" and i == 0:
+            along("z", {})
         else:
-            links.steps(path[i], lambda step: along(**{path[i]: links.peer(path[i], step)}))
-
-    def descriptor(self, slot, j):
-        path = AG_ROUTES[slot]
-        at = {"h": pl.ds(0, self.links.far - 1)} if path[j] == "h" else {}
-        part = self.links.region(self.w, slot, path[:j], **at)
-        sems = [s.at[slot, j] for s in self.sems]
-        return self.links.copy(part, part, *sems, self.links.device(path[j], 1))
+            links.steps(path[i], lambda step: along(path[:i], links.peer(path[i], step)))
+
+    def waits(self, slot, j, wait):
+        path, links = AG_ROUTES[slot], self.links
+
+        def one(step):
+            part = links.region(self.w, slot, path[:j], **links.peer(path[j], step))
+            sems = [s.at[slot, j, (step - 1) % WAYS] for s in self.sems]
+            wait(links.copy(part, part, *sems, links.device(path[j], step)))
+
+        links.steps(path[j], one)
 
     def arrive(self, slot, j):
-        self.descriptor(slot, j).wait_recv()
+        self.waits(slot, j, lambda copy: copy.wait_recv())
 
     def sent(self):
-        for slot in range(MATS):
-            for j in range(len(AXES)):
-                self.descriptor(slot, j).wait_send()
+        for slot, path in enumerate(AG_ROUTES):
+            for j in range(len(path)):
+                self.waits(slot, j, lambda copy: copy.wait_send())
 
     def steps(self):
-        for slot in range(MATS):
-            for j in range(len(AXES)):
+        for slot, path in enumerate(AG_ROUTES):
+            for j in range(len(path)):
                 for i in range(-1, j):
-                    yield functools.partial(self.start, slot, i, j)
-            for j in range(len(AXES)):
+                    if path[0] != "z" or j == 0 or i >= 0:
+                        yield functools.partial(self.start, slot, i, j)
+            for j in range(len(path)):
                 yield functools.partial(self.arrive, slot, j)
 
 
@@ -825,25 +848,33 @@
     def box(self, slot, j):
         return self.boxes[slot * len(AXES) + j - 1]
 
+    def merged(self, slot, j):
+        path = RS_ROUTES[slot]
+        return path[-1] == "z" and j == len(path) - 1
+
     def start(self, slot, i, j):
         path, links = RS_ROUTES[slot], self.links
         first = sum(links.count(a) - 1 for a in path[:i]) - 1
-        sems = self.sems[0].at[slot, i], self.sems[1].at[slot, j - 1]
+        skip = first + 1 if path[-1] == "z" and j == len(path) else 0
 
         def go(step):
-            at = {path[i]: links.peer(path[i], step)}
-            into = self.box(slot, j).at[first + step]
+            entry = first + step - skip
+            sems = (
+                self.sems[0].at[slot, i, (first + step) % ENTRIES],
+                self.sems[1].at[slot, j - 1, entry % ENTRIES],
+            )
+            into = self.box(slot, j).at[entry]
             device = links.device(path[i], step)
 
-            def part(into, **more):
-                src = links.region(self.g, slot, path[j + 1 :], **at, **more)
+            def part(into, whole, more):
+                src = links.region(self.g, slot, whole, **links.peer(path[i], step), **more)
                 links.copy(src, into, *sems, device).start()
 
-            if j == len(AXES):
-                part(into)
+            if j == len(path) or self.merged(slot, j):
+                part(into, path[j:], {})
             else:
                 links.steps(
-                    path[j], lambda n: part(into.at[n - 1], **{path[j]: links.peer(path[j], n)})
+                    path[j], lambda n: part(into.at[n - 1], path[j + 1 :], links.peer(path[j], n))
                 )
 
         links.steps(path[i], go)
@@ -851,7 +882,8 @@
     def add(self, slot, j):
         path, links = RS_ROUTES[slot], self.links
         box = self.box(slot, j)
-        self.arrived(slot, j).wait_recv()
+        for e in range(box.shape[0]):
+            self.entry(slot, j, e, (0, j - 1), box.at[e]).wait_recv()
 
         def total(own, pick):
             value = own[...].astype(F32)
@@ -859,37 +891,45 @@
                 value = value + pick(box.at[e])[...].astype(F32)
             return value
 
-        if j == len(AXES):
+        if j == len(path):
             own = links.region(self.g, slot, "")
             self.total[SLOT_OF.index(slot)] = total(own, lambda b: b)
             return
 
         def one(n):
-            own = links.region(self.g, slot, path[j + 1 :], **{path[j]: links.peer(path[j], n)})
+            own = links.region(self.g, slot, path[j + 1 :], **links.peer(path[j], n))
             own[...] = total(own, lambda b: b.at[n - 1]).astype(BF16)
 
-        links.steps(path[j], one)
-
-    def arrived(self, slot, j):
-        box = self.box(slot, j)
-        sems = self.sems[0].at[slot, j - 1], self.sems[1].at[slot, j - 1]
-        return self.links.copy(box, box, *sems, self.links.device("c", 1))
+        if self.merged(slot, j):
+            own = links.region(self.g, slot, "z")
+            own[...] = total(own, lambda b: b).astype(BF16)
+        else:
+            links.steps(path[j], one)
+
+    def entry(self, slot, j, e, places, ref):
+        sems = [s.at[slot, n, e % ENTRIES] for s, n in zip(self.sems, places)]
+        return self.links.copy(ref, ref, *sems, self.links.device("c", 1))
 
     def sent(self):
-        for slot in range(MATS):
-            path = RS_ROUTES[slot]
-            for i in range(len(AXES)):
-                at = {"h": pl.ds(0, self.links.far - 1)} if path[i] == "h" else {}
-                part = self.links.region(self.g, slot, path[i + 1 :], **at)
-                sems = [s.at[slot, i] for s in self.sems]
-                self.links.copy(part, part, *sems, self.links.device(path[i], 1)).wait_send()
+        for slot, path in enumerate(RS_ROUTES):
+            for i in range(len(path)):
+                first = sum(self.links.count(a) - 1 for a in path[:i]) - 1
+
+                def one(step):
+                    part = self.links.region(
+                        self.g, slot, path[i + 1 :], **self.links.peer(path[i], step)
+                    )
+                    self.entry(slot, i, first + step, (i, 0), part).wait_send()
+
+                self.links.steps(path[i], one)
 
     def steps(self):
-        for slot in range(MATS):
-            for i in range(len(AXES)):
-                for j in range(i + 1, len(AXES) + 1):
-                    yield functools.partial(self.start, slot, i, j)
-            for j in range(1, len(AXES) + 1):
+        for slot, path in enumerate(RS_ROUTES):
+            for i in range(len(path)):
+                for j in range(i + 1, len(path) + 1):
+                    if not (path[-1] == "z" and j == len(path) and i + 1 < len(path)):
+                        yield functools.partial(self.start, slot, i, j)
+            for j in range(1, len(path) + 1):
                 yield functools.partial(self.add, slot, j)
 
 
@@ -1082,28 +1122,20 @@
         mass = jnp.sum(row, axis=0, keepdims=True)
         self.sq_share.start(jnp.concatenate([sums, mass], axis=0))
 
-    def apply(self):
+    def rates(self):
         total = self.sq_share.total()
         mean = total[1:2] * (1.0 / (D * lax.axis_size(HEAD)))
         rms = jnp.sqrt(total[0:1] * mean * (1.0 / (D * D)))
         rate = STEP_RATE * jnp.sqrt(mean) / jnp.maximum(1.0, rms)
-        for k in range(self.lo, self.hi):
-            new = self.weights[k] - rate[:, k : k + 1] * self.upd[k]
-            self.new_weights[k] = new
-            self.copy[k] = new.astype(BF16)
-            self.new_ema[k] = AVERAGE_KEEP * self.ema[k] + (1.0 - AVERAGE_KEEP) * new
-        self.rms[self.lo // 4 : self.lo // 4 + 1, :] = rms
+        lanes = lax.broadcasted_iota(jnp.int32, (1, LANES), 1)
+        mine = (lanes >= self.lo) & (lanes < self.hi)
+        self.clip[0:1, :] = jnp.where(mine, rms, self.clip[0:1, :])
+        self.clip[1:2, :] = jnp.where(mine, rate, self.clip[1:2, :])
 
 
 class SmallStep:
     def __init__(self, refs):
         self.__dict__.update(refs)
-
-    def clips(self):
-        lanes = lax.broadcasted_iota(jnp.int32, (1, LANES), 1)
-        clip = jnp.where(lanes < EARLY, self.rms[0:1, :], self.rms[1:2, :])
-        clip = jnp.where(lanes < MATS, clip, self.small_clip[...])
-        self.clip[...] = clip[:, 0 : self.clip.shape[1]]
 
     def small_step(self):
         count, full = self.small.shape[0], self.full
@@ -1121,7 +1153,9 @@
         r = lax.broadcasted_iota(jnp.int32, (count, LANES), 0)
         c = lax.broadcasted_iota(jnp.int32, (count, LANES), 1)
         picked = jnp.where(c == r + MATS, rms, 0.0)
-        self.small_clip[...] = jnp.sum(picked, axis=0, keepdims=True)
+        small = jnp.sum(picked, axis=0, keepdims=True)
+        lanes = lax.broadcasted_iota(jnp.int32, (1, LANES), 1)
+        self.clip[0:1, :] = jnp.where(lanes < MATS, self.clip[0:1, :], small)
 
 
 class Inputs(NamedTuple):
@@ -1132,7 +1166,6 @@
     weights: Any
     row_state: Any
     col_state: Any
-    ema: Any
     small: Any
     small_state: Any
     small_ema: Any
@@ -1144,13 +1177,11 @@
     wg: Any
     new_rows: Any
     new_cols: Any
-    new_weights: Any
-    copy: Any
-    new_ema: Any
     small_grads: Any
     new_small_state: Any
     new_small: Any
     new_small_ema: Any
+    upd: Any
     clip: Any
 
 
@@ -1158,9 +1189,18 @@
     for path in RS_ROUTES:
         for j in range(1, len(AXES) + 1):
             entries = sum(links.count(a) - 1 for a in path[:j])
-            ways = [links.count(path[j]) - 1] if j < len(AXES) else []
-            rest = [links.count(a) for a in AXES if a in path[j + 1 :]]
-            yield pltpu.VMEM((entries, *ways, *rest, *block), BF16)
+            if j > len(path):
+                shape = (1, SLOTS, LANES)
+            elif j == len(path):
+                first = links.count("z") - 1 if path[-1] == "z" else entries
+                shape = (first, *block)
+            elif path[-1] == "z" and j == len(path) - 1:
+                shape = (entries, links.count("h"), links.count("l"), *block)
+            else:
+                rest = path[j + 1 :].replace("z", "hl").replace("d", "xy")
+                rest = [links.count(a) for a in AXES if a in rest]
+                shape = (entries, links.count(path[j]) - 1, *rest, *block)
+            yield pltpu.VMEM(shape, BF16)
 
 
 def shared_of(weights, parts, heads):
@@ -1190,13 +1230,10 @@
         row_box=f(2, heads, SLOTS, LANES),
         col_box=f(2, parts, SLOTS, LANES),
         sq_box=f(2, parts * heads, 2, LANES),
-        upd=f(MATS, *block),
-        small_clip=f(1, LANES),
-        rms=f(2, LANES),
-        ag_send=dma((MATS, len(AXES))),
-        ag_recv=dma((MATS, len(AXES))),
-        rs_send=dma((MATS, len(AXES))),
-        rs_recv=dma((MATS, len(AXES))),
+        ag_send=dma((MATS, len(AXES), WAYS)),
+        ag_recv=dma((MATS, len(AXES), WAYS)),
+        rs_send=dma((MATS, len(AXES), ENTRIES)),
+        rs_recv=dma((MATS, len(AXES), ENTRIES)),
         small_send=dma((7,)),
         small_recv=dma((7,)),
         out_send=dma((3,)),
@@ -1243,7 +1280,7 @@
     boxes = refs[len(names) :]
     links = Links()
     links.signal()
-    for one in (fetch.weights, *fetch[0:2], fetch.small, *fetch[2:4], *fetch[5:8], *fetch[9:]):
+    for one in (fetch.weights, *fetch[0:2], fetch.small, *fetch[2:4], *fetch[5:7], *fetch[8:]):
         one.start()
     r.out_own = r.out_rows.at[lax.axis_index(HEAD)]
     r.in_own = r.in_rows.at[lax.axis_index(HEAD)]
@@ -1270,30 +1307,50 @@
     step = SmallStep(vars(r))
 
     def round_weights():
+        r.clip[...] = jnp.zeros(r.clip.shape, F32)
         for k in range(MATS):
             mine = links.region(r.w, SLOT_OF[k], "")
             mine[...] = r.weights[k].astype(BF16)
 
     ops = [*gather.steps(), *scatter.steps()]
     ops += [then(fetch.weights.wait, round_weights), links.meet]
-    ops += [
-        then(fetch.small.wait, fetch.cls.wait, fetch.img.wait, blk.setup),
-        then(fetch.tokens.wait, blk.read_tokens),
-        blk.norm_one,
-        then(fetch.cot.wait, blk.read_cotangent),
-    ]
-    ops += [functools.partial(blk.project, k) for k in range(3)]
-    ops += [blk.softmax, blk.contexts, blk.fill_window]
-    ops += [functools.partial(blk.window_sum, c) for c in range(D // LANES)]
-    ops += [blk.mix, blk.norm_two]
-    for i in range(4):
-        ops += [functools.partial(blk.hidden_block, i), functools.partial(blk.hidden_grads, i)]
-    ops += [blk.finish_out, blk.back_two, blk.grad_proj, blk.back_heads, blk.back_query_key]
-    ops += [functools.partial(blk.grad_of, k) for k in range(2)]
-    ops += [functools.partial(blk.back_window, c) for c in range(D // LANES)]
-    ops += [blk.back_value]
-    ops += [functools.partial(blk.window_taps, c) for c in range(D // LANES)]
-    ops += [blk.back_project, blk.back_one, blk.back_position, blk.position_taps, blk.finish_in]
+    ops += [then(fetch.small.wait, fetch.cls.wait, fetch.img.wait, blk.setup)]
+    ops += [fetch.tokens.wait, fetch.cot.wait]
+
+    def each(step, *ranges):
+        for place in itertools.product(*map(range, ranges)):
+            ops.append(functools.partial(step, *place))
+
+    each(blk.read_tokens, PIECES)
+    each(blk.position, D // LANES)
+    each(blk.norm_one, PIECES)
+    ops.append(blk.turn_one)
+    each(blk.read_cotangent, PIECES)
+    ops.append(blk.turn_cotangent)
+    each(blk.project, 3, 2)
+    ops += [blk.key_tops, blk.key_powers, blk.key_shares]
+    each(blk.contexts, 2)
+    ops.append(blk.fill_window)
+    each(blk.window_sum, D // LANES)
+    ops.append(blk.mix)
+    each(blk.attend, 2)
+    each(blk.norm_two, PIECES)
+    ops.append(blk.turn_two)
+    each(blk.hidden_in, 4)
+    each(blk.hidden_out, 4)
+    each(blk.grad_down, 4)
+    each(blk.grad_up, 4)
+    each(blk.add_down, 4)
+    each(blk.add_back, 4)
+    ops += [blk.finish_out, blk.back_two, blk.grad_proj, blk.back_mixed, blk.back_fill]
+    each(blk.back_heads, 2)
+    ops += [blk.back_inner, blk.back_query_key]
+    each(blk.back_window, D // LANES)
+    ops.append(blk.back_value)
+    each(blk.grad_of, 3)
+    each(blk.window_taps, D // LANES)
+    each(blk.back_project, 2)
+    ops += [blk.back_one, blk.back_position, blk.position_taps, blk.finish_in]
     for rows, done in ((out_rows, store.out), (in_rows, store.grad_in)):
         ops += [functools.partial(rows.tick, stage) for stage in range(2)]
         ops += [then(functools.partial(rows.tick, 2), done.start)]
@@ -1311,12 +1368,10 @@
         opts[1].squares,
         then(store.wg.start, opts[0].squares),
         then(fetch.row_state.wait, fetch.col_state.wait, opts[1].scale),
-        then(opts[0].scale, store.new_rows.start, store.new_cols.start),
-        then(fetch.ema.wait, opts[1].apply),
-        then(
-            opts[0].apply, store.new_weights.start, store.copy.start, store.new_ema.start
-        ),
-        then(step.clips, store.clip.start),
+        then(opts[0].scale, store.upd.start, store.new_rows.start, store.new_cols.start),
+        opts[1].rates,
+        opts[0].rates,
+        store.clip.start,
     ]
     for i in ORDER:
         ops[i]()
@@ -1326,16 +1381,32 @@
         one.wait()
 
 
-def finish_kernel(count, *refs):
+PASSED = 9
+
+
+def finish_kernel(*refs):
+    count = PASSED + 4
     ins, outs, held = refs[:count], refs[count : 2 * count], refs[2 * count : 3 * count]
-    took, gave = refs[3 * count :]
+    new_weights, low, new_ema, clips, took, gave = refs[3 * count :]
+    upd, clip, weights, ema = held[PASSED:]
     come = [pltpu.make_async_copy(a, b, took.at[i]) for i, (a, b) in enumerate(zip(ins, held))]
-    leave = [pltpu.make_async_copy(a, b, gave.at[i]) for i, (a, b) in enumerate(zip(held, outs))]
-    for one in come:
+    leave = [*held[:5], new_weights, low, new_ema, *held[5:PASSED], clips]
+    leave = [pltpu.make_async_copy(a, b, gave.at[i]) for i, (a, b) in enumerate(zip(leave, outs))]
+    for one in come[::-1]:
         one.start()
-    for one, other in zip(come, leave):
+    for one in come[PASSED:]:
         one.wait()
-        other.start()
+    for k in range(weights.shape[0]):
+        new = weights[k] - clip[1:2, k : k + 1] * upd[k]
+        new_weights[k] = new
+        low[k] = new.astype(BF16)
+        new_ema[k] = AVERAGE_KEEP * ema[k] + (1.0 - AVERAGE_KEEP) * new
+    clips[...] = clip[0:1, 0 : clips.shape[1]]
+    for i in (5, 6, 7, count - 1):
+        leave[i].start()
+    for i in range(PASSED):
+        come[i].wait()
+        leave[i if i < 5 else i + 3].start()
     for one in leave:
         one.wait()
 
@@ -1361,21 +1432,14 @@
         return jax.ShapeDtypeStruct(x.shape, dtype or x.dtype)
 
     clips = weights.shape[0] + small_params.shape[0]
-    outs = (
-        like(tokens),
-        like(tokens),
-        like(weights),
-        like(row_state),
-        like(col_state),
-        like(weights),
-        like(weights, BF16),
-        like(weights),
-        like(small_params),
-        like(small_params),
-        like(small_params),
-        like(small_params),
-        jax.ShapeDtypeStruct((1, clips), F32),
+    passed = (
+        *[like(x) for x in (tokens, tokens, weights, row_state, col_state)],
+        *[like(small_params)] * 4,
     )
+    middle = (*passed, like(weights), jax.ShapeDtypeStruct((2, LANES), F32))
+    stepped = (like(weights), like(weights, BF16), like(weights))
+    last = jax.ShapeDtypeStruct((1, clips), F32)
+    outs = (*passed[:5], *stepped, *passed[5:], last)
     args = Inputs(
         crop_class,
         crop_image,
@@ -1384,20 +1448,19 @@
         weights,
         row_state,
         col_state,
-        weights_ema,
         small_params,
         small_state,
         small_ema,
     )
     staged = [pltpu.SMEM(x.shape, x.dtype) for x in args[:2]]
-    staged += [pltpu.VMEM(x.shape, x.dtype) for x in (*args[2:], *outs)]
+    staged += [pltpu.VMEM(x.shape, x.dtype) for x in (*args[2:], *middle)]
     names = (*shared, *own, *Inputs._fields, *Outputs._fields)
     far = pl.BlockSpec(memory_space=pltpu.HBM)
     res = pl.pallas_call(
         functools.partial(block_kernel, names),
-        out_shape=outs,
+        out_shape=middle,
         in_specs=[far] * len(args),
-        out_specs=(far,) * len(outs),
+        out_specs=(far,) * len(middle),
         scratch_shapes=[
             *shared.values(),
             *own.values(),
@@ -1409,19 +1472,17 @@
         ),
         name="block",
     )(*args)
+    ins = (*res, weights, weights_ema)
+    kept = [pltpu.VMEM(x.shape, x.dtype) for x in (*middle, weights, weights_ema, *stepped, last)]
     res = pl.pallas_call(
-        functools.partial(finish_kernel, len(outs)),
+        finish_kernel,
         out_shape=outs,
-        in_specs=[far] * len(outs),
+        in_specs=[far] * len(ins),
         out_specs=(far,) * len(outs),
-        scratch_shapes=[
-            *[pltpu.VMEM(x.shape, x.dtype) for x in outs],
-            pltpu.SemaphoreType.DMA((len(outs),)),
-            pltpu.SemaphoreType.DMA((len(outs),)),
-        ],
+        scratch_shapes=[*kept, *[pltpu.SemaphoreType.DMA((len(outs),))] * 2],
         compiler_params=pltpu.CompilerParams(vmem_limit_bytes=63 << 20),
         name="finish",
-    )(*res)
+    )(*ins)
     return (*res[:-1], res[-1].reshape(clips))
 
 

time: 87.3 us -> 93.5 us (1.071)
  Pallas kernels: 86.3 us -> 92.5 us
    pallas_call x2, Pallas kernels: 86.3 us -> 92.5 us  [the longest x1 88.3 us: local(): pl.pallas_call(functools.partial(block_kernel, names), out_shape=middle,...]
where the time goes in v10:
time: 93.5 us; the launch traced here: 93.4 us
  Pallas kernels  92.5 us (99%)
    pallas_call x1, Pallas kernels, local(): pl.pallas_call(functools.partial(block_kernel, names), out_shape=middle,...  88.3 us
    pallas_call x1, Pallas kernels, local(): pl.pallas_call(finish_kernel, out_shape=outs, in_specs=[far] * len(ins),...  4.29 us

profile of v10, /device:TPU:0, one launch (start us, length us, event | category | flops | bytes accessed | tf_op | source)
XLA Modules:
  0.0 93.4 jit_solution(842032130584268118)
XLA Ops:
  0.6 88.3 %block.1 = (bf16[1176,512]{1,0:T(8,128)(2,1)}, bf16[1176,512]{1,0:T(8,128)(2,1)}, f32[12,64,128]{2,1,0:T(8,128)}, f32[12,64]{1,0:T(8,128)}, f32[12,128]{1,0:T(8,...) custom-call(s32[4,6]{1,0:T(4,128)} %refs_0_.1, ...), custom_call_target="tpu_custom_call" | custom-call | tf_op jit(solution)/shard_map/block/pallas_call | solution.py:1459
  88.9 4.3 %finish.1 = (bf16[1176,512]{1,0:T(8,128)(2,1)}, bf16[1176,512]{1,0:T(8,128)(2,1)}, f32[12,64,128]{2,1,0:T(8,128)}, f32[12,64]{1,0:T(8,128)}, f32[12,128]{1,0:T(8...) custom-call(bf16[1176,512]{1,0:T(8,128)(2,1)} %get-tuple-element.37., ...), custom_call_target="tpu_custom_call" | custom-call | tf_op jit(solution)/shard_map/finish/pallas_call | solution.py:1477

commit v11 on v10

--- a/solution.py
+++ b/solution.py
@@ -617,38 +617,39 @@
 MATS = len(SLOT_OF)
 EARLY = 4
 AXES = "xchly"
-WAYS, ENTRIES = 3, 6
 HEAD_ROWS = 320
 SMALL_ROWS = 72
-AG_ROUTES = ("zyxc", "zyxc", "zxyc", "zxyc", "zxyc", "zyxc", "yhxlc", "xylhc", "xhylc", "hlyxc", "hxlyc", "hlyxc")
-RS_ROUTES = ("cyxz", "cxyz", "cyxz", "cyxz", "cxhyl", "cyhlx", "cxlhy", "cyhlx", "cylxh", "clyxh", "cyxhl", "chlxy")
+AG_ROUTES = ("zxyc", "zxyc", "zyxc", "zyxc", "zxyc", "zyxc", "yhxlc", "yxhlc", "hlxyc", "lhyxc", "hxlyc", "lyhxc")
+RS_ROUTES = ("clyhx", "cxlyh", "cyhlx", "cyxlh", "clxhy", "cxhyl", "cylhx", "clyhx", "cxylh", "cylxh", "clxyh", "cylhx")
 ORDER = (
-    390, 392, 393, 399, 397, 394, 395, 391, 11, 66, 129, 152, 136, 76, 156, 106, 132, 116, 109, 169,
-    396, 22, 69, 87, 96, 398, 403, 401, 72, 400, 147, 412, 0, 414, 172, 411, 127, 81, 77, 70,
-    121, 110, 117, 410, 73, 86, 176, 402, 33, 406, 404, 407, 18, 12, 15, 13, 149, 408, 44, 405,
-    409, 413, 415, 29, 24, 23, 26, 101, 97, 88, 167, 55, 7, 4, 1, 2, 89, 126, 113, 19,
-    16, 14, 67, 40, 37, 35, 90, 108, 112, 30, 27, 25, 34, 68, 102, 98, 51, 48, 91, 46,
-    94, 45, 8, 5, 62, 59, 146, 56, 141, 137, 128, 20, 17, 3, 166, 107, 130, 41, 38, 36,
-    57, 92, 21, 418, 31, 28, 82, 78, 103, 99, 419, 74, 422, 423, 52, 133, 49, 47, 424, 71,
-    95, 142, 138, 32, 420, 421, 161, 157, 427, 148, 9, 6, 150, 131, 430, 63, 60, 58, 153, 181,
-    168, 177, 428, 431, 170, 93, 134, 122, 118, 111, 114, 429, 10, 417, 42, 39, 426, 83, 75, 79,
-    162, 158, 154, 173, 416, 425, 53, 50, 151, 182, 174, 171, 178, 43, 432, 64, 61, 143, 135, 434,
-    139, 433, 437, 436, 435, 54, 104, 438, 123, 119, 115, 100, 439, 65, 441, 84, 80, 445, 449, 252,
-    250, 251, 163, 155, 461, 253, 254, 159, 105, 457, 144, 140, 183, 175, 440, 453, 230, 85, 232, 231,
-    442, 265, 256, 258, 255, 234, 233, 124, 120, 179, 446, 450, 293, 290, 291, 292, 145, 458, 257, 294,
-    245, 237, 235, 454, 270, 271, 274, 272, 462, 273, 164, 160, 125, 443, 305, 297, 296, 298, 295, 236,
-    184, 180, 447, 455, 311, 314, 313, 312, 310, 285, 276, 459, 277, 165, 463, 278, 451, 332, 334, 266,
-    261, 260, 333, 330, 331, 275, 185, 444, 259, 448, 460, 325, 318, 317, 316, 315, 246, 456, 352, 351,
-    353, 350, 345, 335, 238, 465, 338, 354, 492, 452, 336, 373, 306, 372, 464, 370, 466, 337, 301, 374,
-    371, 468, 365, 358, 355, 286, 300, 469, 357, 281, 483, 299, 485, 267, 356, 385, 467, 346, 339, 262,
-    219, 221, 220, 482, 263, 471, 326, 340, 341, 375, 477, 319, 226, 222, 476, 366, 320, 223, 470, 360,
-    268, 264, 376, 474, 475, 347, 342, 343, 307, 302, 303, 478, 361, 378, 481, 208, 210, 209, 359, 279,
-    472, 473, 327, 322, 323, 377, 480, 197, 198, 199, 321, 241, 227, 224, 269, 479, 215, 211, 212, 348,
-    344, 187, 186, 386, 381, 188, 484, 308, 379, 493, 487, 304, 239, 486, 204, 200, 367, 488, 328, 287,
-    362, 193, 189, 380, 490, 201, 324, 190, 498, 494, 216, 363, 309, 228, 213, 282, 489, 349, 387, 283,
-    499, 491, 205, 202, 247, 243, 280, 225, 242, 368, 382, 364, 383, 194, 240, 329, 191, 217, 214, 495,
-    288, 284, 500, 388, 384, 206, 203, 369, 229, 195, 192, 289, 248, 244, 501, 389, 218, 207, 249, 507,
-    196, 508, 502, 496, 503, 509, 510, 497, 504, 505, 506, 511, 512, 513,
+    426, 428, 429, 435, 431, 434, 427, 22, 69, 76, 66, 86, 116, 109, 129, 96, 132, 87, 136, 176,
+    167, 432, 112, 172, 430, 152, 156, 147, 450, 11, 446, 448, 447, 72, 92, 433, 0, 439, 81, 77,
+    70, 436, 437, 101, 97, 88, 438, 440, 33, 442, 441, 29, 24, 23, 26, 444, 73, 443, 55, 445,
+    449, 451, 18, 12, 15, 13, 102, 98, 94, 44, 7, 4, 2, 1, 107, 67, 30, 27, 25, 93,
+    40, 37, 35, 34, 68, 126, 90, 19, 14, 16, 149, 62, 57, 56, 59, 106, 166, 91, 8, 5,
+    3, 51, 45, 48, 46, 141, 130, 128, 137, 31, 28, 41, 38, 82, 78, 36, 74, 89, 181, 177,
+    168, 146, 20, 17, 32, 456, 71, 121, 117, 113, 457, 463, 108, 127, 466, 63, 60, 58, 169, 464,
+    21, 454, 170, 465, 467, 9, 6, 52, 110, 133, 47, 49, 455, 103, 99, 95, 458, 122, 118, 111,
+    459, 161, 148, 42, 39, 157, 114, 460, 150, 173, 153, 142, 138, 131, 134, 10, 452, 83, 75, 79,
+    453, 182, 178, 462, 174, 461, 64, 61, 43, 171, 468, 104, 100, 53, 50, 470, 469, 472, 473, 123,
+    119, 115, 475, 65, 162, 151, 158, 154, 471, 143, 139, 135, 474, 105, 84, 80, 476, 54, 477, 481,
+    489, 266, 267, 268, 485, 289, 288, 287, 286, 85, 290, 269, 270, 183, 175, 179, 497, 163, 155, 159,
+    493, 124, 120, 478, 281, 271, 144, 140, 482, 494, 486, 328, 327, 326, 329, 330, 272, 301, 293, 292,
+    294, 291, 490, 306, 307, 309, 308, 310, 125, 498, 273, 145, 479, 184, 164, 160, 274, 180, 483, 341,
+    334, 333, 491, 348, 347, 349, 346, 282, 331, 350, 275, 321, 314, 312, 313, 276, 311, 277, 499, 495,
+    165, 487, 368, 370, 369, 366, 367, 185, 480, 332, 484, 361, 352, 353, 354, 351, 496, 302, 296, 492,
+    297, 390, 389, 386, 388, 387, 381, 374, 372, 373, 371, 488, 406, 408, 283, 407, 278, 409, 410, 501,
+    342, 336, 337, 335, 528, 279, 500, 502, 322, 315, 401, 503, 421, 411, 412, 247, 249, 248, 250, 246,
+    393, 413, 414, 504, 317, 505, 316, 519, 391, 521, 518, 506, 261, 254, 362, 356, 357, 355, 252, 284,
+    253, 323, 251, 318, 382, 375, 511, 319, 280, 507, 343, 338, 513, 339, 377, 512, 422, 415, 402, 397,
+    295, 508, 324, 320, 383, 378, 379, 509, 417, 516, 209, 208, 206, 207, 210, 416, 515, 344, 340, 187,
+    186, 188, 376, 190, 189, 392, 396, 395, 510, 514, 517, 423, 418, 363, 226, 228, 419, 230, 227, 229,
+    520, 221, 211, 529, 522, 213, 212, 358, 325, 523, 359, 201, 192, 303, 298, 299, 524, 345, 214, 384,
+    191, 241, 231, 262, 255, 526, 256, 285, 534, 257, 403, 398, 233, 530, 424, 364, 360, 420, 193, 232,
+    399, 234, 525, 222, 215, 304, 535, 380, 527, 216, 531, 217, 242, 235, 202, 195, 196, 197, 404, 263,
+    236, 365, 259, 400, 425, 223, 218, 219, 258, 237, 385, 536, 300, 203, 198, 194, 199, 243, 238, 224,
+    220, 394, 264, 260, 537, 305, 239, 204, 200, 244, 240, 405, 543, 225, 265, 532, 205, 245, 544, 538,
+    533, 545, 539, 546, 540, 547, 541, 542, 548, 549,
 )
 
 
@@ -722,6 +723,9 @@
             return {one: self.next(one, step // 2), two: self.next(two, step % 2)}
         return {axis: self.next(axis, step)}
 
+    def other(self):
+        return self.device("c", 1)
+
     def next(self, axis, step):
         return lax.rem(self.at[axis] + step, self.count(axis))
 
@@ -790,8 +794,8 @@
 
 
 class Gather:
-    def __init__(self, links, w, send, recv):
-        self.links, self.w, self.sems = links, w, (send, recv)
+    def __init__(self, links, w, sizes, send, recv):
+        self.links, self.w, self.sizes, self.send, self.recv = links, w, sizes, send, recv
 
     def start(self, slot, i, j):
         path, links = AG_ROUTES[slot], self.links
@@ -800,7 +804,7 @@
             part = links.region(self.w, slot, whole, **at)
 
             def go(step):
-                sems = [s.at[slot, j, (step - 1) % WAYS] for s in self.sems]
+                sems = self.send.at[slot], self.recv.at[slot, j]
                 links.copy(part, part, *sems, links.device(path[j], step)).start()
 
             links.steps(path[j], go)
@@ -812,23 +816,16 @@
         else:
             links.steps(path[i], lambda step: along(path[:i], links.peer(path[i], step)))
 
-    def waits(self, slot, j, wait):
+    def arrive(self, slot, j):
         path, links = AG_ROUTES[slot], self.links
-
-        def one(step):
-            part = links.region(self.w, slot, path[:j], **links.peer(path[j], step))
-            sems = [s.at[slot, j, (step - 1) % WAYS] for s in self.sems]
-            wait(links.copy(part, part, *sems, links.device(path[j], step)))
-
-        links.steps(path[j], one)
-
-    def arrive(self, slot, j):
-        self.waits(slot, j, lambda copy: copy.wait_recv())
+        blocks = (links.count(path[j]) - 1) * math.prod(links.count(a) for a in path[:j])
+        size = self.sizes.at[pl.ds(0, blocks)]
+        links.copy(size, size, self.send.at[slot], self.recv.at[slot, j], links.other()).wait_recv()
 
     def sent(self):
-        for slot, path in enumerate(AG_ROUTES):
-            for j in range(len(path)):
-                self.waits(slot, j, lambda copy: copy.wait_send())
+        for slot in range(MATS):
+            sems = self.send.at[slot], self.recv.at[slot, 0]
+            self.links.copy(self.sizes, self.sizes, *sems, self.links.other()).wait_send()
 
     def steps(self):
         for slot, path in enumerate(AG_ROUTES):
@@ -841,9 +838,9 @@
 
 
 class Scatter:
-    def __init__(self, links, g, boxes, total, send, recv):
+    def __init__(self, links, g, boxes, total, sizes, send, recv):
         self.links, self.g, self.boxes, self.total = links, g, boxes, total
-        self.sems = (send, recv)
+        self.sizes, self.send, self.recv = sizes, send, recv
 
     def box(self, slot, j):
         return self.boxes[slot * len(AXES) + j - 1]
@@ -859,10 +856,7 @@
 
         def go(step):
             entry = first + step - skip
-            sems = (
-                self.sems[0].at[slot, i, (first + step) % ENTRIES],
-                self.sems[1].at[slot, j - 1, entry % ENTRIES],
-            )
+            sems = self.send.at[slot], self.recv.at[slot, j - 1]
             into = self.box(slot, j).at[entry]
             device = links.device(path[i], step)
 
@@ -882,8 +876,8 @@
     def add(self, slot, j):
         path, links = RS_ROUTES[slot], self.links
         box = self.box(slot, j)
-        for e in range(box.shape[0]):
-            self.entry(slot, j, e, (0, j - 1), box.at[e]).wait_recv()
+        sems = self.send.at[slot], self.recv.at[slot, j - 1]
+        links.copy(box, box, *sems, links.other()).wait_recv()
 
         def total(own, pick):
             value = own[...].astype(F32)
@@ -906,22 +900,10 @@
         else:
             links.steps(path[j], one)
 
-    def entry(self, slot, j, e, places, ref):
-        sems = [s.at[slot, n, e % ENTRIES] for s, n in zip(self.sems, places)]
-        return self.links.copy(ref, ref, *sems, self.links.device("c", 1))
-
     def sent(self):
-        for slot, path in enumerate(RS_ROUTES):
-            for i in range(len(path)):
-                first = sum(self.links.count(a) - 1 for a in path[:i]) - 1
-
-                def one(step):
-                    part = self.links.region(
-                        self.g, slot, path[i + 1 :], **self.links.peer(path[i], step)
-                    )
-                    self.entry(slot, i, first + step, (i, 0), part).wait_send()
-
-                self.links.steps(path[i], one)
+        for slot in range(MATS):
+            sems = self.send.at[slot], self.recv.at[slot, 0]
+            self.links.copy(self.sizes, self.sizes, *sems, self.links.other()).wait_send()
 
     def steps(self):
         for slot, path in enumerate(RS_ROUTES):
@@ -1122,20 +1104,28 @@
         mass = jnp.sum(row, axis=0, keepdims=True)
         self.sq_share.start(jnp.concatenate([sums, mass], axis=0))
 
-    def rates(self):
+    def apply(self):
         total = self.sq_share.total()
         mean = total[1:2] * (1.0 / (D * lax.axis_size(HEAD)))
         rms = jnp.sqrt(total[0:1] * mean * (1.0 / (D * D)))
         rate = STEP_RATE * jnp.sqrt(mean) / jnp.maximum(1.0, rms)
-        lanes = lax.broadcasted_iota(jnp.int32, (1, LANES), 1)
-        mine = (lanes >= self.lo) & (lanes < self.hi)
-        self.clip[0:1, :] = jnp.where(mine, rms, self.clip[0:1, :])
-        self.clip[1:2, :] = jnp.where(mine, rate, self.clip[1:2, :])
+        for k in range(self.lo, self.hi):
+            new = self.weights[k] - rate[:, k : k + 1] * self.upd[k]
+            self.new_weights[k] = new
+            self.copy[k] = new.astype(BF16)
+            self.new_ema[k] = AVERAGE_KEEP * self.ema[k] + (1.0 - AVERAGE_KEEP) * new
+        self.rms[self.lo // 4 : self.lo // 4 + 1, :] = rms
 
 
 class SmallStep:
     def __init__(self, refs):
         self.__dict__.update(refs)
+
+    def clips(self):
+        lanes = lax.broadcasted_iota(jnp.int32, (1, LANES), 1)
+        clip = jnp.where(lanes < EARLY, self.rms[0:1, :], self.rms[1:2, :])
+        clip = jnp.where(lanes < MATS, clip, self.small_clip[...])
+        self.clip[...] = clip[:, 0 : self.clip.shape[1]]
 
     def small_step(self):
         count, full = self.small.shape[0], self.full
@@ -1153,9 +1143,7 @@
         r = lax.broadcasted_iota(jnp.int32, (count, LANES), 0)
         c = lax.broadcasted_iota(jnp.int32, (count, LANES), 1)
         picked = jnp.where(c == r + MATS, rms, 0.0)
-        small = jnp.sum(picked, axis=0, keepdims=True)
-        lanes = lax.broadcasted_iota(jnp.int32, (1, LANES), 1)
-        self.clip[0:1, :] = jnp.where(lanes < MATS, self.clip[0:1, :], small)
+        self.small_clip[...] = jnp.sum(picked, axis=0, keepdims=True)
 
 
 class Inputs(NamedTuple):
@@ -1166,6 +1154,7 @@
     weights: Any
     row_state: Any
     col_state: Any
+    ema: Any
     small: Any
     small_state: Any
     small_ema: Any
@@ -1177,11 +1166,13 @@
     wg: Any
     new_rows: Any
     new_cols: Any
+    new_weights: Any
+    copy: Any
+    new_ema: Any
     small_grads: Any
     new_small_state: Any
     new_small: Any
     new_small_ema: Any
-    upd: Any
     clip: Any
 
 
@@ -1230,10 +1221,14 @@
         row_box=f(2, heads, SLOTS, LANES),
         col_box=f(2, parts, SLOTS, LANES),
         sq_box=f(2, parts * heads, 2, LANES),
-        ag_send=dma((MATS, len(AXES), WAYS)),
-        ag_recv=dma((MATS, len(AXES), WAYS)),
-        rs_send=dma((MATS, len(AXES), ENTRIES)),
-        rs_recv=dma((MATS, len(AXES), ENTRIES)),
+        upd=f(MATS, *block),
+        small_clip=f(1, LANES),
+        rms=f(2, LANES),
+        sizes=pltpu.VMEM((parts * heads - 1, *block), BF16),
+        ag_send=dma((MATS,)),
+        ag_recv=dma((MATS, len(AXES))),
+        rs_send=dma((MATS,)),
+        rs_recv=dma((MATS, len(AXES))),
         small_send=dma((7,)),
         small_recv=dma((7,)),
         out_send=dma((3,)),
@@ -1280,14 +1275,14 @@
     boxes = refs[len(names) :]
     links = Links()
     links.signal()
-    for one in (fetch.weights, *fetch[0:2], fetch.small, *fetch[2:4], *fetch[5:7], *fetch[8:]):
+    for one in (fetch.weights, *fetch[0:2], fetch.small, *fetch[2:4], *fetch[5:8], *fetch[9:]):
         one.start()
     r.out_own = r.out_rows.at[lax.axis_index(HEAD)]
     r.in_own = r.in_rows.at[lax.axis_index(HEAD)]
     own = r.cls.shape[1] * CELLS
     blk = Block(vars(r))
-    gather = Gather(links, r.w, r.ag_send, r.ag_recv)
-    scatter = Scatter(links, r.g, boxes, r.wg, r.rs_send, r.rs_recv)
+    gather = Gather(links, r.w, r.sizes, r.ag_send, r.ag_recv)
+    scatter = Scatter(links, r.g, boxes, r.wg, r.sizes, r.rs_send, r.rs_recv)
     small = Small(
         links,
         *(r.sums, r.parts, r.in_c, r.in_x, r.in_y, r.in_h, r.in_l, r.full),
@@ -1307,7 +1302,6 @@
     step = SmallStep(vars(r))
 
     def round_weights():
-        r.clip[...] = jnp.zeros(r.clip.shape, F32)
         for k in range(MATS):
             mine = links.region(r.w, SLOT_OF[k], "")
             mine[...] = r.weights[k].astype(BF16)
@@ -1368,10 +1362,12 @@
         opts[1].squares,
         then(store.wg.start, opts[0].squares),
         then(fetch.row_state.wait, fetch.col_state.wait, opts[1].scale),
-        then(opts[0].scale, store.upd.start, store.new_rows.start, store.new_cols.start),
-        opts[1].rates,
-        opts[0].rates,
-        store.clip.start,
+        then(opts[0].scale, store.new_rows.start, store.new_cols.start),
+        then(fetch.ema.wait, opts[1].apply),
+        then(
+            opts[0].apply, store.new_weights.start, store.copy.start, store.new_ema.start
+        ),
+        then(step.clips, store.clip.start),
     ]
     for i in ORDER:
         ops[i]()
@@ -1381,32 +1377,16 @@
         one.wait()
 
 
-PASSED = 9
-
-
-def finish_kernel(*refs):
-    count = PASSED + 4
+def finish_kernel(count, *refs):
     ins, outs, held = refs[:count], refs[count : 2 * count], refs[2 * count : 3 * count]
-    new_weights, low, new_ema, clips, took, gave = refs[3 * count :]
-    upd, clip, weights, ema = held[PASSED:]
+    took, gave = refs[3 * count :]
     come = [pltpu.make_async_copy(a, b, took.at[i]) for i, (a, b) in enumerate(zip(ins, held))]
-    leave = [*held[:5], new_weights, low, new_ema, *held[5:PASSED], clips]
-    leave = [pltpu.make_async_copy(a, b, gave.at[i]) for i, (a, b) in enumerate(zip(leave, outs))]
-    for one in come[::-1]:
+    leave = [pltpu.make_async_copy(a, b, gave.at[i]) for i, (a, b) in enumerate(zip(held, outs))]
+    for one in come:
         one.start()
-    for one in come[PASSED:]:
+    for one, other in zip(come, leave):
         one.wait()
-    for k in range(weights.shape[0]):
-        new = weights[k] - clip[1:2, k : k + 1] * upd[k]
-        new_weights[k] = new
-        low[k] = new.astype(BF16)
-        new_ema[k] = AVERAGE_KEEP * ema[k] + (1.0 - AVERAGE_KEEP) * new
-    clips[...] = clip[0:1, 0 : clips.shape[1]]
-    for i in (5, 6, 7, count - 1):
-        leave[i].start()
-    for i in range(PASSED):
-        come[i].wait()
-        leave[i if i < 5 else i + 3].start()
+        other.start()
     for one in leave:
         one.wait()
 
@@ -1432,14 +1412,21 @@
         return jax.ShapeDtypeStruct(x.shape, dtype or x.dtype)
 
     clips = weights.shape[0] + small_params.shape[0]
-    passed = (
-        *[like(x) for x in (tokens, tokens, weights, row_state, col_state)],
-        *[like(small_params)] * 4,
+    outs = (
+        like(tokens),
+        like(tokens),
+        like(weights),
+        like(row_state),
+        like(col_state),
+        like(weights),
+        like(weights, BF16),
+        like(weights),
+        like(small_params),
+        like(small_params),
+        like(small_params),
+        like(small_params),
+        jax.ShapeDtypeStruct((1, clips), F32),
     )
-    middle = (*passed, like(weights), jax.ShapeDtypeStruct((2, LANES), F32))
-    stepped = (like(weights), like(weights, BF16), like(weights))
-    last = jax.ShapeDtypeStruct((1, clips), F32)
-    outs = (*passed[:5], *stepped, *passed[5:], last)
     args = Inputs(
         crop_class,
         crop_image,
@@ -1448,19 +1435,20 @@
         weights,
         row_state,
         col_state,
+        weights_ema,
         small_params,
         small_state,
         small_ema,
     )
     staged = [pltpu.SMEM(x.shape, x.dtype) for x in args[:2]]
-    staged += [pltpu.VMEM(x.shape, x.dtype) for x in (*args[2:], *middle)]
+    staged += [pltpu.VMEM(x.shape, x.dtype) for x in (*args[2:], *outs)]
     names = (*shared, *own, *Inputs._fields, *Outputs._fields)
     far = pl.BlockSpec(memory_space=pltpu.HBM)
     res = pl.pallas_call(
         functools.partial(block_kernel, names),
-        out_shape=middle,
+        out_shape=outs,
         in_specs=[far] * len(args),
-        out_specs=(far,) * len(middle),
+        out_specs=(far,) * len(outs),
         scratch_shapes=[
             *shared.values(),
             *own.values(),
@@ -1472,17 +1460,19 @@
         ),
         name="block",
     )(*args)
-    ins = (*res, weights, weights_ema)
-    kept = [pltpu.VMEM(x.shape, x.dtype) for x in (*middle, weights, weights_ema, *stepped, last)]
     res = pl.pallas_call(
-        finish_kernel,
+        functools.partial(finish_kernel, len(outs)),
         out_shape=outs,
-        in_specs=[far] * len(ins),
+        in_specs=[far] * len(outs),
         out_specs=(far,) * len(outs),
-        scratch_shapes=[*kept, *[pltpu.SemaphoreType.DMA((len(outs),))] * 2],
+        scratch_shapes=[
+            *[pltpu.VMEM(x.shape, x.dtype) for x in outs],
+            pltpu.SemaphoreType.DMA((len(outs),)),
+            pltpu.SemaphoreType.DMA((len(outs),)),
+        ],
         compiler_params=pltpu.CompilerParams(vmem_limit_bytes=63 << 20),
         name="finish",
-    )(*ins)
+    )(*res)
     return (*res[:-1], res[-1].reshape(clips))
 
 

time: 93.5 us -> 86.1 us (0.921)
  Pallas kernels: 92.5 us -> 85.2 us
    pallas_call x2, Pallas kernels: 92.5 us -> 85.2 us  [the longest x1 81.6 us: local(): pl.pallas_call(functools.partial(block_kernel, names), out_shape=outs, in...]
where the time goes in v11:
time: 86.1 us; the launch traced here: 86 us
  Pallas kernels  85.2 us (99%)
    pallas_call x1, Pallas kernels, local(): pl.pallas_call(functools.partial(block_kernel, names), out_shape=outs, in...  81.6 us
    pallas_call x1, Pallas kernels, local(): pl.pallas_call(functools.partial(finish_kernel, len(outs)), out_shape=out...  3.58 us

profile of v11, /device:TPU:0, one launch (start us, length us, event | category | flops | bytes accessed | tf_op | source)
XLA Modules:
  0.0 86.0 jit_solution(14611410106883655918)
XLA Ops:
  0.6 81.6 %block.1 = (bf16[1176,512]{1,0:T(8,128)(2,1)}, bf16[1176,512]{1,0:T(8,128)(2,1)}, f32[12,64,128]{2,1,0:T(8,128)}, f32[12,64]{1,0:T(8,128)}, f32[12,128]{1,0:T(8,...) custom-call(s32[4,6]{1,0:T(4,128)} %refs_0_.1, ...), custom_call_target="tpu_custom_call" | custom-call | tf_op jit(solution)/shard_map/block/pallas_call | solution.py:1447
  82.2 3.6 %finish.1 = (bf16[1176,512]{1,0:T(8,128)(2,1)}, bf16[1176,512]{1,0:T(8,128)(2,1)}, f32[12,64,128]{2,1,0:T(8,128)}, f32[12,64]{1,0:T(8,128)}, f32[12,128]{1,0:T(8...) custom-call(bf16[1176,512]{1,0:T(8,128)(2,1)} %get-tuple-element.39., ...), custom_call_target="tpu_custom_call" | custom-call | tf_op jit(solution)/shard_map/finish/pallas_call | solution.py:1463

commit v12 on v11

--- a/solution.py
+++ b/solution.py
@@ -619,36 +619,36 @@
 AXES = "xchly"
 HEAD_ROWS = 320
 SMALL_ROWS = 72
-AG_ROUTES = ("zxyc", "zxyc", "zyxc", "zyxc", "zxyc", "zyxc", "yhxlc", "yxhlc", "hlxyc", "lhyxc", "hxlyc", "lyhxc")
-RS_ROUTES = ("clyhx", "cxlyh", "cyhlx", "cyxlh", "clxhy", "cxhyl", "cylhx", "clyhx", "cxylh", "cylxh", "clxyh", "cylhx")
+AG_ROUTES = ("zyxc", "zyxc", "zxyc", "zxyc", "zyxc", "zxyc", "xhlyc", "xyhlc", "xylhc", "hyxlc", "lhxyc", "hlyxc")
+RS_ROUTES = ("cylhx", "cxylh", "clyhx", "cyxhl", "cxylh", "cyhxl", "cylhx", "cxyhl", "cxhyl", "clyxh", "clyxh", "cylhx")
 ORDER = (
-    426, 428, 429, 435, 431, 434, 427, 22, 69, 76, 66, 86, 116, 109, 129, 96, 132, 87, 136, 176,
-    167, 432, 112, 172, 430, 152, 156, 147, 450, 11, 446, 448, 447, 72, 92, 433, 0, 439, 81, 77,
-    70, 436, 437, 101, 97, 88, 438, 440, 33, 442, 441, 29, 24, 23, 26, 444, 73, 443, 55, 445,
-    449, 451, 18, 12, 15, 13, 102, 98, 94, 44, 7, 4, 2, 1, 107, 67, 30, 27, 25, 93,
-    40, 37, 35, 34, 68, 126, 90, 19, 14, 16, 149, 62, 57, 56, 59, 106, 166, 91, 8, 5,
-    3, 51, 45, 48, 46, 141, 130, 128, 137, 31, 28, 41, 38, 82, 78, 36, 74, 89, 181, 177,
-    168, 146, 20, 17, 32, 456, 71, 121, 117, 113, 457, 463, 108, 127, 466, 63, 60, 58, 169, 464,
-    21, 454, 170, 465, 467, 9, 6, 52, 110, 133, 47, 49, 455, 103, 99, 95, 458, 122, 118, 111,
-    459, 161, 148, 42, 39, 157, 114, 460, 150, 173, 153, 142, 138, 131, 134, 10, 452, 83, 75, 79,
-    453, 182, 178, 462, 174, 461, 64, 61, 43, 171, 468, 104, 100, 53, 50, 470, 469, 472, 473, 123,
-    119, 115, 475, 65, 162, 151, 158, 154, 471, 143, 139, 135, 474, 105, 84, 80, 476, 54, 477, 481,
-    489, 266, 267, 268, 485, 289, 288, 287, 286, 85, 290, 269, 270, 183, 175, 179, 497, 163, 155, 159,
-    493, 124, 120, 478, 281, 271, 144, 140, 482, 494, 486, 328, 327, 326, 329, 330, 272, 301, 293, 292,
-    294, 291, 490, 306, 307, 309, 308, 310, 125, 498, 273, 145, 479, 184, 164, 160, 274, 180, 483, 341,
-    334, 333, 491, 348, 347, 349, 346, 282, 331, 350, 275, 321, 314, 312, 313, 276, 311, 277, 499, 495,
-    165, 487, 368, 370, 369, 366, 367, 185, 480, 332, 484, 361, 352, 353, 354, 351, 496, 302, 296, 492,
-    297, 390, 389, 386, 388, 387, 381, 374, 372, 373, 371, 488, 406, 408, 283, 407, 278, 409, 410, 501,
-    342, 336, 337, 335, 528, 279, 500, 502, 322, 315, 401, 503, 421, 411, 412, 247, 249, 248, 250, 246,
-    393, 413, 414, 504, 317, 505, 316, 519, 391, 521, 518, 506, 261, 254, 362, 356, 357, 355, 252, 284,
-    253, 323, 251, 318, 382, 375, 511, 319, 280, 507, 343, 338, 513, 339, 377, 512, 422, 415, 402, 397,
-    295, 508, 324, 320, 383, 378, 379, 509, 417, 516, 209, 208, 206, 207, 210, 416, 515, 344, 340, 187,
-    186, 188, 376, 190, 189, 392, 396, 395, 510, 514, 517, 423, 418, 363, 226, 228, 419, 230, 227, 229,
-    520, 221, 211, 529, 522, 213, 212, 358, 325, 523, 359, 201, 192, 303, 298, 299, 524, 345, 214, 384,
-    191, 241, 231, 262, 255, 526, 256, 285, 534, 257, 403, 398, 233, 530, 424, 364, 360, 420, 193, 232,
-    399, 234, 525, 222, 215, 304, 535, 380, 527, 216, 531, 217, 242, 235, 202, 195, 196, 197, 404, 263,
-    236, 365, 259, 400, 425, 223, 218, 219, 258, 237, 385, 536, 300, 203, 198, 194, 199, 243, 238, 224,
-    220, 394, 264, 260, 537, 305, 239, 204, 200, 244, 240, 405, 543, 225, 265, 532, 205, 245, 544, 538,
+    426, 428, 429, 431, 432, 430, 435, 427, 22, 72, 66, 76, 87, 156, 149, 116, 169, 96, 152, 106,
+    127, 434, 11, 136, 86, 107, 446, 129, 450, 172, 176, 448, 69, 433, 0, 439, 436, 437, 81, 73,
+    77, 438, 70, 440, 92, 442, 33, 121, 117, 108, 444, 101, 97, 88, 443, 29, 23, 24, 26, 441,
+    93, 445, 68, 447, 449, 55, 451, 18, 15, 12, 13, 122, 118, 132, 102, 98, 109, 44, 7, 4,
+    1, 2, 30, 25, 27, 110, 147, 40, 34, 37, 35, 111, 126, 19, 14, 16, 67, 146, 91, 62,
+    57, 56, 59, 8, 3, 5, 167, 94, 51, 48, 46, 45, 89, 31, 28, 41, 36, 38, 123, 119,
+    166, 90, 141, 130, 137, 128, 161, 157, 150, 153, 20, 17, 133, 32, 456, 82, 78, 74, 148, 457,
+    463, 71, 464, 466, 21, 63, 60, 454, 58, 113, 115, 465, 455, 458, 52, 47, 9, 6, 459, 49,
+    181, 168, 177, 173, 460, 103, 95, 170, 99, 467, 42, 39, 83, 79, 75, 162, 158, 154, 142, 131,
+    151, 138, 10, 452, 461, 134, 453, 114, 462, 43, 468, 53, 50, 182, 174, 171, 178, 470, 64, 61,
+    112, 469, 472, 143, 139, 135, 473, 471, 104, 100, 474, 163, 155, 159, 475, 84, 80, 54, 476, 65,
+    477, 481, 489, 85, 183, 175, 266, 485, 287, 286, 288, 105, 493, 290, 289, 179, 144, 124, 497, 140,
+    478, 164, 160, 281, 274, 272, 267, 120, 273, 482, 486, 328, 327, 326, 301, 330, 291, 292, 494, 329,
+    294, 293, 490, 308, 310, 269, 145, 165, 306, 309, 270, 271, 498, 184, 180, 268, 125, 479, 341, 334,
+    333, 332, 331, 483, 491, 348, 347, 349, 346, 321, 314, 313, 312, 311, 185, 480, 350, 302, 295, 307,
+    495, 487, 369, 296, 368, 282, 275, 367, 366, 276, 277, 499, 484, 361, 352, 353, 354, 351, 496, 492,
+    387, 389, 388, 390, 386, 297, 488, 409, 408, 406, 381, 373, 372, 501, 410, 407, 528, 371, 500, 342,
+    336, 337, 335, 502, 303, 322, 401, 503, 421, 413, 394, 411, 412, 414, 392, 246, 248, 250, 247, 283,
+    504, 298, 299, 505, 393, 249, 518, 391, 519, 521, 506, 343, 362, 356, 357, 261, 251, 253, 252, 254,
+    382, 376, 511, 315, 377, 370, 520, 507, 355, 422, 513, 417, 416, 338, 508, 402, 415, 395, 396, 397,
+    509, 339, 516, 209, 208, 206, 210, 207, 262, 255, 256, 257, 317, 512, 323, 318, 319, 375, 515, 186,
+    188, 187, 278, 510, 190, 189, 514, 363, 359, 221, 211, 213, 212, 214, 358, 517, 226, 227, 228, 316,
+    374, 279, 522, 423, 344, 418, 419, 403, 201, 191, 192, 399, 398, 304, 529, 193, 194, 523, 340, 229,
+    524, 241, 231, 263, 526, 534, 364, 258, 324, 284, 383, 378, 379, 230, 320, 525, 360, 222, 217, 215,
+    216, 259, 530, 424, 420, 202, 195, 345, 535, 280, 527, 232, 531, 404, 400, 242, 235, 237, 236, 384,
+    380, 197, 365, 264, 325, 196, 223, 425, 219, 218, 203, 198, 536, 199, 285, 260, 243, 238, 233, 239,
+    405, 300, 385, 234, 224, 220, 537, 204, 200, 265, 244, 240, 305, 543, 225, 532, 205, 245, 544, 538,
     533, 545, 539, 546, 540, 547, 541, 542, 548, 549,
 )
 
@@ -771,10 +771,12 @@
                 device_id_type=pl.DeviceIdType.MESH,
             )
 
-        self.others(ALL, one)
+        self.others(DP, one)
+        self.others(HEAD, one)
 
     def meet(self):
-        pl.semaphore_wait(pltpu.get_barrier_semaphore(), lax.axis_size(ALL) - 1)
+        count = lax.axis_size(DP) + lax.axis_size(HEAD) - 2
+        pl.semaphore_wait(pltpu.get_barrier_semaphore(), count)
 
     def copy(self, src, dst, send, recv, device):
         return pltpu.make_async_remote_copy(

time: 86.1 us -> 85 us (0.987)
  Pallas kernels: 85.2 us -> 84 us
    pallas_call x1, Pallas kernels: 81.6 us -> 80.4 us  [local(): pl.pallas_call(functools.partial(block_kernel, names), out_shape=outs, in...]
where the time goes in v12:
time: 85 us; the launch traced here: 84.8 us
  Pallas kernels  84 us (99%)
    pallas_call x1, Pallas kernels, local(): pl.pallas_call(functools.partial(block_kernel, names), out_shape=outs, in...  80.4 us
    pallas_call x1, Pallas kernels, local(): pl.pallas_call(functools.partial(finish_kernel, len(outs)), out_shape=out...  3.58 us

profile of v12, /device:TPU:0, one launch (start us, length us, event | category | flops | bytes accessed | tf_op | source)
XLA Modules:
  0.0 84.8 jit_solution(12416885668111684724)
XLA Ops:
  0.6 80.4 %block.1 = (bf16[1176,512]{1,0:T(8,128)(2,1)}, bf16[1176,512]{1,0:T(8,128)(2,1)}, f32[12,64,128]{2,1,0:T(8,128)}, f32[12,64]{1,0:T(8,128)}, f32[12,128]{1,0:T(8,...) custom-call(s32[4,6]{1,0:T(4,128)} %refs_0_.1, ...), custom_call_target="tpu_custom_call" | custom-call | tf_op jit(solution)/shard_map/block/pallas_call | solution.py:1449
  81.1 3.6 %finish.1 = (bf16[1176,512]{1,0:T(8,128)(2,1)}, bf16[1176,512]{1,0:T(8,128)(2,1)}, f32[12,64,128]{2,1,0:T(8,128)}, f32[12,64]{1,0:T(8,128)}, f32[12,128]{1,0:T(8...) custom-call(bf16[1176,512]{1,0:T(8,128)(2,1)} %get-tuple-element.39., ...), custom_call_target="tpu_custom_call" | custom-call | tf_op jit(solution)/shard_map/finish/pallas_call | solution.py:1465

commit v13 on v12

--- a/solution.py
+++ b/solution.py
@@ -209,14 +209,14 @@
         self.rel_taps[...] = self.small[22 : 22 + WINDOW * WINDOW, :] * mask
 
     def place(self, rows_ref, first, r0, size):
-        count = rows_ref.shape[0]
+        base = pl.multiple_of(first // 16 * 16, 16)
         r = r0 + lax.broadcasted_iota(jnp.int32, (size, 1), 0)
         cell, slot = r >> 3, r & 7
-        want = first + slot * CELLS + cell
+        want = first - base + slot * CELLS + cell
         want = jnp.where((slot < self.cls.shape[1]) & (cell < CELLS), want, -1)
-        col = lax.broadcasted_iota(jnp.int32, (size, count), 1)
+        col = lax.broadcasted_iota(jnp.int32, (size, HEAD_ROWS), 1)
         pick = jnp.where(col == want, 1.0, 0.0).astype(BF16)
-        return dot(pick, rows_ref[...])
+        return dot(pick, rows_ref[pl.ds(base, HEAD_ROWS), :])
 
     def unplace(self, src_ref, out_ref):
         count = out_ref.shape[0]
@@ -1262,9 +1262,17 @@
     n_in, n_out = len(Inputs._fields), len(Outputs._fields)
     ins, outs, refs = Inputs(*refs[:n_in]), Outputs(*refs[n_in : n_in + n_out]), refs[n_in + n_out :]
     r = types.SimpleNamespace(**dict(zip(names, refs)))
+    for rows in (r.tokens, r.cot):
+        rows[rows.shape[0] - 32 :, :] = jnp.zeros((32, D), BF16)
+
+    def near(ref, scratch):
+        if ref.shape == scratch.shape:
+            return scratch
+        return scratch.at[pl.ds(0, ref.shape[0])]
+
     fetch = Inputs(
         *[
-            Ready(ref, getattr(r, name), r.fetched.at[i])
+            Ready(ref, near(ref, getattr(r, name)), r.fetched.at[i])
             for i, (name, ref) in enumerate(zip(Inputs._fields, ins))
         ]
     )
@@ -1443,7 +1451,9 @@
         small_ema,
     )
     staged = [pltpu.SMEM(x.shape, x.dtype) for x in args[:2]]
-    staged += [pltpu.VMEM(x.shape, x.dtype) for x in (*args[2:], *outs)]
+    last_rows = tokens.shape[0] // heads * (heads - 1) // 16 * 16
+    staged += [pltpu.VMEM((last_rows + HEAD_ROWS, D), BF16)] * 2
+    staged += [pltpu.VMEM(x.shape, x.dtype) for x in (*args[4:], *outs)]
     names = (*shared, *own, *Inputs._fields, *Outputs._fields)
     far = pl.BlockSpec(memory_space=pltpu.HBM)
     res = pl.pallas_call(

time: 85 us -> 84.9 us (level)
  no operation moved by 1% of the time
where the time goes in v13:
time: 84.9 us; the launch traced here: 84.7 us
  Pallas kernels  83.9 us (99%)
    pallas_call x1, Pallas kernels, local(): pl.pallas_call(functools.partial(block_kernel, names), out_shape=outs, in...  80.3 us
    pallas_call x1, Pallas kernels, local(): pl.pallas_call(functools.partial(finish_kernel, len(outs)), out_shape=out...  3.58 us

profile of v13, /device:TPU:0, one launch (start us, length us, event | category | flops | bytes accessed | tf_op | source)
XLA Modules:
  0.0 84.7 jit_solution(15932027315508211317)
XLA Ops:
  0.6 80.3 %block.1 = (bf16[1176,512]{1,0:T(8,128)(2,1)}, bf16[1176,512]{1,0:T(8,128)(2,1)}, f32[12,64,128]{2,1,0:T(8,128)}, f32[12,64]{1,0:T(8,128)}, f32[12,128]{1,0:T(8,...) custom-call(s32[4,6]{1,0:T(4,128)} %refs_0_.1, ...), custom_call_target="tpu_custom_call" | custom-call | tf_op jit(solution)/shard_map/block/pallas_call | solution.py:1459
  81.0 3.6 %finish.1 = (bf16[1176,512]{1,0:T(8,128)(2,1)}, bf16[1176,512]{1,0:T(8,128)(2,1)}, f32[12,64,128]{2,1,0:T(8,128)}, f32[12,64]{1,0:T(8,128)}, f32[12,128]{1,0:T(8...) custom-call(bf16[1176,512]{1,0:T(8,128)(2,1)} %get-tuple-element.39., ...), custom_call_target="tpu_custom_call" | custom-call | tf_op jit(solution)/shard_map/finish/pallas_call | solution.py:1475
